TPU v7x, 32 devices: a whole 2x2x4 slice. The times are simulated.
32 devices in a mesh: front: 2 (over y), row: 4 (over x, core), col: 4 (over z).
Axes of the slice: x: 2, y: 2, z: 4, core: 2. Of those that a mesh axis runs over, the one named last changes fastest.
Arguments:
- kids: bfloat16 [2, 2, 3072, 3072], P('front', None, 'row'), as said below
- maps: int32 [2, 2, 72, 24], P('front'), may hold values from 0 to 1, as said below
- mask: int32 [2, 72, 4], P('front'), may hold values 0 or 1
- diag: float32 [2, 9216], P('front', 'row'), may hold values from 1 to 2
Outputs:
- front: float32 [2, 9216, 512], P('front', 'row', 'col')
Inputs may be any that keep to these rules, and one draw needn't show every extreme that they name: Each kids[f, k] is symmetric. Each maps[f, k] has a single 1 in every column and at most one 1 in every row; all other entries are 0.
All inputs are finite; a program needn't handle non-finite values. No bound on the sum of `mask` on one device may be relied on, other than what follows from the above.
Results may differ from a plain program's by a relative error of at most 0.0003.
Values may be sent and summed in bfloat16 or wider, within the bound.
No kernel may reach another device: no remote copies, remote signals or barrier semaphores. Data moves between devices by JAX's collectives and lax.ppermute only.
A program may use at most 128 MiB of HBM per device.

v0:
```python
import jax
import jax.numpy as jnp
from jax import lax
from jax.sharding import PartitionSpec as P

BLOCK = 128
G = 3072
PW = 128
NPANEL = 2


def shifted(x, axis, by):
    length = lax.axis_size(axis)
    return lax.ppermute(x, axis, [(i, (i + by) % length) for i in range(length)])


def broadcast(value, axis, source):
    kept = jnp.where(lax.axis_index(axis) == source, value, 0).astype(value.dtype)
    return lax.psum(kept, axis)


def select_cols(child, col_table, col_index):
    blocks = PW // BLOCK
    window = lax.dynamic_slice_in_dim(col_table, col_index * blocks, blocks, 0)
    rows_here = child.shape[0]
    shaped = child.reshape(rows_here, G // BLOCK, BLOCK)
    picked = jnp.einsum("wk,jkb->jwb", window, shaped, preferred_element_type=jnp.float32)
    return picked.reshape(rows_here, PW).astype(jnp.bfloat16)


def body(kids, maps, mask, diag):
    row_index = lax.axis_index("row")
    col_index = lax.axis_index("col")
    rows_dev = diag.shape[1]
    row_blocks = rows_dev // BLOCK
    own_map = maps[0, 0].astype(jnp.bfloat16)
    own_band = select_cols(kids[0, 0], own_map, col_index)
    far_child, far_map = shifted((kids[0, 1], maps[0, 1].astype(jnp.bfloat16)), "front", -1)
    far_band = select_cols(far_child, far_map, col_index)
    own_rows = lax.dynamic_slice_in_dim(own_map, row_index * row_blocks, row_blocks, 0)
    far_rows = lax.dynamic_slice_in_dim(far_map, row_index * row_blocks, row_blocks, 0)
    running = jnp.zeros((rows_dev, PW), jnp.float32)
    pieces = (
        lax.all_gather(own_band, "row", axis=0, tiled=True),
        lax.all_gather(far_band, "row", axis=0, tiled=True),
    )
    block_count = pieces[0].shape[0] // BLOCK
    for row_table, band_piece in ((own_rows, pieces[0]), (far_rows, pieces[1])):
        placed = jnp.einsum(
            "pj,jax->pax",
            row_table,
            band_piece.reshape(block_count, BLOCK, PW),
            preferred_element_type=jnp.float32,
        )
        running = running + placed.reshape(rows_dev, PW)
    global_rows = row_index * rows_dev + jnp.arange(rows_dev)
    global_cols = col_index * PW + jnp.arange(PW)
    front_tile = running + jnp.where(
        global_rows[:, None] == global_cols[None, :], diag[0][:, None], jnp.float32(0.0)
    )
    block_mask = lax.dynamic_slice(
        mask[0], (row_index * row_blocks, col_index * (PW // BLOCK)), (row_blocks, PW // BLOCK)
    ).astype(jnp.float32)
    expanded = jnp.repeat(jnp.repeat(block_mask, BLOCK, 0), BLOCK, 1)
    update_mask = jnp.where(global_cols[None, :] < NPANEL * PW, jnp.float32(1.0), expanded)
    for panel_index in range(NPANEL):
        lower = panel_index * PW
        upper = lower + PW
        column_slab = broadcast(front_tile, "col", panel_index)
        pivot = broadcast(lax.slice_in_dim(column_slab, lower, upper, axis=0), "row", 0)
        factor = jnp.linalg.cholesky(pivot)
        solved = lax.linalg.triangular_solve(
            factor, column_slab, left_side=False, lower=True, transpose_a=True
        )
        padded = jnp.pad(factor, ((lower, rows_dev - upper), (0, 0)))
        inside = (global_rows[:, None] >= lower) & (global_rows[:, None] < upper)
        below = global_rows[:, None] >= upper
        panel_rows = jnp.where(inside, padded, jnp.where(below, solved, jnp.float32(0.0)))
        mirror_root = col_index * PW // rows_dev
        mirror_offset = col_index * PW % rows_dev
        mirrored = broadcast(
            lax.dynamic_slice_in_dim(panel_rows, mirror_offset, PW, 0), "row", mirror_root
        )
        product = jnp.dot(panel_rows, mirrored.T, precision=lax.Precision.HIGHEST)
        front_tile = (
            front_tile
            - jnp.where(global_cols[None, :] >= upper, update_mask, jnp.float32(0.0)) * product
        )
        front_tile = jnp.where(col_index == panel_index, panel_rows, front_tile)
    return front_tile[None]


def solution(mesh):
    in_specs = (
        P("front", None, "row", None),
        P("front", None, None, None),
        P("front", None, None),
        P("front", "row"),
    )
    out_specs = P("front", "row", "col")
    return jax.shard_map(body, mesh=mesh, in_specs=in_specs, out_specs=out_specs, check_vma=False)
```

profile of v0, /device:TPU:0, one launch (start us, length us, event | category | flops | bytes accessed | tf_op | source)
XLA Modules:
  0.0 449.3 jit_solution(16271439157960173430)
XLA Ops:
  6.5 9.2 %slice_bitcast_fusion = (bf16[768,3072]{1,0:T(8,128)(2,1)}, bf16[96,8,24,128]{3,1,2,0:T(8,128)(2,1)}) fusion(bf16[1,2,768,3072]{3,2,1,0:T(8,128)(2,1)} %param.7), kind=kLoop, calls=%fused_computation | loop fusion | bytes 18874368 | tf_op jit(solution)/shard_map/squeeze | solution.py:38
  15.8 3.0 collective-permute-start.1
  19.0 5.9 %copy.27 = bf16[96,8,24,128]{3,2,1,0:T(8,128)(2,1)} copy(bf16[96,8,24,128]{3,1,2,0:T(8,128)(2,1)} %get-tuple-element.14) | data formatting | bytes 9437184
  24.8 3.2 fusion.35
  28.1 9.1 %all_gather.6 = bf16[3072,128]{1,0:T(8,128)(2,1)S(1)} all-gather(bf16[768,128]{1,0:T(8,128)(2,1)S(1)} %convert_element_type.33), channel_id=1, replica_groups=mesh['front'=2,'row'=4,'col'=4] {'row'}, dimensions={0}, use_global_device_ids=true | all-gather | bytes 983040 | tf_op jit(solution)/shard_map/all_gather | solution.py:44
  37.9 83.2 %collective-permute-done.1 = bf16[768,3072]{1,0:T(8,128)(2,1)} collective-permute-done((bf16[768,3072]{1,0:T(8,128)(2,1)}, bf16[768,3072]{1,0:T(8,128)(2,1)}, u32[]{:S(2)}, u32[]{:S(2)}) %collective-permute-start.1) | collective-permute-done | bytes 4718624 | tf_op jit(solution)/shard_map/ppermute | solution.py:14
  121.1 3.7 copy.28
  125.8 8.8 %all_gather.7 = bf16[3072,128]{1,0:T(8,128)(2,1)S(1)} all-gather(bf16[768,128]{1,0:T(8,128)(2,1)S(1)} %convert_element_type.35), channel_id=1, replica_groups=mesh['front'=2,'row'=4,'col'=4] {'row'}, dimensions={0}, use_global_device_ids=true | all-gather | bytes 983040 | tf_op jit(solution)/shard_map/all_gather | solution.py:45
  135.5 2.1 broadcast_select_fusion.1
  138.6 55.5 %all-reduce.9.cloned.1.call-done = f32[2304,128]{1,0:T(8,128)} async-done(((f32[2304,128]{1,0:T(8,128)}), f32[2304,128]{1,0:T(8,128)}) %all-reduce.9.cloned.1.call-update) | async-done | bytes 1179664 | tf_op jit(solution)/shard_map/psum | solution.py:19
  195.9 31.2 %all-reduce.11.cloned.1.call-done = f32[128,128]{1,0:T(8,128)} async-done(((f32[128,128]{1,0:T(8,128)}), f32[128,128]{1,0:T(8,128)}) %all-reduce.11.cloned.1.call-update) | async-done | bytes 65552 | tf_op jit(solution)/shard_map/psum | solution.py:19
  228.9 11.7 %cholesky.44 = f32[128,128]{1,0:T(8,128)S(1)} custom-call(f32[128,128]{1,0:T(8,128)S(1)} %copy.18), custom_call_target="Cholesky" | custom-call | tf_op jit(solution)/shard_map/jit(cholesky)/cholesky | solution.py:71
  242.0 9.8 %custom-call.6 = f32[1,128,128]{1,2,0:T(8,128)S(1)} custom-call(f32[1,128,128]{2,1,0:T(8,128)S(1)} %get-tuple-element.9), custom_call_target="InvertDiagBlocksLowerTriangular" | custom-call | tf_op jit(solution)/shard_map/triangular_solve/custom-call.0 | solution.py:72
  251.8 3.6 fusion.8
  256.7 30.6 %all-reduce.13.cloned.1.call-done = f32[128,128]{1,0:T(8,128)} async-done(((f32[128,128]{1,0:T(8,128)}), f32[128,128]{1,0:T(8,128)}) %all-reduce.13.cloned.1.call-update) | async-done | bytes 65552 | tf_op jit(solution)/shard_map/psum | solution.py:19
  287.3 3.0 broadcast_select_fusion
  290.4 56.0 %all-reduce.15.cloned.1.call-done = f32[2304,128]{1,0:T(8,128)} async-done(((f32[2304,128]{1,0:T(8,128)}), f32[2304,128]{1,0:T(8,128)}) %all-reduce.15.cloned.1.call-update) | async-done | bytes 1179664 | tf_op jit(solution)/shard_map/psum | solution.py:19
  346.4 1.5 slice_select_fusion
  348.2 31.0 %all-reduce.17.cloned.1.call-done = f32[128,128]{1,0:T(8,128)} async-done(((f32[128,128]{1,0:T(8,128)}), f32[128,128]{1,0:T(8,128)}) %all-reduce.17.cloned.1.call-update) | async-done | bytes 65552 | tf_op jit(solution)/shard_map/psum | solution.py:19
  381.1 11.7 %cholesky.55 = f32[128,128]{1,0:T(8,128)S(1)} custom-call(f32[128,128]{1,0:T(8,128)S(1)} %copy.21), custom_call_target="Cholesky" | custom-call | tf_op jit(solution)/shard_map/jit(cholesky)/cholesky | solution.py:71
  394.2 9.8 %custom-call.7 = f32[1,128,128]{1,2,0:T(8,128)S(1)} custom-call(f32[1,128,128]{2,1,0:T(8,128)S(1)} %get-tuple-element.6), custom_call_target="InvertDiagBlocksLowerTriangular" | custom-call | tf_op jit(solution)/shard_map/triangular_solve/custom-call.0 | solution.py:72
  404.0 3.6 fusion.6
  408.2 31.2 %all-reduce.19.cloned.1.call-done = f32[128,128]{1,0:T(8,128)} async-done(((f32[128,128]{1,0:T(8,128)}), f32[128,128]{1,0:T(8,128)}) %all-reduce.19.cloned.1.call-update) | async-done | bytes 65552 | tf_op jit(solution)/shard_map/psum | solution.py:19
  439.4 3.0 fusion.4
  (51 shorter events, 14.1 us)
Async XLA Ops:
  6.5 12.2 %copy-start = (s32[1,2,72,24]{2,3,1,0:T(8,128)S(1)}, s32[1,2,72,24]{2,3,1,0:T(8,128)}, u32[]{:S(2)}) copy-start(s32[1,2,72,24]{2,3,1,0:T(8,128)} %param.8) | copy-start | bytes 41476
  6.5 187.6 %all-reduce.9.cloned.1.call-start = ((), (), s32[]{:S(2)}) async-start(), calls=%async_computation | async-start | bytes 2359296 | tf_op jit(solution)/shard_map/psum | solution.py:19
  15.8 105.3 %collective-permute-start.1 = (bf16[768,3072]{1,0:T(8,128)(2,1)}, bf16[768,3072]{1,0:T(8,128)(2,1)}, u32[]{:S(2)}, u32[]{:S(2)}) collective-permute-start(bf16[768,3072]{1,0:T(8,128)(2,1)} %get-tuple-element.13), channel_id=1, source_target_pairs={{0,16},{16,0},{1,17},{17,1},{2,18},{18,2},{3,19},{19,3},{4,20},{20... | collective-permute-start | bytes 14155784 | tf_op jit(solution)/shard_map/ppermute | solution.py:14
  18.9 105.9 %collective-permute-start = (bf16[72,24]{1,0:T(8,128)(2,1)S(1)}, bf16[72,24]{1,0:T(8,128)(2,1)S(1)}, u32[]{:S(2)}, u32[]{:S(2)}) collective-permute-start(bf16[72,24]{1,0:T(8,128)(2,1)S(1)} %get-tuple-element.15), channel_id=1, source_target_pairs={{0,16},{16,0},{1,17},{17,1},{2,18},{18,2},{3,19},{19,3},{4,20},{20... | collective-permute-start | bytes 10376 | tf_op jit(solution)/shard_map/ppermute | solution.py:14
  37.1 0.7 copy-start.1
  137.7 89.4 %all-reduce.11.cloned.1.call-start = ((), (), s32[]{:S(2)}) async-start(), calls=%async_computation.1 | async-start | bytes 131072 | tf_op jit(solution)/shard_map/psum | solution.py:19
  195.6 91.7 %all-reduce.13.cloned.1.call-start = ((), (), s32[]{:S(2)}) async-start(), calls=%async_computation.2 | async-start | bytes 131072 | tf_op jit(solution)/shard_map/psum | solution.py:19
  256.1 90.3 %all-reduce.15.cloned.1.call-start = ((), (), s32[]{:S(2)}) async-start(), calls=%async_computation.3 | async-start | bytes 2359296 | tf_op jit(solution)/shard_map/psum | solution.py:19
  290.3 88.9 %all-reduce.17.cloned.1.call-start = ((), (), s32[]{:S(2)}) async-start(), calls=%async_computation.4 | async-start | bytes 131072 | tf_op jit(solution)/shard_map/psum | solution.py:19
  347.9 91.5 %all-reduce.19.cloned.1.call-start = ((), (), s32[]{:S(2)}) async-start(), calls=%async_computation.5 | async-start | bytes 131072 | tf_op jit(solution)/shard_map/psum | solution.py:19
Sparse Core Ops, SparseCore 0:
  137.8 56.2 all-reduce.8
  196.4 30.6 all-reduce.10
  256.2 31.0 all-reduce.12
  290.5 55.8 all-reduce.14
  348.6 30.6 all-reduce.16
  408.3 31.0 all-reduce.18
where the time goes:
time: 450 us; the launch traced here: 449 us
  waiting for transfers between devices  319 us (71%)
  other arithmetic  55.2 us (12%)
  local copies, waits for them, and re-layouts  21.3 us (5%)
  matrix products  18.7 us (4%)
  blocking collectives  17.9 us (4%)
  between operations  13.7 us (3%)
    psum x6, waiting for transfers between devices, broadcast(): return lax.psum(kept, axis)  236 us
    ppermute x2, waiting for transfers between devices, shifted(): lax.ppermute(x, axis, [(i, (i + by) % length) for i in range(length)])  83.2 us
    another operation x6, other arithmetic, body(): factor = jnp.linalg.cholesky(pivot)  24.8 us
    another operation x4, other arithmetic, body(): lax.linalg.triangular_solve(factor, column_slab, left_side=False, lower=T...  20.9 us
    unnamed x7, local copies, waits for them, and re-layouts  9.68 us
    squeeze x1, local copies, waits for them, and re-layouts, body(): kids[0, 1]  9.24 us
    all_gather x1, blocking collectives, body(): lax.all_gather(own_band, 'row', axis=0, tiled=True)  9.08 us
  transfers between devices with their start and end apart: 8, of which 7 were waited for; matrix products, arithmetic and copies ran while one was open for 3% of the time, Pallas kernels for 0%

commit v1 on v0

v1 whole, which is shorter than its diff:
```python
import functools

import jax
import jax.numpy as jnp
from jax import lax
from jax.experimental import pallas as pl
from jax.experimental.pallas import tpu as pltpu
from jax.sharding import PartitionSpec as P

BLOCK = 128
PW = 128
NPANEL = 2
F32 = jnp.float32
BF16 = jnp.bfloat16
HIGHEST = lax.Precision.HIGHEST
VMEM_LIMIT = 40 * 1024 * 1024


def params():
    return pltpu.CompilerParams(vmem_limit_bytes=VMEM_LIMIT)


def child_block(maps, child, row):
    index, found = jnp.int32(0), jnp.int32(0)
    for j in range(maps.shape[3]):
        value = maps[0, child, row, j]
        index = index + value * j
        found = found + value
    return index, found


def window_kernel(maps, diag, kids, own, far, sems):
    me = lax.axis_index("row")
    local = kids.shape[2] // BLOCK
    copies = []
    for child, out in ((0, own), (1, far)):
        found = [child_block(maps, child, w) for w in range(NPANEL)]
        for at, (w, p) in enumerate(((0, 0), (1, 0), (1, 1))):
            row, row_ok = found[w]
            col, col_ok = found[p]
            offset = row - me * local
            here = (row_ok > 0) & (col_ok > 0) & (offset >= 0) & (offset < local)
            target = out.at[pl.ds(at * BLOCK, BLOCK)]
            copy = pltpu.make_async_copy(
                kids.at[
                    0,
                    child,
                    pl.ds(pl.multiple_of(offset * BLOCK, BLOCK), BLOCK),
                    pl.ds(pl.multiple_of(col * BLOCK, BLOCK), BLOCK),
                ],
                target,
                sems.at[child, at],
            )
            copies.append((here, copy, target))
    for here, copy, target in copies:

        @pl.when(here)
        def _():
            copy.start()

        @pl.when(jnp.logical_not(here))
        def _():
            target[...] = jnp.zeros_like(target)

    line = lax.broadcasted_iota(jnp.int32, (16, BLOCK), 0)
    pieces = jnp.zeros((16, BLOCK), F32)
    for p in range(NPANEL):
        rest = jnp.broadcast_to(diag[0:1, p * PW : (p + 1) * PW], (16, BLOCK))
        for at in range(3):
            part = rest.astype(BF16).astype(F32)
            pieces = jnp.where(line == 3 * p + at, part, pieces)
            rest = rest - part
    own[3 * BLOCK :, :] = jnp.where(me == 0, pieces, 0.0).astype(BF16)
    for here, copy, target in copies:

        @pl.when(here)
        def _():
            copy.wait()


def bands_kernel(maps, kids, own, far, sems):
    col_index = lax.axis_index("col")
    copies = []
    for child, out in ((0, own), (1, far)):
        for at, row in enumerate((0, 1, col_index)):
            col, ok = child_block(maps, child, row)
            target = out.at[:, pl.ds(at * BLOCK, BLOCK)]
            copy = pltpu.make_async_copy(
                kids.at[0, child, :, pl.ds(pl.multiple_of(col * BLOCK, BLOCK), BLOCK)],
                target,
                sems.at[child, at],
            )
            copies.append((ok > 0, copy, target))
    for here, copy, target in copies:

        @pl.when(here)
        def _():
            copy.start()

        @pl.when(jnp.logical_not(here))
        def _():
            target[...] = jnp.zeros_like(target)

    for here, copy, target in copies:

        @pl.when(here)
        def _():
            copy.wait()


def inverse_factor(tiles):
    tiles = list(tiles)
    count = len(tiles)
    lane = lax.broadcasted_iota(jnp.int32, (8, BLOCK), 1)
    line = lax.broadcasted_iota(jnp.int32, (8, BLOCK), 0)
    wide = lambda x: jnp.broadcast_to(x, (8, BLOCK))
    result = []
    for b in range(count):
        low = 8 * b
        tile = tiles[b]
        columns = [wide(tile[:, low + j : low + j + 1]) for j in range(8)]
        d = [[wide(columns[j][i : i + 1, :]) if i >= j else None for j in range(8)] for i in range(8)]
        inside = (lane >= low) & (lane < low + 8)
        rows = [
            jnp.where(inside, (lane == low + i).astype(F32), wide(tile[i : i + 1, :]))
            for i in range(8)
        ]
        scale = []
        for j in range(8):
            scale.append(lax.rsqrt(d[j][j]))
            for i in range(j + 1, 8):
                d[i][j] = d[i][j] * scale[j]
            for k in range(j + 1, 8):
                for i in range(k, 8):
                    d[i][k] = d[i][k] - d[i][j] * d[k][j]
            rows[j] = rows[j] * scale[j]
            for i in range(j + 1, 8):
                rows[i] = rows[i] - d[i][j] * rows[j]
        merged = rows[0]
        for j in range(1, 8):
            merged = jnp.where(line == j, rows[j], merged)
        result.append(jnp.where(lane < low + 8, merged, 0.0))
        for t in range(b + 1, count):
            tile = tiles[t]
            columns = [wide(tile[:, low + j : low + j + 1]) for j in range(8)]
            tile = jnp.where(inside, 0.0, tile)
            for j in range(8):
                for m in range(j):
                    columns[j] = columns[j] - columns[m] * d[j][m]
                columns[j] = columns[j] * scale[j]
                tile = tile - columns[j] * rows[j]
            tiles[t] = tile
    return result


def dot(a, b, lhs=1, rhs=0):
    return lax.dot_general(
        a, b, (((lhs,), (rhs,)), ((), ())), precision=HIGHEST, preferred_element_type=F32
    )


def factor_kernel(n_own, *refs):
    own, far, out = refs[:n_own], refs[n_own:-1], refs[-1]

    def total(at):
        value = None
        for ref in own + far:
            block = ref[at * BLOCK : (at + 1) * BLOCK, :].astype(F32)
            value = block if value is None else value + block
        return value

    pieces = None
    for ref in own:
        part = ref[3 * BLOCK :, :].astype(F32)
        pieces = part if pieces is None else pieces + part
    eye = lax.broadcasted_iota(jnp.int32, (BLOCK, BLOCK), 0) == lax.broadcasted_iota(
        jnp.int32, (BLOCK, BLOCK), 1
    )

    def diagonal(p):
        line = pieces[3 * p : 3 * p + 1] + pieces[3 * p + 1 : 3 * p + 2]
        line = line + pieces[3 * p + 2 : 3 * p + 3]
        return jnp.where(eye, jnp.broadcast_to(line, (BLOCK, BLOCK)), 0.0)

    def invert(block):
        return jnp.concatenate(
            inverse_factor([block[8 * t : 8 * t + 8, :] for t in range(BLOCK // 8)]), axis=0
        )

    first = invert(total(0) + diagonal(0))
    cross = dot(total(1), first, 1, 1)
    second = invert(total(2) + diagonal(1) - dot(cross, cross, 1, 1))
    out[0:BLOCK, 0:BLOCK] = first
    out[0:BLOCK, BLOCK:] = jnp.zeros((BLOCK, BLOCK), F32)
    out[BLOCK:, 0:BLOCK] = -dot(second, dot(cross, first))
    out[BLOCK:, BLOCK:] = second


def front_kernel(owners, n_row, row_blocks, tables, mask, diag, inverse, *refs):
    count = len(owners(0))
    own, far = refs[:count], refs[count : 2 * count]
    out, buffer, sems = refs[2 * count :]
    me = lax.axis_index("row")
    col_index = lax.axis_index("col")
    rows_here = own[0].shape[0]
    zero_block = n_row * rows_here // BLOCK
    copies = []
    for child, group in ((0, own), (1, far)):
        for at, (owner, ref) in enumerate(zip(owners(me), group)):
            copy = pltpu.make_async_copy(
                ref,
                buffer.at[child, pl.ds(pl.multiple_of(owner * rows_here, BLOCK), rows_here)],
                sems.at[child, at],
            )
            copy.start()
            copies.append(copy)
        buffer[child, zero_block * BLOCK :, :] = jnp.zeros((BLOCK, buffer.shape[2]), BF16)
    for copy in copies:
        copy.wait()

    def block(child, index, start, width):
        return buffer[child, pl.ds(pl.multiple_of(index * BLOCK, BLOCK), BLOCK), start : start + width]

    wide = NPANEL * PW
    lower = inverse[...]
    mirrored = block(0, tables[0, col_index], 0, wide).astype(F32) + block(
        1, tables[1, col_index], 0, wide
    ).astype(F32)
    row_id = lax.broadcasted_iota(jnp.int32, (wide, PW), 0)
    col_id = lax.broadcasted_iota(jnp.int32, (wide, PW), 1)
    picked = -(row_id == col_id + col_index * PW).astype(F32)
    solved = jnp.where(col_index < NPANEL, picked, dot(lower, mirrored, 1, 1))
    weight = dot(lower, solved, 0, 0)
    high = weight.astype(BF16)
    low = (weight - high.astype(F32)).astype(BF16)
    both = jnp.concatenate([high, low], axis=1)
    both = jnp.concatenate([both, both], axis=0)
    is_panel = col_index < NPANEL
    for p in range(row_blocks):
        at = me * row_blocks + p
        first, second = tables[0, at], tables[1, at]
        left = jnp.concatenate([block(0, first, 0, wide), block(1, second, 0, wide)], axis=1)
        product = jnp.dot(left, both, preferred_element_type=F32)
        product = product[:, :PW] + product[:, PW:]
        base = block(0, first, wide, PW).astype(F32) + block(1, second, wide, PW).astype(F32)
        keep = jnp.where(is_panel | (mask[0, at, col_index] > 0), 1.0, 0.0)
        out[0, p * BLOCK : (p + 1) * BLOCK, :] = jnp.where(is_panel, 0.0, base) - keep * product

    eye = lax.broadcasted_iota(jnp.int32, (BLOCK, BLOCK), 0) == lax.broadcasted_iota(
        jnp.int32, (BLOCK, BLOCK), 1
    )

    def diagonal(p):
        return jnp.where(
            eye, jnp.broadcast_to(diag[0:1, p * BLOCK : (p + 1) * BLOCK], (BLOCK, BLOCK)), 0.0
        )

    for p in range(NPANEL):

        @pl.when(me == 0)
        def _():
            keep = jnp.where(is_panel | (mask[0, p, col_index] > 0), 1.0, 0.0)
            column = jnp.sum(diagonal(p), axis=1, keepdims=True)
            value = out[0, p * BLOCK : (p + 1) * BLOCK, :]
            value = value - keep * column * weight[p * BLOCK : (p + 1) * BLOCK, :]
            row = lax.broadcasted_iota(jnp.int32, (BLOCK, BLOCK), 0) + p * BLOCK
            col = lax.broadcasted_iota(jnp.int32, (BLOCK, BLOCK), 1) + col_index * PW
            out[0, p * BLOCK : (p + 1) * BLOCK, :] = jnp.where(is_panel & (row < col), 0.0, value)

    for p in range(row_blocks):

        @pl.when(jnp.logical_not(is_panel) & (me * row_blocks + p == col_index))
        def _():
            out[0, p * BLOCK : (p + 1) * BLOCK, :] += diagonal(p)


def body(kids, maps, mask, diag):
    fronts, n_row = lax.axis_size("front"), lax.axis_size("row")
    chips = n_row // 2
    rows_dev = diag.shape[1]
    row_blocks = rows_dev // BLOCK
    rows_here = kids.shape[2]
    vmem, smem = pl.BlockSpec(memory_space=pltpu.VMEM), pl.BlockSpec(memory_space=pltpu.SMEM)
    anywhere = pl.BlockSpec(memory_space=pl.ANY)

    def along(x, by):
        return lax.ppermute(x, "row", [(i, (i + 2 * by) % n_row) for i in range(n_row)])

    def partner(x):
        return lax.ppermute(x, "row", [(i, i ^ 1) for i in range(n_row)])

    def parent(x, by):
        pairs = []
        for f in range(fronts):
            for i in range(n_row):
                pairs.append((f * n_row + i, (f - 1) % fronts * n_row + (i + 2 * by) % n_row))
        return lax.ppermute(x, ("front", "row"), pairs)

    own_window, far_window = pl.pallas_call(
        window_kernel,
        out_shape=[
            jax.ShapeDtypeStruct((3 * BLOCK + 16, BLOCK), BF16),
            jax.ShapeDtypeStruct((3 * BLOCK, BLOCK), BF16),
        ],
        in_specs=[smem, vmem, anywhere],
        out_specs=[vmem, vmem],
        scratch_shapes=[pltpu.SemaphoreType.DMA((2, 3))],
        compiler_params=params(),
        name="window_blocks",
    )(maps, diag, kids)
    own_parts = [own_window] + [along(own_window, s) for s in range(1, chips)]
    far_parts = [parent(far_window, s) for s in range(chips)]
    own_parts = own_parts + [partner(x) for x in own_parts]
    far_parts = far_parts + [partner(x) for x in far_parts]

    own_bands, far_bands = pl.pallas_call(
        bands_kernel,
        out_shape=[jax.ShapeDtypeStruct((rows_here, 3 * BLOCK), BF16)] * 2,
        in_specs=[smem, anywhere],
        out_specs=[vmem, vmem],
        scratch_shapes=[pltpu.SemaphoreType.DMA((2, 3))],
        compiler_params=params(),
        name="bands",
    )(maps, kids)
    far_bands = parent(far_bands, 0)
    own_all = [own_bands] + [along(own_bands, s) for s in range(1, chips)]
    far_all = [far_bands] + [along(far_bands, s) for s in range(1, chips)]
    own_all = own_all + [partner(x) for x in own_all]
    far_all = far_all + [partner(x) for x in far_all]

    def owners(me):
        here = [(me + n_row - 2 * s) % n_row for s in range(chips)]
        other = me + 1 - 2 * (me % 2)
        return here + [(other + n_row - 2 * s) % n_row for s in range(chips)]

    inverse = pl.pallas_call(
        functools.partial(factor_kernel, len(own_parts)),
        out_shape=jax.ShapeDtypeStruct((NPANEL * PW, NPANEL * PW), F32),
        compiler_params=params(),
        name="factor",
    )(*own_parts, *far_parts)

    count = maps.shape[3]
    found = jnp.sum(maps[0], axis=2)
    table = jnp.sum(maps[0] * jnp.arange(count), axis=2) + (1 - found) * count
    tables = jnp.stack([table[0], parent(table[1], 0)])

    return pl.pallas_call(
        functools.partial(front_kernel, owners, n_row, row_blocks),
        out_shape=jax.ShapeDtypeStruct((1, rows_dev, PW), F32),
        in_specs=[smem, smem, vmem, vmem] + [anywhere] * (2 * len(own_all)),
        out_specs=vmem,
        scratch_shapes=[
            pltpu.VMEM((2, n_row * rows_here + BLOCK, 3 * BLOCK), BF16),
            pltpu.SemaphoreType.DMA((2, len(own_all))),
        ],
        compiler_params=params(),
        name="front",
    )(tables, mask, diag, inverse, *own_all, *far_all)


def solution(mesh):
    in_specs = (
        P("front", None, "row", None),
        P("front", None, None, None),
        P("front", None, None),
        P("front", "row"),
    )
    out_specs = P("front", "row", "col")
    return jax.shard_map(body, mesh=mesh, in_specs=in_specs, out_specs=out_specs, check_vma=False)
```

time: 450 us -> 70.8 us (0.16)
  waiting for transfers between devices: 319 us -> 30.9 us
  other arithmetic: 55.2 us -> 0.06 us
  Pallas kernels: 0 us -> 20.8 us
  matrix products: 18.7 us -> 0 us
  blocking collectives: 17.9 us -> 0 us
  local copies, waits for them, and re-layouts: 21.3 us -> 6.16 us
  between operations: 13.7 us -> 0.09 us
  starting transfers between devices: 3.65 us -> 12.6 us
    psum x6 -> x0, waiting for transfers between devices: 236 us -> none  [broadcast(): return lax.psum(kept, axis)]
    ppermute x2 -> x15, waiting for transfers between devices: 83.2 us -> 30.9 us  [the longest x4 21.8 us: parent(): return lax.ppermute(x, ('front', 'row'), pairs)]
    another operation x11 -> x1, other arithmetic: 45.7 us -> 0.01 us  [body(): tables = jnp.stack([table[0], parent(table[1], 0)])]
    pallas_call x0 -> x4, Pallas kernels: none -> 20.8 us  [the longest x1 10.1 us: body(): pl.pallas_call(functools.partial(factor_kernel, len(own_parts)), out_shap...]
    all_gather x2 -> x0, blocking collectives: 17.9 us -> none  [the longest x1 9.08 us: body(): lax.all_gather(own_band, 'row', axis=0, tiled=True)]
    dot_general x6 -> x0, matrix products: 11.5 us -> none  [the longest x2 6.01 us: body(): product = jnp.dot(panel_rows, mirrored.T, precision=lax.Precision.HIGHEST)]
    ppermute x2 -> x15, starting transfers between devices: 3.04 us -> 12.6 us  [the longest x4 6.44 us: parent(): return lax.ppermute(x, ('front', 'row'), pairs)]
    squeeze x1 -> x0, local copies, waits for them, and re-layouts: 9.24 us -> none  [body(): kids[0, 1]]
  transfers between devices with their start and end apart: 8 -> 15, of which waited for: 7 -> 8; matrix products, arithmetic and copies ran while one was open for 3% -> 0% of each run, Pallas kernels for 0% -> 17%
where the time goes in v1:
time: 70.8 us; the launch traced here: 70.5 us
  waiting for transfers between devices  30.9 us (44%)
  Pallas kernels  20.8 us (29%)
  starting transfers between devices  12.6 us (18%)
  local copies, waits for them, and re-layouts  6.16 us (9%)
    ppermute x4, waiting for transfers between devices, parent(): return lax.ppermute(x, ('front', 'row'), pairs)  21.8 us
    pallas_call x1, Pallas kernels, body(): pl.pallas_call(functools.partial(factor_kernel, len(own_parts)), out_shap...  10.1 us
    ppermute x4, starting transfers between devices, parent(): return lax.ppermute(x, ('front', 'row'), pairs)  6.44 us
    pallas_call x1, Pallas kernels, body(): pl.pallas_call(functools.partial(front_kernel, owners, n_row, row_blocks)...  6.27 us
    unnamed x16, local copies, waits for them, and re-layouts  6.15 us
    ppermute x8, waiting for transfers between devices, partner(): return lax.ppermute(x, 'row', [(i, i ^ 1) for i in range(n_row)])  5.37 us
    ppermute x3, starting transfers between devices, along(): lax.ppermute(x, 'row', [(i, (i + 2 * by) % n_row) for i in range(n_row)])  4.82 us
    ppermute x3, waiting for transfers between devices, along(): lax.ppermute(x, 'row', [(i, (i + 2 * by) % n_row) for i in range(n_row)])  3.66 us
  transfers between devices with their start and end apart: 15, of which 8 were waited for; matrix products, arithmetic and copies ran while one was open for 0% of the time, Pallas kernels for 17%

profile of v1, /device:TPU:0, one launch (start us, length us, event | category | flops | bytes accessed | tf_op | source)
XLA Modules:
  0.0 70.5 jit_solution(8363213805945650346)
XLA Ops:
  0.0 0.8 %copy.5.maps = s32[1,2,72,24]{3,2,1,0:T(8,128)S(1)} copy(s32[1,2,72,24]{2,3,1,0:T(8,128)} %param.5) | data formatting | bytes 27648 | tf_op args[1]
  0.8 3.7 %copy-done = bf16[1,2,768,3072]{3,2,1,0:T(8,128)(2,1)S(1)} copy-done((bf16[1,2,768,3072]{3,2,1,0:T(8,128)(2,1)S(1)}, bf16[1,2,768,3072]{3,2,1,0:T(8,128)(2,1)}, u32[]{:S(2)}) %copy-start) | copy-done | bytes 9437208
  4.5 2.4 %bands.1 = (bf16[768,384]{1,0:T(8,128)(2,1)S(1)}, bf16[768,384]{1,0:T(8,128)(2,1)S(1)}) custom-call(s32[1,2,72,24]{3,2,1,0:T(8,128)S(1)} %copy.5.maps, bf16[1,2,768,3072]{3,2,1,0:T(8,128)(2,1)S(1)} %copy-done), custom_call_target="tpu_custom_call" | custom-call | tf_op jit(solution)/shard_map/bands/pallas_call | solution.py:316
  6.9 2.9 %collective-permute-start.11 = (bf16[768,384]{1,0:T(8,128)(2,1)S(1)}, bf16[768,384]{1,0:T(8,128)(2,1)S(1)}, u32[]{:S(2)}, u32[]{:S(2)}) collective-permute-start(bf16[768,384]{1,0:T(8,128)(2,1)S(1)} %get-tuple-element.12), channel_id=1, source_target_pairs={{0,16},{4,20},{8,24},{12,28},{16,0},{20,4},{24,8},{28,12},{1,17},{... | collective-permute-start | bytes 1769480 | tf_op jit(solution)/shard_map/ppermute | solution.py:297
  9.8 1.5 %collective-permute-start.8 = (bf16[768,384]{1,0:T(8,128)(2,1)S(1)}, bf16[768,384]{1,0:T(8,128)(2,1)S(1)}, u32[]{:S(2)}, u32[]{:S(2)}) collective-permute-start(bf16[768,384]{1,0:T(8,128)(2,1)S(1)} %get-tuple-element.11.refs_0_), channel_id=1, source_target_pairs={{0,8},{4,12},{8,0},{12,4},{1,9},{5,13},{9,1},{13,5},{2,10},{6,14},... | collective-permute-start | bytes 1769480 | tf_op jit(solution)/shard_map/ppermute | solution.py:287
  11.3 11.8 %collective-permute-done.11.refs_4_ = bf16[768,384]{1,0:T(8,128)(2,1)S(1)} collective-permute-done((bf16[768,384]{1,0:T(8,128)(2,1)S(1)}, bf16[768,384]{1,0:T(8,128)(2,1)S(1)}, u32[]{:S(2)}, u32[]{:S(2)}) %collective-permute-start.11) | collective-permute-done | bytes 589856 | tf_op jit(solution)/shard_map/ppermute | solution.py:297
  23.1 1.8 %collective-permute-start.12 = (bf16[768,384]{1,0:T(8,128)(2,1)S(1)}, bf16[768,384]{1,0:T(8,128)(2,1)S(1)}, u32[]{:S(2)}, u32[]{:S(2)}) collective-permute-start(bf16[768,384]{1,0:T(8,128)(2,1)S(1)} %collective-permute-done.11.refs_4_), channel_id=1, source_target_pairs={{0,8},{4,12},{8,0},{12,4},{1,9},{5,13},{9,1},{13,5},{2,10},{6,14},... | collective-permute-start | bytes 1769480 | tf_op jit(solution)/shard_map/ppermute | solution.py:287
  25.0 2.0 %window_blocks.1 = (bf16[400,128]{1,0:T(8,128)(2,1)S(1)}, bf16[384,128]{1,0:T(8,128)(2,1)S(1)}) custom-call(s32[1,2,72,24]{3,2,1,0:T(8,128)S(1)} %copy.5.maps, f32[1,2304]{1,0:T(1,128)S(1)} %copy-done.4, bf16[1,2,768,3072]{3,2,1,0:T(8,128)(2,1)S(1)} %copy-done.1), custom_call_target="tpu_custom_call" | custom-call | tf_op jit(solution)/shard_map/window_blocks/pallas_call | solution.py:299
  27.0 1.4 %collective-permute-start.5 = (bf16[384,128]{1,0:T(8,128)(2,1)S(1)}, bf16[384,128]{1,0:T(8,128)(2,1)S(1)}, u32[]{:S(2)}, u32[]{:S(2)}) collective-permute-start(bf16[384,128]{1,0:T(8,128)(2,1)S(1)} %get-tuple-element.10), channel_id=1, source_target_pairs={{0,24},{4,28},{8,16},{12,20},{16,8},{20,12},{24,0},{28,4},{1,25},{... | collective-permute-start | bytes 294920 | tf_op jit(solution)/shard_map/ppermute | solution.py:297
  28.8 1.8 %collective-permute-start = (s32[72]{0:T(128)S(1)}, s32[72]{0:T(128)S(1)}, u32[]{:S(2)}, u32[]{:S(2)}) collective-permute-start(s32[72]{0:T(128)S(1)} %get-tuple-element.14), channel_id=1, source_target_pairs={{0,16},{4,20},{8,24},{12,28},{16,0},{20,4},{24,8},{28,12},{1,17},{... | collective-permute-start | bytes 872 | tf_op jit(solution)/shard_map/ppermute | solution.py:297
  30.6 2.5 %collective-permute-done = s32[72]{0:T(128)S(1)} collective-permute-done((s32[72]{0:T(128)S(1)}, s32[72]{0:T(128)S(1)}, u32[]{:S(2)}, u32[]{:S(2)}) %collective-permute-start) | collective-permute-done | bytes 320 | tf_op jit(solution)/shard_map/ppermute | solution.py:297
  33.1 7.5 %collective-permute-done.5.refs_5_ = bf16[384,128]{1,0:T(8,128)(2,1)S(1)} collective-permute-done((bf16[384,128]{1,0:T(8,128)(2,1)S(1)}, bf16[384,128]{1,0:T(8,128)(2,1)S(1)}, u32[]{:S(2)}, u32[]{:S(2)}) %collective-permute-start.5) | collective-permute-done | bytes 98336 | tf_op jit(solution)/shard_map/ppermute | solution.py:297
  40.6 0.5 collective-permute-start.10
  41.2 0.4 collective-permute-start.2
  41.7 1.7 %collective-permute-done.2.refs_2_ = bf16[400,128]{1,0:T(8,128)(2,1)S(1)} collective-permute-done((bf16[400,128]{1,0:T(8,128)(2,1)S(1)}, bf16[400,128]{1,0:T(8,128)(2,1)S(1)}, u32[]{:S(2)}, u32[]{:S(2)}) %collective-permute-start.2) | collective-permute-done | bytes 102432 | tf_op jit(solution)/shard_map/ppermute | solution.py:290
  43.4 1.5 %collective-permute-start.1 = (bf16[400,128]{1,0:T(8,128)(2,1)S(1)}, bf16[400,128]{1,0:T(8,128)(2,1)S(1)}, u32[]{:S(2)}, u32[]{:S(2)}) collective-permute-start(bf16[400,128]{1,0:T(8,128)(2,1)S(1)} %get-tuple-element.9.refs_0_), channel_id=1, source_target_pairs={{0,8},{4,12},{8,0},{12,4},{1,9},{5,13},{9,1},{13,5},{2,10},{6,14},... | collective-permute-start | bytes 307208 | tf_op jit(solution)/shard_map/ppermute | solution.py:287
  44.9 3.7 %collective-permute-done.1.refs_1_ = bf16[400,128]{1,0:T(8,128)(2,1)S(1)} collective-permute-done((bf16[400,128]{1,0:T(8,128)(2,1)S(1)}, bf16[400,128]{1,0:T(8,128)(2,1)S(1)}, u32[]{:S(2)}, u32[]{:S(2)}) %collective-permute-start.1) | collective-permute-done | bytes 102432 | tf_op jit(solution)/shard_map/ppermute | solution.py:287
  48.6 1.3 %collective-permute-done.7.refs_7_ = bf16[384,128]{1,0:T(8,128)(2,1)S(1)} collective-permute-done((bf16[384,128]{1,0:T(8,128)(2,1)S(1)}, bf16[384,128]{1,0:T(8,128)(2,1)S(1)}, u32[]{:S(2)}, u32[]{:S(2)}) %collective-permute-start.7) | collective-permute-done | bytes 98336 | tf_op jit(solution)/shard_map/ppermute | solution.py:290
  49.9 0.6 copy-done.2
  50.8 1.2 %collective-permute-done.6.refs_6_ = bf16[384,128]{1,0:T(8,128)(2,1)} collective-permute-done((bf16[384,128]{1,0:T(8,128)(2,1)S(1)}, bf16[384,128]{1,0:T(8,128)(2,1)}, u32[]{:S(2)}, u32[]{:S(2)}) %collective-permute-start.6) | collective-permute-done | bytes 98336 | tf_op jit(solution)/shard_map/ppermute | solution.py:290
  52.1 1.1 %collective-permute-done.3.refs_3_ = bf16[400,128]{1,0:T(8,128)(2,1)S(1)} collective-permute-done((bf16[400,128]{1,0:T(8,128)(2,1)S(1)}, bf16[400,128]{1,0:T(8,128)(2,1)S(1)}, u32[]{:S(2)}, u32[]{:S(2)}) %collective-permute-start.3) | collective-permute-done | bytes 102432 | tf_op jit(solution)/shard_map/ppermute | solution.py:290
  53.2 0.9 %copy-done.3 = bf16[384,128]{1,0:T(8,128)(2,1)S(1)} copy-done((bf16[384,128]{1,0:T(8,128)(2,1)S(1)}, bf16[384,128]{1,0:T(8,128)(2,1)}, u32[]{:S(2)}) %copy-start.3) | copy-done | bytes 98328
  54.1 10.1 %factor.1.inverse = f32[256,256]{1,0:T(8,128)S(1)} custom-call(bf16[400,128]{1,0:T(8,128)(2,1)S(1)} %get-tuple-element.9.refs_0_, bf16[400,128]{1,0:T(8,128)(2,1)S(1)} %collective-permute-done.1.refs_1_, bf16[400,128]{1,0:T(8,128)(2,1)S(1)} %collective-permute-done.2.refs_2_, bf16[400,128]{1,0:T(8,128)(2,1)S(1)} %collective-permute-done.3.refs_3_, ...), custom_call_target="tpu_custom_call" | custom-call | tf_op jit(solution)/shard_map/factor/pallas_call | solution.py:336
  64.3 6.3 %front.1 = f32[1,2304,128]{2,1,0:T(8,128)} custom-call(s32[2,72]{1,0:T(2,128)S(1)} %pad_add_fusion.tables, s32[1,72,4]{2,1,0:T(8,128)S(1)} %copy.7.mask, f32[1,2304]{1,0:T(1,128)S(1)} %copy-done.4, f32[256,256]{1,0:T(8,128)S(1)} %factor.1.inverse, bf16[768,384]{1,0:T(8,128)(2,1)S(1)} %get-tuple-element.11.refs_0_, ...), custom_call_target="tpu_custom_call" | custom-call | tf_op jit(solution)/shard_map/front/pallas_call | solution.py:348
  (31 shorter events, 0.9 us)
Async XLA Ops:
  0.0 25.0 %copy-start.4 = (f32[1,2304]{1,0:T(1,128)S(1)}, f32[1,2304]{1,0:T(1,128)}, u32[]{:S(2)}) copy-start(f32[1,2304]{1,0:T(1,128)} %diag.3) | copy-start | bytes 27652
  0.8 3.7 %copy-start = (bf16[1,2,768,3072]{3,2,1,0:T(8,128)(2,1)S(1)}, bf16[1,2,768,3072]{3,2,1,0:T(8,128)(2,1)}, u32[]{:S(2)}) copy-start(bf16[1,2,768,3072]{3,2,1,0:T(8,128)(2,1)} %kids.3) | copy-start | bytes 28311556
  4.5 20.5 %copy-start.1 = (bf16[1,2,768,3072]{3,2,1,0:T(8,128)(2,1)S(1)}, bf16[1,2,768,3072]{3,2,1,0:T(8,128)(2,1)}, u32[]{:S(2)}) copy-start(bf16[1,2,768,3072]{3,2,1,0:T(8,128)(2,1)} %kids.3) | copy-start | bytes 28311556
  4.5 24.2 %copy-start.5 = (s32[1,2,72,24]{2,3,1,0:T(8,128)S(1)}, s32[1,2,72,24]{2,3,1,0:T(8,128)}, u32[]{:S(2)}) copy-start(s32[1,2,72,24]{2,3,1,0:T(8,128)} %param.5) | copy-start | bytes 41476
  4.5 46.1 %copy-start.6 = (s32[1,72,4]{1,2,0:T(4,128)S(1)}, s32[1,72,4]{1,2,0:T(4,128)}, u32[]{:S(2)}) copy-start(s32[1,72,4]{1,2,0:T(4,128)} %param.6) | copy-start | bytes 3460
  6.9 16.2 %collective-permute-start.11 = (bf16[768,384]{1,0:T(8,128)(2,1)S(1)}, bf16[768,384]{1,0:T(8,128)(2,1)S(1)}, u32[]{:S(2)}, u32[]{:S(2)}) collective-permute-start(bf16[768,384]{1,0:T(8,128)(2,1)S(1)} %get-tuple-element.12), channel_id=1, source_target_pairs={{0,16},{4,20},{8,24},{12,28},{16,0},{20,4},{24,8},{28,12},{1,17},{... | collective-permute-start | bytes 1769480 | tf_op jit(solution)/shard_map/ppermute | solution.py:297
  9.8 30.8 %collective-permute-start.8 = (bf16[768,384]{1,0:T(8,128)(2,1)S(1)}, bf16[768,384]{1,0:T(8,128)(2,1)S(1)}, u32[]{:S(2)}, u32[]{:S(2)}) collective-permute-start(bf16[768,384]{1,0:T(8,128)(2,1)S(1)} %get-tuple-element.11.refs_0_), channel_id=1, source_target_pairs={{0,8},{4,12},{8,0},{12,4},{1,9},{5,13},{9,1},{13,5},{2,10},{6,14},... | collective-permute-start | bytes 1769480 | tf_op jit(solution)/shard_map/ppermute | solution.py:287
  23.1 18.0 %collective-permute-start.12 = (bf16[768,384]{1,0:T(8,128)(2,1)S(1)}, bf16[768,384]{1,0:T(8,128)(2,1)S(1)}, u32[]{:S(2)}, u32[]{:S(2)}) collective-permute-start(bf16[768,384]{1,0:T(8,128)(2,1)S(1)} %collective-permute-done.11.refs_4_), channel_id=1, source_target_pairs={{0,8},{4,12},{8,0},{12,4},{1,9},{5,13},{9,1},{13,5},{2,10},{6,14},... | collective-permute-start | bytes 1769480 | tf_op jit(solution)/shard_map/ppermute | solution.py:287
  27.0 13.6 %collective-permute-start.5 = (bf16[384,128]{1,0:T(8,128)(2,1)S(1)}, bf16[384,128]{1,0:T(8,128)(2,1)S(1)}, u32[]{:S(2)}, u32[]{:S(2)}) collective-permute-start(bf16[384,128]{1,0:T(8,128)(2,1)S(1)} %get-tuple-element.10), channel_id=1, source_target_pairs={{0,24},{4,28},{8,16},{12,20},{16,8},{20,12},{24,0},{28,4},{1,25},{... | collective-permute-start | bytes 294920 | tf_op jit(solution)/shard_map/ppermute | solution.py:297
  28.5 12.8 %collective-permute-start.4 = (bf16[384,128]{1,0:T(8,128)(2,1)S(1)}, bf16[384,128]{1,0:T(8,128)(2,1)S(1)}, u32[]{:S(2)}, u32[]{:S(2)}) collective-permute-start(bf16[384,128]{1,0:T(8,128)(2,1)S(1)} %get-tuple-element.10), channel_id=1, source_target_pairs={{0,16},{4,20},{8,24},{12,28},{16,0},{20,4},{24,8},{28,12},{1,17},{... | collective-permute-start | bytes 294920 | tf_op jit(solution)/shard_map/ppermute | solution.py:297
  28.8 4.3 %collective-permute-start = (s32[72]{0:T(128)S(1)}, s32[72]{0:T(128)S(1)}, u32[]{:S(2)}, u32[]{:S(2)}) collective-permute-start(s32[72]{0:T(128)S(1)} %get-tuple-element.14), channel_id=1, source_target_pairs={{0,16},{4,20},{8,24},{12,28},{16,0},{20,4},{24,8},{28,12},{1,17},{... | collective-permute-start | bytes 872 | tf_op jit(solution)/shard_map/ppermute | solution.py:297
  33.1 31.1 %collective-permute-start.9 = (bf16[768,384]{1,0:T(8,128)(2,1)S(1)}, bf16[768,384]{1,0:T(8,128)(2,1)S(1)}, u32[]{:S(2)}, u32[]{:S(2)}) collective-permute-start(bf16[768,384]{1,0:T(8,128)(2,1)S(1)} %get-tuple-element.11.refs_0_), channel_id=1, source_target_pairs={{0,4},{4,0},{8,12},{12,8},{1,5},{5,1},{9,13},{13,9},{2,6},{6,2},{1... | collective-permute-start | bytes 1769480 | tf_op jit(solution)/shard_map/ppermute | solution.py:290
  40.6 23.6 %collective-permute-start.13 = (bf16[768,384]{1,0:T(8,128)(2,1)S(1)}, bf16[768,384]{1,0:T(8,128)(2,1)}, u32[]{:S(2)}, u32[]{:S(2)}) collective-permute-start(bf16[768,384]{1,0:T(8,128)(2,1)S(1)} %collective-permute-done.11.refs_4_), channel_id=1, source_target_pairs={{0,4},{4,0},{8,12},{12,8},{1,5},{5,1},{9,13},{13,9},{2,6},{6,2},{1... | collective-permute-start | bytes 1769480 | tf_op jit(solution)/shard_map/ppermute | solution.py:290
  40.6 23.6 %collective-permute-start.10 = (bf16[768,384]{1,0:T(8,128)(2,1)S(1)}, bf16[768,384]{1,0:T(8,128)(2,1)}, u32[]{:S(2)}, u32[]{:S(2)}) collective-permute-start(bf16[768,384]{1,0:T(8,128)(2,1)S(1)} %collective-permute-done.8.refs_1_), channel_id=1, source_target_pairs={{0,4},{4,0},{8,12},{12,8},{1,5},{5,1},{9,13},{13,9},{2,6},{6,2},{1... | collective-permute-start | bytes 1769480 | tf_op jit(solution)/shard_map/ppermute | solution.py:290
  41.1 23.1 %collective-permute-start.14 = (bf16[768,384]{1,0:T(8,128)(2,1)S(1)}, bf16[768,384]{1,0:T(8,128)(2,1)}, u32[]{:S(2)}, u32[]{:S(2)}) collective-permute-start(bf16[768,384]{1,0:T(8,128)(2,1)S(1)} %collective-permute-done.12.refs_5_), channel_id=1, source_target_pairs={{0,4},{4,0},{8,12},{12,8},{1,5},{5,1},{9,13},{13,9},{2,6},{6,2},{1... | collective-permute-start | bytes 1769480 | tf_op jit(solution)/shard_map/ppermute | solution.py:290
  41.2 2.2 %collective-permute-start.2 = (bf16[400,128]{1,0:T(8,128)(2,1)S(1)}, bf16[400,128]{1,0:T(8,128)(2,1)S(1)}, u32[]{:S(2)}, u32[]{:S(2)}) collective-permute-start(bf16[400,128]{1,0:T(8,128)(2,1)S(1)} %get-tuple-element.9.refs_0_), channel_id=1, source_target_pairs={{0,4},{4,0},{8,12},{12,8},{1,5},{5,1},{9,13},{13,9},{2,6},{6,2},{1... | collective-permute-start | bytes 307208 | tf_op jit(solution)/shard_map/ppermute | solution.py:290
  43.4 5.2 %collective-permute-start.1 = (bf16[400,128]{1,0:T(8,128)(2,1)S(1)}, bf16[400,128]{1,0:T(8,128)(2,1)S(1)}, u32[]{:S(2)}, u32[]{:S(2)}) collective-permute-start(bf16[400,128]{1,0:T(8,128)(2,1)S(1)} %get-tuple-element.9.refs_0_), channel_id=1, source_target_pairs={{0,8},{4,12},{8,0},{12,4},{1,9},{5,13},{9,1},{13,5},{2,10},{6,14},... | collective-permute-start | bytes 307208 | tf_op jit(solution)/shard_map/ppermute | solution.py:287
  48.6 1.3 %collective-permute-start.7 = (bf16[384,128]{1,0:T(8,128)(2,1)S(1)}, bf16[384,128]{1,0:T(8,128)(2,1)S(1)}, u32[]{:S(2)}, u32[]{:S(2)}) collective-permute-start(bf16[384,128]{1,0:T(8,128)(2,1)S(1)} %collective-permute-done.5.refs_5_), channel_id=1, source_target_pairs={{0,4},{4,0},{8,12},{12,8},{1,5},{5,1},{9,13},{13,9},{2,6},{6,2},{1... | collective-permute-start | bytes 294920 | tf_op jit(solution)/shard_map/ppermute | solution.py:290
  49.9 0.6 copy-start.2
  50.5 1.4 %collective-permute-start.6 = (bf16[384,128]{1,0:T(8,128)(2,1)S(1)}, bf16[384,128]{1,0:T(8,128)(2,1)}, u32[]{:S(2)}, u32[]{:S(2)}) collective-permute-start(bf16[384,128]{1,0:T(8,128)(2,1)S(1)} %collective-permute-done.4.refs_4_), channel_id=1, source_target_pairs={{0,4},{4,0},{8,12},{12,8},{1,5},{5,1},{9,13},{13,9},{2,6},{6,2},{1... | collective-permute-start | bytes 294920 | tf_op jit(solution)/shard_map/ppermute | solution.py:290
  51.9 1.3 %collective-permute-start.3 = (bf16[400,128]{1,0:T(8,128)(2,1)S(1)}, bf16[400,128]{1,0:T(8,128)(2,1)S(1)}, u32[]{:S(2)}, u32[]{:S(2)}) collective-permute-start(bf16[400,128]{1,0:T(8,128)(2,1)S(1)} %collective-permute-done.1.refs_1_), channel_id=1, source_target_pairs={{0,4},{4,0},{8,12},{12,8},{1,5},{5,1},{9,13},{13,9},{2,6},{6,2},{1... | collective-permute-start | bytes 307208 | tf_op jit(solution)/shard_map/ppermute | solution.py:290
  53.2 0.9 %copy-start.3 = (bf16[384,128]{1,0:T(8,128)(2,1)S(1)}, bf16[384,128]{1,0:T(8,128)(2,1)}, u32[]{:S(2)}) copy-start(bf16[384,128]{1,0:T(8,128)(2,1)} %copy-done.2) | copy-start | bytes 294916

commit v2 on v1

v2 whole, which is shorter than its diff:
```python
import functools

import jax
import jax.numpy as jnp
from jax import lax
from jax.experimental import pallas as pl
from jax.experimental.pallas import tpu as pltpu
from jax.sharding import PartitionSpec as P

BLOCK = 128
PW = 128
NPANEL = 2
F32 = jnp.float32
BF16 = jnp.bfloat16
HIGHEST = lax.Precision.HIGHEST
MIB = 1024 * 1024


def params(mib=40):
    return pltpu.CompilerParams(vmem_limit_bytes=mib * MIB)


def select_kernel(maps, diag, kids, tables, *refs):
    own_side, own_rest, far_window, far_side, far_pair, far_column, sems = refs
    lines = far_window.shape[0]
    me, col_index = lax.axis_index("row"), lax.axis_index("col")
    rows = kids.shape[2]
    local = rows // BLOCK
    none = kids.shape[3] // BLOCK
    places = maps.shape[3]
    child_id = lax.broadcasted_iota(jnp.int32, (none, places), 0)
    place_id = lax.broadcasted_iota(jnp.int32, (1, places), 1)
    found = []
    for child in range(2):
        ones = maps[0, child].astype(F32)
        line = jnp.sum(ones * (child_id - none).astype(F32), axis=0, keepdims=True) + none
        tables[child : child + 1, :] = line.astype(jnp.int32)
        found.append(
            [
                jnp.sum(jnp.where(place_id == w, line, 0.0)).astype(jnp.int32)
                for w in (0, 1, col_index)
            ]
        )
        if child == 1:
            line = jnp.broadcast_to(line, (16, places)).astype(BF16)
            far_side[3 * BLOCK : lines, 0:places] = line
            far_window[3 * BLOCK :, 0:places] = line
    copies = []

    def add(here, source, target):
        copy = pltpu.make_async_copy(source, target, sems.at[len(copies)])
        copies.append((here, copy))

        @pl.when(here)
        def _():
            copy.start()

        @pl.when(jnp.logical_not(here))
        def _():
            target[...] = jnp.zeros_like(target)

    def columns(start, size, child, col):
        return kids.at[0, child, pl.ds(start, size), pl.ds(pl.multiple_of(col * BLOCK, BLOCK), BLOCK)]

    for child, out in ((1, far_window), (0, own_side), (1, far_side)):
        for at, (w, p) in enumerate(((0, 0), (1, 0), (1, 1))):
            row, col = found[child][w], found[child][p]
            offset = row - me * local
            here = (row < none) & (col < none) & (offset >= 0) & (offset < local)
            start = pl.multiple_of(offset * BLOCK, BLOCK)
            add(here, columns(start, BLOCK, child, col), out.at[pl.ds(at * BLOCK, BLOCK)])
    half = rows // 2
    here, other = (
        pl.multiple_of(side * half, half) for side in (col_index % 2, 1 - col_index % 2)
    )
    side = [(0, here, half), (1, here, half)]
    rest = [(0, other, half), (1, other, half)]
    column = [(2, 0, rows)]
    for child, out, at, parts in (
        (0, own_side, lines, side + column),
        (1, far_side, lines, side + column),
        (1, far_pair, 0, side + rest),
        (1, far_column, 0, column),
        (0, own_rest, 0, rest),
    ):
        for p, start, size in parts:
            col = found[child][p]
            add(col < none, columns(start, size, child, col), out.at[pl.ds(at, size)])
            at += size

    line = lax.broadcasted_iota(jnp.int32, (16, BLOCK), 0)
    pieces = jnp.zeros((16, BLOCK), F32)
    for p in range(NPANEL):
        rest = jnp.broadcast_to(diag[0:1, p * PW : (p + 1) * PW], (16, BLOCK))
        for at in range(3):
            part = rest.astype(BF16).astype(F32)
            pieces = jnp.where(line == 3 * p + at, part, pieces)
            rest = rest - part
    own_side[3 * BLOCK : lines, :] = jnp.where(me == 0, pieces, 0.0).astype(BF16)
    for here, copy in copies:

        @pl.when(here)
        def _():
            copy.wait()


def cost(microseconds):
    return pl.CostEstimate(flops=microseconds * 10**9, bytes_accessed=0, transcendentals=0)


def inverse_factor(tiles):
    tiles = list(tiles)
    count = len(tiles)
    lane = lax.broadcasted_iota(jnp.int32, (8, BLOCK), 1)
    line = lax.broadcasted_iota(jnp.int32, (8, BLOCK), 0)
    wide = lambda x: jnp.broadcast_to(x, (8, BLOCK))
    result = []
    for b in range(count):
        low = 8 * b
        tile = tiles[b]
        columns = [wide(tile[:, low + j : low + j + 1]) for j in range(8)]
        d = [[wide(columns[j][i : i + 1, :]) if i >= j else None for j in range(8)] for i in range(8)]
        inside = (lane >= low) & (lane < low + 8)
        rows = [
            jnp.where(inside, (lane == low + i).astype(F32), wide(tile[i : i + 1, :]))
            for i in range(8)
        ]
        scale = []
        for j in range(8):
            scale.append(lax.rsqrt(d[j][j]))
            for i in range(j + 1, 8):
                d[i][j] = d[i][j] * scale[j]
            for k in range(j + 1, 8):
                for i in range(k, 8):
                    d[i][k] = d[i][k] - d[i][j] * d[k][j]
            rows[j] = rows[j] * scale[j]
            for i in range(j + 1, 8):
                rows[i] = rows[i] - d[i][j] * rows[j]
        merged = rows[0]
        for j in range(1, 8):
            merged = jnp.where(line == j, rows[j], merged)
        result.append(jnp.where(lane < low + 8, merged, 0.0))
        for t in range(b + 1, count):
            tile = tiles[t]
            columns = [wide(tile[:, low + j : low + j + 1]) for j in range(8)]
            tile = jnp.where(inside, 0.0, tile)
            for j in range(8):
                for m in range(j):
                    columns[j] = columns[j] - columns[m] * d[j][m]
                columns[j] = columns[j] * scale[j]
                tile = tile - columns[j] * rows[j]
            tiles[t] = tile
    return result


def dot(a, b, lhs=1, rhs=0):
    return lax.dot_general(
        a, b, (((lhs,), (rhs,)), ((), ())), precision=HIGHEST, preferred_element_type=F32
    )


def factor_kernel(n_own, *refs):
    own, far, out = refs[:n_own], refs[n_own:-1], refs[-1]

    def total(at):
        value = None
        for ref in own + far:
            block = ref[at * BLOCK : (at + 1) * BLOCK, :].astype(F32)
            value = block if value is None else value + block
        return value

    pieces = None
    for ref in own:
        part = ref[3 * BLOCK : 3 * BLOCK + 16, :].astype(F32)
        pieces = part if pieces is None else pieces + part
    eye = lax.broadcasted_iota(jnp.int32, (BLOCK, BLOCK), 0) == lax.broadcasted_iota(
        jnp.int32, (BLOCK, BLOCK), 1
    )

    def diagonal(p):
        line = pieces[3 * p : 3 * p + 1] + pieces[3 * p + 1 : 3 * p + 2]
        line = line + pieces[3 * p + 2 : 3 * p + 3]
        return jnp.where(eye, jnp.broadcast_to(line, (BLOCK, BLOCK)), 0.0)

    def invert(block):
        return jnp.concatenate(
            inverse_factor([block[8 * t : 8 * t + 8, :] for t in range(BLOCK // 8)]), axis=0
        )

    first = invert(total(0) + diagonal(0))
    cross = dot(total(1), first, 1, 1)
    second = invert(total(2) + diagonal(1) - dot(cross, cross, 1, 1))
    out[0:BLOCK, 0:BLOCK] = first
    out[0:BLOCK, BLOCK:] = jnp.zeros((BLOCK, BLOCK), F32)
    out[BLOCK:, 0:BLOCK] = -dot(second, dot(cross, first))
    out[BLOCK:, BLOCK:] = second


def product_kernel(layout, n_row, lines, tables, inverse, *refs):
    sources = list(refs[:-2])
    weight, product = refs[-2:]
    me, col_index = lax.axis_index("row"), lax.axis_index("col")
    rows = (product.shape[1] - BLOCK) // n_row
    half = rows // 2
    wide = NPANEL * PW
    parts = []
    for child, owner, whole in layout:
        first = sources.pop(0)
        second = first if whole else sources.pop(0)
        parts.append((child, owner(me), first, 0 if whole else lines, col_index % 2))
        parts.append((child, owner(me), second, rows if whole else 0, 1 - col_index % 2))

    mirrored = jnp.zeros((BLOCK, wide), F32)
    for child, owner, ref, at, side in parts:
        index = tables[child, col_index] * BLOCK
        for step in range(0, BLOCK, BLOCK // 2):
            place = index + step - owner * rows - side * half
            inside = (place >= 0) & (place < half)
            place = pl.multiple_of(jnp.where(inside, place, 0), BLOCK // 2)
            lines = [ref[pl.ds(at + p * half + place, BLOCK // 2), :] for p in range(NPANEL)]
            lines = jnp.where(inside, jnp.concatenate(lines, axis=1).astype(F32), 0.0)
            empty = jnp.zeros_like(lines)
            lines = [lines, empty] if step == 0 else [empty, lines]
            mirrored = mirrored + jnp.concatenate(lines, axis=0)

    lower = inverse[...]
    row_id = lax.broadcasted_iota(jnp.int32, (wide, PW), 0)
    col_id = lax.broadcasted_iota(jnp.int32, (wide, PW), 1)
    picked = -(row_id == col_id + col_index * PW).astype(F32)
    solved = jnp.where(col_index < NPANEL, picked, dot(lower, mirrored, 1, 1))
    weight[...] = dot(lower, solved, 0, 0)
    high = weight[...].astype(BF16)
    low = (weight[...] - high.astype(F32)).astype(BF16)
    both = jnp.concatenate([high, low], axis=1)
    for child, owner, ref, at, side in parts:
        left = jnp.concatenate([ref[at + p * half : at + (p + 1) * half, :] for p in range(NPANEL)], axis=1)
        value = jnp.dot(left, both, preferred_element_type=F32)
        start = pl.multiple_of(owner * rows + side * half, half)
        product[child, pl.ds(start, half), :] = value[:, :PW] + value[:, PW:]
    for child in range(2):
        product[child, n_row * rows :, :] = jnp.zeros((BLOCK, PW), F32)


def front_kernel(layout, n_row, row_blocks, tables, mask, diag, weight, product, *refs):
    sources = refs[: len(layout)]
    out, buffer = refs[len(layout) :]
    me, col_index = lax.axis_index("row"), lax.axis_index("col")
    rows = (product.shape[1] - BLOCK) // n_row
    is_panel = col_index < NPANEL
    for (child, owner, at), ref in zip(layout, sources):
        start = pl.multiple_of(owner(me) * rows, rows)
        buffer[child, pl.ds(start, rows), :] = ref[at : at + rows, :]
    for child in range(2):
        buffer[child, n_row * rows :, :] = jnp.zeros((BLOCK, PW), BF16)
    for p in range(row_blocks):
        at = me * row_blocks + p
        first, second = (
            pl.ds(pl.multiple_of(tables[child, at] * BLOCK, BLOCK), BLOCK) for child in range(2)
        )
        base = buffer[0, first, :].astype(F32) + buffer[1, second, :].astype(F32)
        keep = jnp.where(is_panel | (mask[0, col_index, at] > 0), 1.0, 0.0)
        value = jnp.where(is_panel, 0.0, base) - keep * (product[0, first, :] + product[1, second, :])
        out[0, p * BLOCK : (p + 1) * BLOCK, :] = value

    row_id = lax.broadcasted_iota(jnp.int32, (BLOCK, BLOCK), 0)
    col_id = lax.broadcasted_iota(jnp.int32, (BLOCK, BLOCK), 1)

    def diagonal(p):
        line = jnp.broadcast_to(diag[0:1, p * BLOCK : (p + 1) * BLOCK], (BLOCK, BLOCK))
        return jnp.where(row_id == col_id, line, 0.0)

    for p in range(NPANEL):

        @pl.when(me == 0)
        def _():
            keep = jnp.where(is_panel | (mask[0, col_index, p] > 0), 1.0, 0.0)
            column = jnp.sum(diagonal(p), axis=1, keepdims=True)
            value = out[0, p * BLOCK : (p + 1) * BLOCK, :]
            value = value - keep * column * weight[p * BLOCK : (p + 1) * BLOCK, :]
            above = row_id + p * BLOCK < col_id + col_index * PW
            out[0, p * BLOCK : (p + 1) * BLOCK, :] = jnp.where(is_panel & above, 0.0, value)

    for p in range(row_blocks):

        @pl.when(jnp.logical_not(is_panel) & (me * row_blocks + p == col_index))
        def _():
            out[0, p * BLOCK : (p + 1) * BLOCK, :] += diagonal(p)


def body(kids, maps, mask, diag):
    fronts, n_row, n_col = (lax.axis_size(name) for name in ("front", "row", "col"))
    chips = n_row // 2
    rows_dev = diag.shape[1]
    row_blocks = rows_dev // BLOCK
    rows_here = kids.shape[2]
    vmem, smem = pl.BlockSpec(memory_space=pltpu.VMEM), pl.BlockSpec(memory_space=pltpu.SMEM)
    anywhere = pl.BlockSpec(memory_space=pl.ANY)

    def along(x, by):
        return lax.ppermute(x, "row", [(i, (i + 2 * by) % n_row) for i in range(n_row)])

    def partner(x):
        return lax.ppermute(x, "row", [(i, i ^ 1) for i in range(n_row)])

    def parent(x, by):
        pairs = []
        for f in range(fronts):
            for i in range(n_row):
                pairs.append((f * n_row + i, (f - 1) % fronts * n_row + (i + 2 * by) % n_row))
        return lax.ppermute(x, ("front", "row"), pairs)

    def neighbour(x):
        return lax.ppermute(x, "col", [(i, i ^ 1) for i in range(n_col)])

    lines = 3 * BLOCK + 16
    maps = jnp.swapaxes(maps, 2, 3)
    mask = jnp.swapaxes(mask, 1, 2)
    side = lines + 2 * rows_here
    shapes = [side, rows_here, lines, side, 2 * rows_here, rows_here]
    shapes = [jax.ShapeDtypeStruct((size, BLOCK), BF16) for size in shapes]
    shapes = [jax.ShapeDtypeStruct((2, maps.shape[3]), jnp.int32)] + shapes
    tables, own_side, own_rest, far_window, far_side, far_pair, far_column = pl.pallas_call(
        select_kernel,
        out_shape=shapes,
        in_specs=[vmem, vmem, pl.BlockSpec(memory_space=pltpu.HBM)],
        out_specs=[vmem] * len(shapes),
        scratch_shapes=[pltpu.SemaphoreType.DMA((22,))],
        compiler_params=params(55),
        cost_estimate=cost(2),
        name="select",
    )(maps, diag, kids)

    def both(x):
        return x, partner(x)

    far_windows = [parent(far_window, s) for s in range(1, chips)]
    own_sides = [along(own_side, s) for s in range(1, chips)]
    far_near = parent(far_side, 0)
    far_windows, own_sides, far_near, own_side = lax.optimization_barrier(
        (far_windows, own_sides, far_near, own_side)
    )
    far_windows = [both(x) for x in far_windows]
    own_sides = [both(own_side)] + [both(x) for x in own_sides]
    far_near = both(far_near)
    far_pairs = [parent(far_pair, s) for s in range(1, chips)]
    far_columns = [parent(far_column, s) for s in range(1, chips)]
    middle = slice(lines, lines + rows_here)
    own_others = [neighbour(x[middle]) for x, _ in own_sides[1:]]
    far_other = neighbour(far_near[0][middle])
    own_parts = [x for pair in own_sides for x in pair]
    far_parts = list(far_near) + [x for pair in far_windows for x in pair]
    far_table = far_near[0][3 * BLOCK, : tables.shape[1]].astype(jnp.int32)
    inverse = pl.pallas_call(
        functools.partial(factor_kernel, len(own_parts)),
        out_shape=jax.ShapeDtypeStruct((NPANEL * PW, NPANEL * PW), F32),
        compiler_params=params(),
        cost_estimate=cost(0),
        name="factor",
    )(*own_parts, *far_parts)

    remote = (own_rest, own_others, far_other, far_pairs, far_columns)
    remote, inverse = lax.optimization_barrier((remote, inverse))
    own_rest, own_others, far_other, far_pairs, far_columns = remote

    def owner(side, s):
        def position(me):
            core = me + 1 - 2 * (me % 2) if side else me
            return (core + n_row - 2 * s) % n_row

        return position

    pairs, columns, arrays, column_arrays = [], [], [], []

    def add(child, s, first, second, column, at):
        for core in range(2):
            pairs.append((child, owner(core, s), second is None))
            arrays.extend([first[core]] if second is None else [first[core], second[core]])
            columns.append((child, owner(core, s), at))
            column_arrays.append(column[core])

    at = lines + rows_here
    add(0, 0, own_sides[0], both(own_rest), own_sides[0], at)
    add(1, 0, far_near, both(far_other), far_near, at)
    for s in range(1, chips):
        add(0, s, own_sides[s], both(own_others[s - 1]), own_sides[s], at)
        add(1, s, both(far_pairs[s - 1]), None, both(far_columns[s - 1]), 0)

    tables = jnp.stack([tables[0], far_table])
    height = n_row * rows_here + BLOCK
    weight, product = pl.pallas_call(
        functools.partial(product_kernel, pairs, n_row, lines),
        out_shape=[
            jax.ShapeDtypeStruct((NPANEL * PW, PW), F32),
            jax.ShapeDtypeStruct((2, height, PW), F32),
        ],
        in_specs=[smem] + [vmem] * (1 + len(arrays)),
        out_specs=[vmem, vmem],
        compiler_params=params(),
        cost_estimate=cost(3),
        name="product",
    )(tables, inverse, *arrays)

    return pl.pallas_call(
        functools.partial(front_kernel, columns, n_row, row_blocks),
        out_shape=jax.ShapeDtypeStruct((1, rows_dev, PW), F32),
        in_specs=[smem, smem] + [vmem] * (3 + len(column_arrays)),
        out_specs=vmem,
        scratch_shapes=[pltpu.VMEM((2, height, PW), BF16)],
        compiler_params=params(),
        cost_estimate=cost(2),
        name="front",
    )(tables, mask, diag, weight, product, *column_arrays)


def solution(mesh):
    in_specs = (
        P("front", None, "row", None),
        P("front", None, None, None),
        P("front", None, None),
        P("front", "row"),
    )
    out_specs = P("front", "row", "col")
    return jax.shard_map(body, mesh=mesh, in_specs=in_specs, out_specs=out_specs, check_vma=False)
```

time: 70.8 us -> 47.4 us (0.67)
  waiting for transfers between devices: 30.9 us -> 16.8 us
  local copies, waits for them, and re-layouts: 6.16 us -> 1.09 us
  Pallas kernels: 20.8 us -> 18.1 us
  starting transfers between devices: 12.6 us -> 11 us
    ppermute x4, waiting for transfers between devices: 21.8 us -> 14 us  [parent(): return lax.ppermute(x, ('front', 'row'), pairs)]
    unnamed x16 -> x12, local copies, waits for them, and re-layouts: 6.15 us -> 1.06 us
    ppermute x3 -> x1, waiting for transfers between devices: 3.66 us -> 0.01 us  [along(): lax.ppermute(x, 'row', [(i, (i + 2 * by) % n_row) for i in range(n_row)])]
    ppermute x8 -> x9, waiting for transfers between devices: 5.37 us -> 2.8 us  [partner(): return lax.ppermute(x, 'row', [(i, i ^ 1) for i in range(n_row)])]
    ppermute x4, starting transfers between devices: 6.44 us -> 4.11 us  [parent(): return lax.ppermute(x, ('front', 'row'), pairs)]
    ppermute x0 -> x2, starting transfers between devices: none -> 2.03 us  [neighbour(): return lax.ppermute(x, 'col', [(i, i ^ 1) for i in range(n_col)])]
    pallas_call x3, Pallas kernels: 10.7 us -> 8.84 us  [the longest x1 3.74 us: body(): pl.pallas_call(select_kernel, out_shape=shapes, in_specs=[vmem, vmem, pl....]
    ppermute x3 -> x1, starting transfers between devices: 4.82 us -> 3 us  [along(): lax.ppermute(x, 'row', [(i, (i + 2 * by) % n_row) for i in range(n_row)])]
  transfers between devices with their start and end apart: 15 -> 16, of which waited for: 8 -> 7; matrix products, arithmetic and copies ran while one was open for 0% -> 0% of each run, Pallas kernels for 17% -> 26%
where the time goes in v2:
time: 47.4 us; the launch traced here: 47.1 us
  Pallas kernels  18.1 us (38%)
  waiting for transfers between devices  16.8 us (35%)
  starting transfers between devices  11 us (23%)
  local copies, waits for them, and re-layouts  1.09 us (2%)
    ppermute x4, waiting for transfers between devices, parent(): return lax.ppermute(x, ('front', 'row'), pairs)  14 us
    pallas_call x1, Pallas kernels, body(): pl.pallas_call(functools.partial(factor_kernel, len(own_parts)), out_shap...  9.22 us
    ppermute x4, starting transfers between devices, parent(): return lax.ppermute(x, ('front', 'row'), pairs)  4.11 us
    pallas_call x1, Pallas kernels, body(): pl.pallas_call(select_kernel, out_shape=shapes, in_specs=[vmem, vmem, pl....  3.74 us
    ppermute x1, starting transfers between devices, along(): lax.ppermute(x, 'row', [(i, (i + 2 * by) % n_row) for i in range(n_row)])  3 us
    pallas_call x1, Pallas kernels, body(): pl.pallas_call(functools.partial(product_kernel, pairs, n_row, lines), ou...  2.87 us
    ppermute x9, waiting for transfers between devices, partner(): return lax.ppermute(x, 'row', [(i, i ^ 1) for i in range(n_row)])  2.8 us
    pallas_call x1, Pallas kernels, body(): pl.pallas_call(functools.partial(front_kernel, columns, n_row, row_blocks...  2.23 us
  transfers between devices with their start and end apart: 16, of which 7 were waited for; matrix products, arithmetic and copies ran while one was open for 0% of the time, Pallas kernels for 26%

profile of v2, /device:TPU:0, one launch (start us, length us, event | category | flops | bytes accessed | tf_op | source)
XLA Modules:
  0.0 47.1 jit_solution(2302630345943741994)
XLA Ops:
  0.0 3.7 %select.1 = (s32[2,72]{1,0:T(2,128)}, bf16[1936,128]{1,0:T(8,128)(2,1)}, bf16[768,128]{1,0:T(8,128)(2,1)}, bf16[400,128]{1,0:T(8,128)(2,1)}, bf16[1936,128]{1,0:...) custom-call(s32[1,2,24,72]{3,2,1,0:T(8,128)} %bitcast.3, f32[1,2304]{1,0:T(1,128)} %diag.3, ...), custom_call_target="tpu_custom_call" | custom-call | flops 2000000000 | tf_op jit(solution)/shard_map/select/pallas_call | solution.py:322
  3.8 3.0 %collective-permute-start.1 = (bf16[1936,128]{1,0:T(8,128)(2,1)}, bf16[1936,128]{1,0:T(8,128)(2,1)S(1)}, u32[]{:S(2)}, u32[]{:S(2)}) collective-permute-start(bf16[1936,128]{1,0:T(8,128)(2,1)} %get-tuple-element.33.refs_0_), channel_id=1, source_target_pairs={{0,8},{4,12},{8,0},{12,4},{1,9},{5,13},{9,1},{13,5},{2,10},{6,14},... | collective-permute-start | bytes 1486856 | tf_op jit(solution)/shard_map/ppermute | solution.py:300
  6.8 0.5 collective-permute-start.2
  7.2 1.1 %collective-permute-start = (bf16[400,128]{1,0:T(8,128)(2,1)}, bf16[400,128]{1,0:T(8,128)(2,1)S(1)}, u32[]{:S(2)}, u32[]{:S(2)}) collective-permute-start(bf16[400,128]{1,0:T(8,128)(2,1)} %get-tuple-element.25), channel_id=1, source_target_pairs={{0,24},{4,28},{8,16},{12,20},{16,8},{20,12},{24,0},{28,4},{1,25},{... | collective-permute-start | bytes 307208 | tf_op jit(solution)/shard_map/ppermute | solution.py:310
  8.3 12.4 %collective-permute-done.refs_6_ = bf16[400,128]{1,0:T(8,128)(2,1)S(1)} collective-permute-done((bf16[400,128]{1,0:T(8,128)(2,1)}, bf16[400,128]{1,0:T(8,128)(2,1)S(1)}, u32[]{:S(2)}, u32[]{:S(2)}) %collective-permute-start) | collective-permute-done | bytes 102432 | tf_op jit(solution)/shard_map/ppermute | solution.py:310
  20.7 1.2 %collective-permute-done.2.refs_4_.refs_2_ = bf16[1936,128]{1,0:T(8,128)(2,1)S(1)} collective-permute-done((bf16[1936,128]{1,0:T(8,128)(2,1)}, bf16[1936,128]{1,0:T(8,128)(2,1)S(1)}, u32[]{:S(2)}, u32[]{:S(2)}) %collective-permute-start.2) | collective-permute-done | bytes 495648 | tf_op jit(solution)/shard_map/ppermute | solution.py:310
  22.0 0.5 %collective-permute-start.8 = (bf16[1936,128]{1,0:T(8,128)(2,1)S(1)}, bf16[1936,128]{1,0:T(8,128)(2,1)S(1)}, u32[]{:S(2)}, u32[]{:S(2)}) collective-permute-start(bf16[1936,128]{1,0:T(8,128)(2,1)S(1)} %collective-permute-done.1.refs_2_.refs_8_.refs_4_), channel_id=1, source_target_pairs={{0,4},{4,0},{8,12},{12,8},{1,5},{5,1},{9,13},{13,9},{2,6},{6,2},{1... | collective-permute-start | bytes 1486856 | tf_op jit(solution)/shard_map/ppermute | solution.py:303
  22.5 1.3 %collective-permute-start.5 = (bf16[1536,128]{1,0:T(8,128)(2,1)}, bf16[1536,128]{1,0:T(8,128)(2,1)S(1)}, u32[]{:S(2)}, u32[]{:S(2)}) collective-permute-start(bf16[1536,128]{1,0:T(8,128)(2,1)} %get-tuple-element.31), channel_id=1, source_target_pairs={{0,24},{4,28},{8,16},{12,20},{16,8},{20,12},{24,0},{28,4},{1,25},{... | collective-permute-start | bytes 1179656 | tf_op jit(solution)/shard_map/ppermute | solution.py:310
  23.7 0.2 collective-permute-start.10
  23.9 1.5 %collective-permute-done.10.refs_7_ = bf16[400,128]{1,0:T(8,128)(2,1)S(1)} collective-permute-done((bf16[400,128]{1,0:T(8,128)(2,1)S(1)}, bf16[400,128]{1,0:T(8,128)(2,1)S(1)}, u32[]{:S(2)}, u32[]{:S(2)}) %collective-permute-start.10) | collective-permute-done | bytes 102432 | tf_op jit(solution)/shard_map/ppermute | solution.py:303
  25.4 1.3 %collective-permute-start.6 = (bf16[768,128]{1,0:T(8,128)(2,1)}, bf16[768,128]{1,0:T(8,128)(2,1)S(1)}, u32[]{:S(2)}, u32[]{:S(2)}) collective-permute-start(bf16[768,128]{1,0:T(8,128)(2,1)} %get-tuple-element.32), channel_id=1, source_target_pairs={{0,24},{4,28},{8,16},{12,20},{16,8},{20,12},{24,0},{28,4},{1,25},{... | collective-permute-start | bytes 589832 | tf_op jit(solution)/shard_map/ppermute | solution.py:310
  26.7 1.3 %collective-permute-start.4 = (bf16[768,128]{1,0:T(8,128)(2,1)S(1)}, bf16[768,128]{1,0:T(8,128)(2,1)S(1)}, u32[]{:S(2)}, u32[]{:S(2)}) collective-permute-start(bf16[768,128]{1,0:T(8,128)(2,1)S(1)} %slice.15), channel_id=1, source_target_pairs={{0,1},{1,0},{2,3},{3,2},{4,5},{5,4},{6,7},{7,6},{8,9},{9,8},{10,11... | collective-permute-start | bytes 589832 | tf_op jit(solution)/shard_map/ppermute | solution.py:313
  28.1 0.7 %collective-permute-start.3 = (bf16[768,128]{1,0:T(8,128)(2,1)S(1)}, bf16[768,128]{1,0:T(8,128)(2,1)S(1)}, u32[]{:S(2)}, u32[]{:S(2)}) collective-permute-start(bf16[768,128]{1,0:T(8,128)(2,1)S(1)} %slice.14), channel_id=1, source_target_pairs={{0,1},{1,0},{2,3},{3,2},{4,5},{5,4},{6,7},{7,6},{8,9},{9,8},{10,11... | collective-permute-start | bytes 589832 | tf_op jit(solution)/shard_map/ppermute | solution.py:313
  28.8 1.0 %copy-done = bf16[1936,128]{1,0:T(8,128)(2,1)S(1)} copy-done((bf16[1936,128]{1,0:T(8,128)(2,1)S(1)}, bf16[1936,128]{1,0:T(8,128)(2,1)}, u32[]{:S(2)}) %copy-start) | copy-done | bytes 495640
  29.8 9.2 %factor.1.inverse = f32[256,256]{1,0:T(8,128)S(1)} custom-call(bf16[1936,128]{1,0:T(8,128)(2,1)S(1)} %copy-done, bf16[1936,128]{1,0:T(8,128)(2,1)S(1)} %collective-permute-done.7.refs_1_.refs_2_, bf16[1936,128]{1,0:T(8,128)(2,1)S(1)} %collective-permute-done.1.refs_2_.refs_8_.refs_4_, bf16[1936,128]{1,0:T(8,128)(2,1)S(1)} %collective-permute-done.8.refs_3_.refs_10_.refs_5_, ...), custom_call_target="tpu_custom_call" | custom-call | tf_op jit(solution)/shard_map/factor/pallas_call | solution.py:353
  39.0 0.3 collective-permute-done.6.refs_6_
  39.5 0.5 %collective-permute-start.11 = (bf16[768,128]{1,0:T(8,128)(2,1)S(1)}, bf16[768,128]{1,0:T(8,128)(2,1)S(1)}, u32[]{:S(2)}, u32[]{:S(2)}) collective-permute-start(bf16[768,128]{1,0:T(8,128)(2,1)S(1)} %copy-done.4), channel_id=1, source_target_pairs={{0,4},{4,0},{8,12},{12,8},{1,5},{5,1},{9,13},{13,9},{2,6},{6,2},{1... | collective-permute-start | bytes 589832 | tf_op jit(solution)/shard_map/ppermute | solution.py:303
  40.0 0.4 collective-permute-start.13
  40.5 0.2 collective-permute-start.15
  40.7 0.8 %collective-permute-done.11.refs_3_ = bf16[768,128]{1,0:T(8,128)(2,1)S(1)} collective-permute-done((bf16[768,128]{1,0:T(8,128)(2,1)S(1)}, bf16[768,128]{1,0:T(8,128)(2,1)S(1)}, u32[]{:S(2)}, u32[]{:S(2)}) %collective-permute-start.11) | collective-permute-done | bytes 196640 | tf_op jit(solution)/shard_map/ppermute | solution.py:303
  41.4 0.3 collective-permute-done.12.refs_7_
  41.7 0.3 collective-permute-done.13.refs_11_
  42.0 2.9 %product.1 = (f32[256,128]{1,0:T(8,128)S(1)}, f32[2,3200,128]{2,1,0:T(8,128)S(1)}) custom-call(s32[2,72]{1,0:T(2,128)S(1)} %pad_add_fusion.tables, f32[256,256]{1,0:T(8,128)S(1)} %factor.1.inverse, bf16[1936,128]{1,0:T(8,128)(2,1)S(1)} %copy-done, bf16[768,128]{1,0:T(8,128)(2,1)S(1)} %copy-done.4, ...), custom_call_target="tpu_custom_call" | custom-call | flops 3000000000 | tf_op jit(solution)/shard_map/product/pallas_call | solution.py:390
  44.9 2.2 %front.1 = f32[1,2304,128]{2,1,0:T(8,128)} custom-call(s32[2,72]{1,0:T(2,128)S(1)} %pad_add_fusion.tables, s32[1,4,72]{2,1,0:T(4,128)S(1)} %bitcast.2, f32[1,2304]{1,0:T(1,128)S(1)} %copy-done.2, f32[256,128]{1,0:T(8,128)S(1)} %get-tuple-element.40.weight, f32[2,3200,128]{2,1,0:T(8,128)S(1)} %get-tuple-element.41.product, bf16[1936,128]{1,0:T(8,128)(2,1)S(1)} %copy-done.1, ...), custom_call_target="tpu_custom_call" | custom-call | flops 2000000000 | tf_op jit(solution)/shard_map/front/pallas_call | solution.py:403
  (29 shorter events, 0.3 us)
Async XLA Ops:
  3.7 35.7 %copy-start.5 = (s32[2,72]{1,0:T(2,128)S(1)}, s32[2,72]{1,0:T(2,128)}, u32[]{:S(2)}) copy-start(s32[2,72]{1,0:T(2,128)} %get-tuple-element.24) | copy-start | bytes 1732
  3.8 35.7 %copy-start.4 = (bf16[768,128]{1,0:T(8,128)(2,1)S(1)}, bf16[768,128]{1,0:T(8,128)(2,1)}, u32[]{:S(2)}) copy-start(bf16[768,128]{1,0:T(8,128)(2,1)} %get-tuple-element.36.refs_1_) | copy-start | bytes 589828
  3.8 17.0 %collective-permute-start.1 = (bf16[1936,128]{1,0:T(8,128)(2,1)}, bf16[1936,128]{1,0:T(8,128)(2,1)S(1)}, u32[]{:S(2)}, u32[]{:S(2)}) collective-permute-start(bf16[1936,128]{1,0:T(8,128)(2,1)} %get-tuple-element.33.refs_0_), channel_id=1, source_target_pairs={{0,8},{4,12},{8,0},{12,4},{1,9},{5,13},{9,1},{13,5},{2,10},{6,14},... | collective-permute-start | bytes 1486856 | tf_op jit(solution)/shard_map/ppermute | solution.py:300
  6.8 15.2 %collective-permute-start.2 = (bf16[1936,128]{1,0:T(8,128)(2,1)}, bf16[1936,128]{1,0:T(8,128)(2,1)S(1)}, u32[]{:S(2)}, u32[]{:S(2)}) collective-permute-start(bf16[1936,128]{1,0:T(8,128)(2,1)} %get-tuple-element.27), channel_id=1, source_target_pairs={{0,16},{4,20},{8,24},{12,28},{16,0},{20,4},{24,8},{28,12},{1,17},{... | collective-permute-start | bytes 1486856 | tf_op jit(solution)/shard_map/ppermute | solution.py:310
  7.2 13.5 %collective-permute-start = (bf16[400,128]{1,0:T(8,128)(2,1)}, bf16[400,128]{1,0:T(8,128)(2,1)S(1)}, u32[]{:S(2)}, u32[]{:S(2)}) collective-permute-start(bf16[400,128]{1,0:T(8,128)(2,1)} %get-tuple-element.25), channel_id=1, source_target_pairs={{0,24},{4,28},{8,16},{12,20},{16,8},{20,12},{24,0},{28,4},{1,25},{... | collective-permute-start | bytes 307208 | tf_op jit(solution)/shard_map/ppermute | solution.py:310
  22.0 4.8 %collective-permute-start.9 = (bf16[1936,128]{1,0:T(8,128)(2,1)S(1)}, bf16[1936,128]{1,0:T(8,128)(2,1)S(1)}, u32[]{:S(2)}, u32[]{:S(2)}) collective-permute-start(bf16[1936,128]{1,0:T(8,128)(2,1)S(1)} %collective-permute-done.2.refs_4_.refs_2_), channel_id=1, source_target_pairs={{0,4},{4,0},{8,12},{12,8},{1,5},{5,1},{9,13},{13,9},{2,6},{6,2},{1... | collective-permute-start | bytes 1486856 | tf_op jit(solution)/shard_map/ppermute | solution.py:303
  22.0 6.1 %collective-permute-start.8 = (bf16[1936,128]{1,0:T(8,128)(2,1)S(1)}, bf16[1936,128]{1,0:T(8,128)(2,1)S(1)}, u32[]{:S(2)}, u32[]{:S(2)}) collective-permute-start(bf16[1936,128]{1,0:T(8,128)(2,1)S(1)} %collective-permute-done.1.refs_2_.refs_8_.refs_4_), channel_id=1, source_target_pairs={{0,4},{4,0},{8,12},{12,8},{1,5},{5,1},{9,13},{13,9},{2,6},{6,2},{1... | collective-permute-start | bytes 1486856 | tf_op jit(solution)/shard_map/ppermute | solution.py:303
  22.5 6.3 %collective-permute-start.7 = (bf16[1936,128]{1,0:T(8,128)(2,1)}, bf16[1936,128]{1,0:T(8,128)(2,1)S(1)}, u32[]{:S(2)}, u32[]{:S(2)}) collective-permute-start(bf16[1936,128]{1,0:T(8,128)(2,1)} %get-tuple-element.33.refs_0_), channel_id=1, source_target_pairs={{0,4},{4,0},{8,12},{12,8},{1,5},{5,1},{9,13},{13,9},{2,6},{6,2},{1... | collective-permute-start | bytes 1486856 | tf_op jit(solution)/shard_map/ppermute | solution.py:303
  22.5 16.9 %collective-permute-start.5 = (bf16[1536,128]{1,0:T(8,128)(2,1)}, bf16[1536,128]{1,0:T(8,128)(2,1)S(1)}, u32[]{:S(2)}, u32[]{:S(2)}) collective-permute-start(bf16[1536,128]{1,0:T(8,128)(2,1)} %get-tuple-element.31), channel_id=1, source_target_pairs={{0,24},{4,28},{8,16},{12,20},{16,8},{20,12},{24,0},{28,4},{1,25},{... | collective-permute-start | bytes 1179656 | tf_op jit(solution)/shard_map/ppermute | solution.py:310
  23.7 1.7 %collective-permute-start.10 = (bf16[400,128]{1,0:T(8,128)(2,1)S(1)}, bf16[400,128]{1,0:T(8,128)(2,1)S(1)}, u32[]{:S(2)}, u32[]{:S(2)}) collective-permute-start(bf16[400,128]{1,0:T(8,128)(2,1)S(1)} %collective-permute-done.refs_6_), channel_id=1, source_target_pairs={{0,4},{4,0},{8,12},{12,8},{1,5},{5,1},{9,13},{13,9},{2,6},{6,2},{1... | collective-permute-start | bytes 307208 | tf_op jit(solution)/shard_map/ppermute | solution.py:303
  25.4 13.9 %collective-permute-start.6 = (bf16[768,128]{1,0:T(8,128)(2,1)}, bf16[768,128]{1,0:T(8,128)(2,1)S(1)}, u32[]{:S(2)}, u32[]{:S(2)}) collective-permute-start(bf16[768,128]{1,0:T(8,128)(2,1)} %get-tuple-element.32), channel_id=1, source_target_pairs={{0,24},{4,28},{8,16},{12,20},{16,8},{20,12},{24,0},{28,4},{1,25},{... | collective-permute-start | bytes 589832 | tf_op jit(solution)/shard_map/ppermute | solution.py:310
  26.7 12.6 %collective-permute-start.4 = (bf16[768,128]{1,0:T(8,128)(2,1)S(1)}, bf16[768,128]{1,0:T(8,128)(2,1)S(1)}, u32[]{:S(2)}, u32[]{:S(2)}) collective-permute-start(bf16[768,128]{1,0:T(8,128)(2,1)S(1)} %slice.15), channel_id=1, source_target_pairs={{0,1},{1,0},{2,3},{3,2},{4,5},{5,4},{6,7},{7,6},{8,9},{9,8},{10,11... | collective-permute-start | bytes 589832 | tf_op jit(solution)/shard_map/ppermute | solution.py:313
  28.1 11.3 %collective-permute-start.3 = (bf16[768,128]{1,0:T(8,128)(2,1)S(1)}, bf16[768,128]{1,0:T(8,128)(2,1)S(1)}, u32[]{:S(2)}, u32[]{:S(2)}) collective-permute-start(bf16[768,128]{1,0:T(8,128)(2,1)S(1)} %slice.14), channel_id=1, source_target_pairs={{0,1},{1,0},{2,3},{3,2},{4,5},{5,4},{6,7},{7,6},{8,9},{9,8},{10,11... | collective-permute-start | bytes 589832 | tf_op jit(solution)/shard_map/ppermute | solution.py:313
  28.7 1.0 %copy-start = (bf16[1936,128]{1,0:T(8,128)(2,1)S(1)}, bf16[1936,128]{1,0:T(8,128)(2,1)}, u32[]{:S(2)}) copy-start(bf16[1936,128]{1,0:T(8,128)(2,1)} %get-tuple-element.33.refs_0_) | copy-start | bytes 1486852
  39.3 2.6 %collective-permute-start.14 = (bf16[1536,128]{1,0:T(8,128)(2,1)S(1)}, bf16[1536,128]{1,0:T(8,128)(2,1)S(1)}, u32[]{:S(2)}, u32[]{:S(2)}) collective-permute-start(bf16[1536,128]{1,0:T(8,128)(2,1)S(1)} %collective-permute-done.5.refs_12_), channel_id=1, source_target_pairs={{0,4},{4,0},{8,12},{12,8},{1,5},{5,1},{9,13},{13,9},{2,6},{6,2},{1... | collective-permute-start | bytes 1179656 | tf_op jit(solution)/shard_map/ppermute | solution.py:303
  39.5 2.0 %collective-permute-start.11 = (bf16[768,128]{1,0:T(8,128)(2,1)S(1)}, bf16[768,128]{1,0:T(8,128)(2,1)S(1)}, u32[]{:S(2)}, u32[]{:S(2)}) collective-permute-start(bf16[768,128]{1,0:T(8,128)(2,1)S(1)} %copy-done.4), channel_id=1, source_target_pairs={{0,4},{4,0},{8,12},{12,8},{1,5},{5,1},{9,13},{13,9},{2,6},{6,2},{1... | collective-permute-start | bytes 589832 | tf_op jit(solution)/shard_map/ppermute | solution.py:303
  39.9 1.8 %collective-permute-start.12 = (bf16[768,128]{1,0:T(8,128)(2,1)S(1)}, bf16[768,128]{1,0:T(8,128)(2,1)S(1)}, u32[]{:S(2)}, u32[]{:S(2)}) collective-permute-start(bf16[768,128]{1,0:T(8,128)(2,1)S(1)} %collective-permute-done.4.refs_5_), channel_id=1, source_target_pairs={{0,4},{4,0},{8,12},{12,8},{1,5},{5,1},{9,13},{13,9},{2,6},{6,2},{1... | collective-permute-start | bytes 589832 | tf_op jit(solution)/shard_map/ppermute | solution.py:303
  40.0 1.9 %collective-permute-start.13 = (bf16[768,128]{1,0:T(8,128)(2,1)S(1)}, bf16[768,128]{1,0:T(8,128)(2,1)S(1)}, u32[]{:S(2)}, u32[]{:S(2)}) collective-permute-start(bf16[768,128]{1,0:T(8,128)(2,1)S(1)} %collective-permute-done.3.refs_9_), channel_id=1, source_target_pairs={{0,4},{4,0},{8,12},{12,8},{1,5},{5,1},{9,13},{13,9},{2,6},{6,2},{1... | collective-permute-start | bytes 589832 | tf_op jit(solution)/shard_map/ppermute | solution.py:303
  40.5 4.4 %copy-start.1 = (bf16[1936,128]{1,0:T(8,128)(2,1)S(1)}, bf16[1936,128]{1,0:T(8,128)(2,1)}, u32[]{:S(2)}) copy-start(bf16[1936,128]{1,0:T(8,128)(2,1)} %get-tuple-element.33.refs_0_) | copy-start | bytes 1486852
  40.5 4.4 %copy-start.2 = (f32[1,2304]{1,0:T(1,128)S(1)}, f32[1,2304]{1,0:T(1,128)}, u32[]{:S(2)}) copy-start(f32[1,2304]{1,0:T(1,128)} %diag.3) | copy-start | bytes 27652
  40.5 4.4 %copy-start.3 = (s32[1,72,4]{1,2,0:T(4,128)S(1)}, s32[1,72,4]{1,2,0:T(4,128)}, u32[]{:S(2)}) copy-start(s32[1,72,4]{1,2,0:T(4,128)} %param.6) | copy-start | bytes 3460
  40.5 4.4 %collective-permute-start.15 = (bf16[768,128]{1,0:T(8,128)(2,1)S(1)}, bf16[768,128]{1,0:T(8,128)(2,1)S(1)}, u32[]{:S(2)}, u32[]{:S(2)}) collective-permute-start(bf16[768,128]{1,0:T(8,128)(2,1)S(1)} %collective-permute-done.6.refs_6_), channel_id=1, source_target_pairs={{0,4},{4,0},{8,12},{12,8},{1,5},{5,1},{9,13},{13,9},{2,6},{6,2},{1... | collective-permute-start | bytes 589832 | tf_op jit(solution)/shard_map/ppermute | solution.py:303

commit v3 on v2

--- a/solution.py
+++ b/solution.py
@@ -20,17 +20,48 @@
     return pltpu.CompilerParams(vmem_limit_bytes=mib * MIB)
 
 
-def select_kernel(maps, diag, kids, tables, *refs):
-    own_side, own_rest, far_window, far_side, far_pair, far_column, sems = refs
-    lines = far_window.shape[0]
+def copy_columns(kids, sems, copies, found, child, p, start, size, target, here=None):
+    none = kids.shape[3] // BLOCK
+    col = found[child][p]
+    here = (col < none) if here is None else here & (col < none)
+    start = pl.multiple_of(jnp.where(here, start, 0), 16)
+    col = pl.multiple_of(jnp.where(here, col, 0) * BLOCK, BLOCK)
+    source = kids.at[0, child, pl.ds(start, size), pl.ds(col, BLOCK)]
+    copy = pltpu.make_async_copy(source, target, sems.at[len(copies)])
+    copies.append((here, copy))
+
+    @pl.when(here)
+    def _():
+        copy.start()
+
+    @pl.when(jnp.logical_not(here))
+    def _():
+        target[...] = jnp.zeros_like(target)
+
+
+def finish(copies):
+    for here, copy in copies:
+
+        @pl.when(here)
+        def _():
+            copy.wait()
+
+
+def select_kernel(maps_hbm, diag_hbm, kids, tables, own_side, far_window, far_side, maps, diag, sems):
+    first = pltpu.make_async_copy(maps_hbm, maps, sems.at[sems.shape[0] - 2])
+    second = pltpu.make_async_copy(diag_hbm, diag, sems.at[sems.shape[0] - 1])
+    first.start()
+    second.start()
     me, col_index = lax.axis_index("row"), lax.axis_index("col")
     rows = kids.shape[2]
     local = rows // BLOCK
     none = kids.shape[3] // BLOCK
+    lines = far_window.shape[0]
     places = maps.shape[3]
     child_id = lax.broadcasted_iota(jnp.int32, (none, places), 0)
     place_id = lax.broadcasted_iota(jnp.int32, (1, places), 1)
     found = []
+    first.wait()
     for child in range(2):
         ones = maps[0, child].astype(F32)
         line = jnp.sum(ones * (child_id - none).astype(F32), axis=0, keepdims=True) + none
@@ -46,48 +77,22 @@
             far_side[3 * BLOCK : lines, 0:places] = line
             far_window[3 * BLOCK :, 0:places] = line
     copies = []
-
-    def add(here, source, target):
-        copy = pltpu.make_async_copy(source, target, sems.at[len(copies)])
-        copies.append((here, copy))
-
-        @pl.when(here)
-        def _():
-            copy.start()
-
-        @pl.when(jnp.logical_not(here))
-        def _():
-            target[...] = jnp.zeros_like(target)
-
-    def columns(start, size, child, col):
-        return kids.at[0, child, pl.ds(start, size), pl.ds(pl.multiple_of(col * BLOCK, BLOCK), BLOCK)]
-
     for child, out in ((1, far_window), (0, own_side), (1, far_side)):
         for at, (w, p) in enumerate(((0, 0), (1, 0), (1, 1))):
-            row, col = found[child][w], found[child][p]
+            row = found[child][w]
             offset = row - me * local
-            here = (row < none) & (col < none) & (offset >= 0) & (offset < local)
-            start = pl.multiple_of(offset * BLOCK, BLOCK)
-            add(here, columns(start, BLOCK, child, col), out.at[pl.ds(at * BLOCK, BLOCK)])
+            here = (row < none) & (offset >= 0) & (offset < local)
+            target = out.at[pl.ds(at * BLOCK, BLOCK)]
+            copy_columns(kids, sems, copies, found, child, p, offset * BLOCK, BLOCK, target, here)
     half = rows // 2
-    here, other = (
-        pl.multiple_of(side * half, half) for side in (col_index % 2, 1 - col_index % 2)
-    )
-    side = [(0, here, half), (1, here, half)]
-    rest = [(0, other, half), (1, other, half)]
-    column = [(2, 0, rows)]
-    for child, out, at, parts in (
-        (0, own_side, lines, side + column),
-        (1, far_side, lines, side + column),
-        (1, far_pair, 0, side + rest),
-        (1, far_column, 0, column),
-        (0, own_rest, 0, rest),
-    ):
-        for p, start, size in parts:
-            col = found[child][p]
-            add(col < none, columns(start, size, child, col), out.at[pl.ds(at, size)])
-            at += size
-
+    for child, out in ((0, own_side), (1, far_side)):
+        for p in range(NPANEL):
+            target = out.at[pl.ds(lines + p * half, half)]
+            copy_columns(kids, sems, copies, found, child, p, col_index % 2 * half, half, target)
+        target = out.at[pl.ds(lines + rows, rows)]
+        copy_columns(kids, sems, copies, found, child, NPANEL, 0, rows, target)
+
+    second.wait()
     line = lax.broadcasted_iota(jnp.int32, (16, BLOCK), 0)
     pieces = jnp.zeros((16, BLOCK), F32)
     for p in range(NPANEL):
@@ -97,11 +102,30 @@
             pieces = jnp.where(line == 3 * p + at, part, pieces)
             rest = rest - part
     own_side[3 * BLOCK : lines, :] = jnp.where(me == 0, pieces, 0.0).astype(BF16)
-    for here, copy in copies:
-
-        @pl.when(here)
-        def _():
-            copy.wait()
+    finish(copies)
+
+
+def remain_kernel(tables, kids, far_all, own_rest, sems):
+    col_index = lax.axis_index("col")
+    rows = kids.shape[2]
+    half = rows // 2
+    here, other = col_index % 2 * half, (1 - col_index % 2) * half
+    found = [[tables[child, w] for w in (0, 1, col_index)] for child in range(2)]
+    copies = []
+    for child, out, parts in (
+        (
+            1,
+            far_all,
+            [(0, here, half), (1, here, half), (0, other, half), (1, other, half), (2, 0, rows)],
+        ),
+        (0, own_rest, [(0, other, half), (1, other, half)]),
+    ):
+        at = 0
+        for p, start, size in parts:
+            target = out.at[pl.ds(at, size)]
+            copy_columns(kids, sems, copies, found, child, p, start, size, target)
+            at += size
+    finish(copies)
 
 
 def cost(microseconds):
@@ -159,8 +183,14 @@
     )
 
 
-def factor_kernel(n_own, *refs):
-    own, far, out = refs[:n_own], refs[n_own:-1], refs[-1]
+def invert(block):
+    tiles = [block[8 * t : 8 * t + 8, :] for t in range(BLOCK // 8)]
+    return jnp.concatenate(inverse_factor(tiles), axis=0)
+
+
+def first_kernel(n_own, *refs):
+    own, far = refs[:n_own], refs[n_own:-3]
+    inverse, below, rest = refs[-3:]
 
     def total(at):
         value = None
@@ -182,33 +212,32 @@
         line = line + pieces[3 * p + 2 : 3 * p + 3]
         return jnp.where(eye, jnp.broadcast_to(line, (BLOCK, BLOCK)), 0.0)
 
-    def invert(block):
-        return jnp.concatenate(
-            inverse_factor([block[8 * t : 8 * t + 8, :] for t in range(BLOCK // 8)]), axis=0
-        )
-
-    first = invert(total(0) + diagonal(0))
-    cross = dot(total(1), first, 1, 1)
-    second = invert(total(2) + diagonal(1) - dot(cross, cross, 1, 1))
-    out[0:BLOCK, 0:BLOCK] = first
+    inverse[...] = invert(total(0) + diagonal(0))
+    below[...] = dot(total(1), inverse[...], 1, 1)
+    rest[...] = total(2) + diagonal(1) - dot(below[...], below[...], 1, 1)
+
+
+def second_kernel(first, below, rest, out):
+    inverse = invert(rest[...])
+    out[0:BLOCK, 0:BLOCK] = first[...]
     out[0:BLOCK, BLOCK:] = jnp.zeros((BLOCK, BLOCK), F32)
-    out[BLOCK:, 0:BLOCK] = -dot(second, dot(cross, first))
-    out[BLOCK:, BLOCK:] = second
-
-
-def product_kernel(layout, n_row, lines, tables, inverse, *refs):
-    sources = list(refs[:-2])
-    weight, product = refs[-2:]
+    out[BLOCK:, 0:BLOCK] = -dot(inverse, dot(below[...], first[...]))
+    out[BLOCK:, BLOCK:] = inverse
+
+
+def front_kernel(layout, n_row, row_blocks, tables, mask, diag, inverse, *refs):
+    out, weight, product, buffer = refs[-4:]
     me, col_index = lax.axis_index("row"), lax.axis_index("col")
+    is_panel = col_index < NPANEL
     rows = (product.shape[1] - BLOCK) // n_row
     half = rows // 2
     wide = NPANEL * PW
     parts = []
-    for child, owner, whole in layout:
-        first = sources.pop(0)
-        second = first if whole else sources.pop(0)
-        parts.append((child, owner(me), first, 0 if whole else lines, col_index % 2))
-        parts.append((child, owner(me), second, rows if whole else 0, 1 - col_index % 2))
+    for child, owner, (first, start), (second, at), column in layout:
+        parts.append((child, owner(me), refs[first], start, col_index % 2))
+        parts.append((child, owner(me), refs[second], at, 1 - col_index % 2))
+        start = pl.multiple_of(owner(me) * rows, rows)
+        buffer[child, pl.ds(start, rows), :] = refs[first][column : column + rows, :]
 
     mirrored = jnp.zeros((BLOCK, wide), F32)
     for child, owner, ref, at, side in parts:
@@ -227,31 +256,22 @@
     row_id = lax.broadcasted_iota(jnp.int32, (wide, PW), 0)
     col_id = lax.broadcasted_iota(jnp.int32, (wide, PW), 1)
     picked = -(row_id == col_id + col_index * PW).astype(F32)
-    solved = jnp.where(col_index < NPANEL, picked, dot(lower, mirrored, 1, 1))
+    solved = jnp.where(is_panel, picked, dot(lower, mirrored, 1, 1))
     weight[...] = dot(lower, solved, 0, 0)
     high = weight[...].astype(BF16)
     low = (weight[...] - high.astype(F32)).astype(BF16)
     both = jnp.concatenate([high, low], axis=1)
     for child, owner, ref, at, side in parts:
-        left = jnp.concatenate([ref[at + p * half : at + (p + 1) * half, :] for p in range(NPANEL)], axis=1)
+        left = jnp.concatenate(
+            [ref[at + p * half : at + (p + 1) * half, :] for p in range(NPANEL)], axis=1
+        )
         value = jnp.dot(left, both, preferred_element_type=F32)
         start = pl.multiple_of(owner * rows + side * half, half)
         product[child, pl.ds(start, half), :] = value[:, :PW] + value[:, PW:]
     for child in range(2):
         product[child, n_row * rows :, :] = jnp.zeros((BLOCK, PW), F32)
-
-
-def front_kernel(layout, n_row, row_blocks, tables, mask, diag, weight, product, *refs):
-    sources = refs[: len(layout)]
-    out, buffer = refs[len(layout) :]
-    me, col_index = lax.axis_index("row"), lax.axis_index("col")
-    rows = (product.shape[1] - BLOCK) // n_row
-    is_panel = col_index < NPANEL
-    for (child, owner, at), ref in zip(layout, sources):
-        start = pl.multiple_of(owner(me) * rows, rows)
-        buffer[child, pl.ds(start, rows), :] = ref[at : at + rows, :]
-    for child in range(2):
         buffer[child, n_row * rows :, :] = jnp.zeros((BLOCK, PW), BF16)
+
     for p in range(row_blocks):
         at = me * row_blocks + p
         first, second = (
@@ -315,52 +335,77 @@
     lines = 3 * BLOCK + 16
     maps = jnp.swapaxes(maps, 2, 3)
     mask = jnp.swapaxes(mask, 1, 2)
-    side = lines + 2 * rows_here
-    shapes = [side, rows_here, lines, side, 2 * rows_here, rows_here]
-    shapes = [jax.ShapeDtypeStruct((size, BLOCK), BF16) for size in shapes]
-    shapes = [jax.ShapeDtypeStruct((2, maps.shape[3]), jnp.int32)] + shapes
-    tables, own_side, own_rest, far_window, far_side, far_pair, far_column = pl.pallas_call(
-        select_kernel,
-        out_shape=shapes,
-        in_specs=[vmem, vmem, pl.BlockSpec(memory_space=pltpu.HBM)],
-        out_specs=[vmem] * len(shapes),
-        scratch_shapes=[pltpu.SemaphoreType.DMA((22,))],
-        compiler_params=params(55),
-        cost_estimate=cost(2),
-        name="select",
-    )(maps, diag, kids)
+    def shapes(*sizes):
+        return [jax.ShapeDtypeStruct((size, BLOCK), BF16) for size in sizes]
 
     def both(x):
         return x, partner(x)
+
+    hbm = pl.BlockSpec(memory_space=pltpu.HBM)
+    kids = pltpu.with_memory_space_constraint(kids, pltpu.HBM)
+    diag_hbm = pltpu.with_memory_space_constraint(diag, pltpu.HBM)
+    tables, own_side, far_window, far_side = pl.pallas_call(
+        select_kernel,
+        out_shape=[jax.ShapeDtypeStruct((2, maps.shape[3]), jnp.int32)]
+        + shapes(lines + 2 * rows_here, lines, lines + 2 * rows_here),
+        in_specs=[hbm] * 3,
+        out_specs=[vmem] * 4,
+        scratch_shapes=[
+            pltpu.VMEM(maps.shape, jnp.int32),
+            pltpu.VMEM(diag.shape, F32),
+            pltpu.SemaphoreType.DMA((17,)),
+        ],
+        compiler_params=params(),
+        cost_estimate=cost(0),
+        name="select",
+    )(pltpu.with_memory_space_constraint(maps, pltpu.HBM), diag_hbm, kids)
+    far_all, own_rest = pl.pallas_call(
+        remain_kernel,
+        out_shape=shapes(3 * rows_here, rows_here),
+        in_specs=[smem, hbm],
+        out_specs=[vmem] * 2,
+        scratch_shapes=[pltpu.SemaphoreType.DMA((7,))],
+        compiler_params=params(),
+        cost_estimate=cost(0),
+        name="remain",
+    )(tables, kids)
 
     far_windows = [parent(far_window, s) for s in range(1, chips)]
     own_sides = [along(own_side, s) for s in range(1, chips)]
     far_near = parent(far_side, 0)
-    far_windows, own_sides, far_near, own_side = lax.optimization_barrier(
-        (far_windows, own_sides, far_near, own_side)
-    )
+    arrived = (far_windows, own_sides, far_near, own_side, far_all)
+    arrived = lax.optimization_barrier(arrived)
+    far_windows, own_sides, far_near, own_side, far_all = arrived
     far_windows = [both(x) for x in far_windows]
     own_sides = [both(own_side)] + [both(x) for x in own_sides]
     far_near = both(far_near)
-    far_pairs = [parent(far_pair, s) for s in range(1, chips)]
-    far_columns = [parent(far_column, s) for s in range(1, chips)]
-    middle = slice(lines, lines + rows_here)
-    own_others = [neighbour(x[middle]) for x, _ in own_sides[1:]]
-    far_other = neighbour(far_near[0][middle])
+    far_alls = [parent(far_all, s) for s in range(1, chips)]
     own_parts = [x for pair in own_sides for x in pair]
     far_parts = list(far_near) + [x for pair in far_windows for x in pair]
+    middle = slice(lines, lines + rows_here)
+    halves = [x[middle] for x, _ in own_sides[1:]] + [far_near[0][middle]]
+    others = neighbour(jnp.concatenate(halves, axis=0))
     far_table = far_near[0][3 * BLOCK, : tables.shape[1]].astype(jnp.int32)
+    square = jax.ShapeDtypeStruct((BLOCK, BLOCK), F32)
+    first = pl.pallas_call(
+        functools.partial(first_kernel, len(own_parts)),
+        out_shape=[square] * 3,
+        compiler_params=params(),
+        cost_estimate=cost(0),
+        name="first_factor",
+    )(*own_parts, *far_parts)
     inverse = pl.pallas_call(
-        functools.partial(factor_kernel, len(own_parts)),
+        second_kernel,
         out_shape=jax.ShapeDtypeStruct((NPANEL * PW, NPANEL * PW), F32),
         compiler_params=params(),
         cost_estimate=cost(0),
-        name="factor",
-    )(*own_parts, *far_parts)
-
-    remote = (own_rest, own_others, far_other, far_pairs, far_columns)
+        name="second_factor",
+    )(*first)
+
+    remote = (own_rest, others, far_alls)
     remote, inverse = lax.optimization_barrier((remote, inverse))
-    own_rest, own_others, far_other, far_pairs, far_columns = remote
+    own_rest, others, far_alls = remote
+    own_rest, others = both(own_rest), both(others)
 
     def owner(side, s):
         def position(me):
@@ -369,47 +414,44 @@
 
         return position
 
-    pairs, columns, arrays, column_arrays = [], [], [], []
-
-    def add(child, s, first, second, column, at):
+    layout, arrays = [], list(others)
+
+    def add(child, s, first, second):
         for core in range(2):
-            pairs.append((child, owner(core, s), second is None))
-            arrays.extend([first[core]] if second is None else [first[core], second[core]])
-            columns.append((child, owner(core, s), at))
-            column_arrays.append(column[core])
-
-    at = lines + rows_here
-    add(0, 0, own_sides[0], both(own_rest), own_sides[0], at)
-    add(1, 0, far_near, both(far_other), far_near, at)
+            if isinstance(second, int):
+                rest = (core, second * rows_here)
+            else:
+                rest = (len(arrays) + 1, 0) if second else (len(arrays), rows_here)
+            start = lines if second is not None else 0
+            column = start + rows_here if second is not None else 2 * rows_here
+            layout.append((child, owner(core, s), (len(arrays), start), rest, column))
+            arrays.append(first[core])
+            if isinstance(second, tuple):
+                arrays.append(second[core])
+
+    far_alls = [both(x) for x in far_alls]
+    add(0, 0, own_sides[0], own_rest)
+    add(1, 0, far_near, chips - 1)
     for s in range(1, chips):
-        add(0, s, own_sides[s], both(own_others[s - 1]), own_sides[s], at)
-        add(1, s, both(far_pairs[s - 1]), None, both(far_columns[s - 1]), 0)
+        add(0, s, own_sides[s], s - 1)
+        add(1, s, far_alls[s - 1], None)
 
     tables = jnp.stack([tables[0], far_table])
     height = n_row * rows_here + BLOCK
-    weight, product = pl.pallas_call(
-        functools.partial(product_kernel, pairs, n_row, lines),
-        out_shape=[
-            jax.ShapeDtypeStruct((NPANEL * PW, PW), F32),
-            jax.ShapeDtypeStruct((2, height, PW), F32),
+    return pl.pallas_call(
+        functools.partial(front_kernel, layout, n_row, row_blocks),
+        out_shape=jax.ShapeDtypeStruct((1, rows_dev, PW), F32),
+        in_specs=[smem, smem] + [vmem] * (2 + len(arrays)),
+        out_specs=vmem,
+        scratch_shapes=[
+            pltpu.VMEM((NPANEL * PW, PW), F32),
+            pltpu.VMEM((2, height, PW), F32),
+            pltpu.VMEM((2, height, PW), BF16),
         ],
-        in_specs=[smem] + [vmem] * (1 + len(arrays)),
-        out_specs=[vmem, vmem],
         compiler_params=params(),
-        cost_estimate=cost(3),
-        name="product",
-    )(tables, inverse, *arrays)
-
-    return pl.pallas_call(
-        functools.partial(front_kernel, columns, n_row, row_blocks),
-        out_shape=jax.ShapeDtypeStruct((1, rows_dev, PW), F32),
-        in_specs=[smem, smem] + [vmem] * (3 + len(column_arrays)),
-        out_specs=vmem,
-        scratch_shapes=[pltpu.VMEM((2, height, PW), BF16)],
-        compiler_params=params(),
-        cost_estimate=cost(2),
+        cost_estimate=cost(0),
         name="front",
-    )(tables, mask, diag, weight, product, *column_arrays)
+    )(tables, mask, diag, inverse, *arrays)
 
 
 def solution(mesh):

time: 47.4 us -> 45 us (0.949)
  starting transfers between devices: 11 us -> 9.58 us
  local copies, waits for them, and re-layouts: 1.09 us -> 0.04 us
    ppermute x1, starting transfers between devices: 3 us -> 1.49 us  [along(): lax.ppermute(x, 'row', [(i, (i + 2 * by) % n_row) for i in range(n_row)])]
    unnamed x12 -> x4, local copies, waits for them, and re-layouts: 1.06 us -> 0.01 us
    ppermute x4 -> x3, waiting for transfers between devices: 14 us -> 14.7 us  [parent(): return lax.ppermute(x, ('front', 'row'), pairs)]
    ppermute x4 -> x3, starting transfers between devices: 4.11 us -> 4.8 us  [parent(): return lax.ppermute(x, ('front', 'row'), pairs)]
    ppermute x9 -> x7, waiting for transfers between devices: 2.8 us -> 2.33 us  [partner(): return lax.ppermute(x, 'row', [(i, i ^ 1) for i in range(n_row)])]
    ppermute x2 -> x1, starting transfers between devices: 2.03 us -> 1.64 us  [neighbour(): return lax.ppermute(x, 'col', [(i, i ^ 1) for i in range(n_col)])]
    ppermute x9 -> x7, starting transfers between devices: 1.89 us -> 1.65 us  [partner(): return lax.ppermute(x, 'row', [(i, i ^ 1) for i in range(n_row)])]
    pallas_call x4 -> x5, Pallas kernels: 18.1 us -> 17.8 us  [the longest x1 5.12 us: body(): pl.pallas_call(functools.partial(first_kernel, len(own_parts)), out_shape...]
  transfers between devices with their start and end apart: 16 -> 12, of which waited for: 7 -> 3; matrix products, arithmetic and copies ran while one was open for 0% -> 0% of each run, Pallas kernels for 26% -> 25%
where the time goes in v3:
time: 45 us; the launch traced here: 44.7 us
  Pallas kernels  17.8 us (40%)
  waiting for transfers between devices  17.1 us (38%)
  starting transfers between devices  9.58 us (21%)
    ppermute x3, waiting for transfers between devices, parent(): return lax.ppermute(x, ('front', 'row'), pairs)  14.7 us
    pallas_call x1, Pallas kernels, body(): pl.pallas_call(functools.partial(first_kernel, len(own_parts)), out_shape...  5.12 us
    ppermute x3, starting transfers between devices, parent(): return lax.ppermute(x, ('front', 'row'), pairs)  4.8 us
    pallas_call x1, Pallas kernels, body(): pl.pallas_call(functools.partial(front_kernel, layout, n_row, row_blocks)...  4.5 us
    pallas_call x1, Pallas kernels, body(): pl.pallas_call(second_kernel, out_shape=jax.ShapeDtypeStruct((NPANEL * PW...  4.37 us
    ppermute x7, waiting for transfers between devices, partner(): return lax.ppermute(x, 'row', [(i, i ^ 1) for i in range(n_row)])  2.33 us
    pallas_call x1, Pallas kernels, body(): pl.pallas_call(select_kernel, out_shape=[jax.ShapeDtypeStruct((2, maps.sh...  2.18 us
    ppermute x7, starting transfers between devices, partner(): return lax.ppermute(x, 'row', [(i, i ^ 1) for i in range(n_row)])  1.65 us
  transfers between devices with their start and end apart: 12, of which 3 were waited for; matrix products, arithmetic and copies ran while one was open for 0% of the time, Pallas kernels for 25%

profile of v3, /device:TPU:0, one launch (start us, length us, event | category | flops | bytes accessed | tf_op | source)
XLA Modules:
  0.0 44.7 jit_solution(8706036388968923698)
XLA Ops:
  0.0 2.2 %select.1 = (s32[2,72]{1,0:T(2,128)S(1)}, bf16[1936,128]{1,0:T(8,128)(2,1)S(1)}, bf16[400,128]{1,0:T(8,128)(2,1)S(1)}, bf16[1936,128]{1,0:T(8,128)(2,1)S(1)}) custom-call(s32[1,2,24,72]{3,2,1,0:T(8,128)} %bitcast.3, f32[1,2304]{1,0:T(1,128)} %diag.1, bf16[1,2,768,3072]{3,2,1,0:T(8,128)(2,1)} %kids.3), custom_call_target="tpu_custom_call" | custom-call | tf_op jit(solution)/shard_map/select/pallas_call | solution.py:347
  2.2 0.0 copy-start
  2.2 0.0 copy-start.1
  2.2 2.2 %collective-permute-start.2 = (bf16[1936,128]{1,0:T(8,128)(2,1)S(1)}, bf16[1936,128]{1,0:T(8,128)(2,1)S(1)}, u32[]{:S(2)}, u32[]{:S(2)}) collective-permute-start(bf16[1936,128]{1,0:T(8,128)(2,1)S(1)} %get-tuple-element.26), channel_id=1, source_target_pairs={{0,16},{4,20},{8,24},{12,28},{16,0},{20,4},{24,8},{28,12},{1,17},{... | collective-permute-start | bytes 1486856 | tf_op jit(solution)/shard_map/ppermute | solution.py:330
  4.4 1.5 %collective-permute-start.1 = (bf16[1936,128]{1,0:T(8,128)(2,1)S(1)}, bf16[1936,128]{1,0:T(8,128)(2,1)S(1)}, u32[]{:S(2)}, u32[]{:S(2)}) collective-permute-start(bf16[1936,128]{1,0:T(8,128)(2,1)S(1)} %get-tuple-element.32.refs_0_.refs_2_), channel_id=1, source_target_pairs={{0,8},{4,12},{8,0},{12,4},{1,9},{5,13},{9,1},{13,5},{2,10},{6,14},... | collective-permute-start | bytes 1486856 | tf_op jit(solution)/shard_map/ppermute | solution.py:320
  5.9 0.8 %collective-permute-start = (bf16[400,128]{1,0:T(8,128)(2,1)S(1)}, bf16[400,128]{1,0:T(8,128)(2,1)S(1)}, u32[]{:S(2)}, u32[]{:S(2)}) collective-permute-start(bf16[400,128]{1,0:T(8,128)(2,1)S(1)} %get-tuple-element.24), channel_id=1, source_target_pairs={{0,24},{4,28},{8,16},{12,20},{16,8},{20,12},{24,0},{28,4},{1,25},{... | collective-permute-start | bytes 307208 | tf_op jit(solution)/shard_map/ppermute | solution.py:330
  6.7 1.6 %remain.1 = (bf16[2304,128]{1,0:T(8,128)(2,1)S(1)}, bf16[768,128]{1,0:T(8,128)(2,1)S(1)}) custom-call(s32[2,72]{1,0:T(2,128)S(1)} %get-tuple-element.23.tables, bf16[1,2,768,3072]{3,2,1,0:T(8,128)(2,1)} %kids.3), custom_call_target="tpu_custom_call" | custom-call | tf_op jit(solution)/shard_map/remain/pallas_call | solution.py:362
  8.3 11.6 %collective-permute-done.refs_6_ = bf16[400,128]{1,0:T(8,128)(2,1)S(1)} collective-permute-done((bf16[400,128]{1,0:T(8,128)(2,1)S(1)}, bf16[400,128]{1,0:T(8,128)(2,1)S(1)}, u32[]{:S(2)}, u32[]{:S(2)}) %collective-permute-start) | collective-permute-done | bytes 102432 | tf_op jit(solution)/shard_map/ppermute | solution.py:330
  19.9 0.0 collective-permute-done.2.refs_4_.refs_6_
  19.9 0.0 collective-permute-done.1.refs_2_.refs_8_
  19.9 0.1 collective-permute-start.6
  20.0 0.6 %collective-permute-start.7 = (bf16[1936,128]{1,0:T(8,128)(2,1)S(1)}, bf16[1936,128]{1,0:T(8,128)(2,1)S(1)}, u32[]{:S(2)}, u32[]{:S(2)}) collective-permute-start(bf16[1936,128]{1,0:T(8,128)(2,1)S(1)} %collective-permute-done.2.refs_4_.refs_6_), channel_id=1, source_target_pairs={{0,4},{4,0},{8,12},{12,8},{1,5},{5,1},{9,13},{13,9},{2,6},{6,2},{1... | collective-permute-start | bytes 1486856 | tf_op jit(solution)/shard_map/ppermute | solution.py:323
  20.6 0.1 collective-permute-start.8
  20.7 0.4 collective-permute-start.5
  21.1 1.8 %collective-permute-start.4 = (bf16[2304,128]{1,0:T(8,128)(2,1)S(1)}, bf16[2304,128]{1,0:T(8,128)(2,1)S(1)}, u32[]{:S(2)}, u32[]{:S(2)}) collective-permute-start(bf16[2304,128]{1,0:T(8,128)(2,1)S(1)} %get-tuple-element.31), channel_id=1, source_target_pairs={{0,24},{4,28},{8,16},{12,20},{16,8},{20,12},{24,0},{28,4},{1,25},{... | collective-permute-start | bytes 1769480 | tf_op jit(solution)/shard_map/ppermute | solution.py:330
  23.0 0.0 collective-permute-done.8.refs_7_
  23.0 1.6 %collective-permute-start.3 = (bf16[1536,128]{1,0:T(8,128)(2,1)S(1)}, bf16[1536,128]{1,0:T(8,128)(2,1)S(1)}, u32[]{:S(2)}, u32[]{:S(2)}) collective-permute-start(bf16[1536,128]{1,0:T(8,128)(2,1)S(1)} %pad_maximum_fusion), channel_id=1, source_target_pairs={{0,1},{1,0},{2,3},{3,2},{4,5},{5,4},{6,7},{7,6},{8,9},{9,8},{10,11... | collective-permute-start | bytes 1179656 | tf_op jit(solution)/shard_map/ppermute | solution.py:333
  24.6 5.1 %first_factor.1 = (f32[128,128]{1,0:T(8,128)S(1)}, f32[128,128]{1,0:T(8,128)S(1)}, f32[128,128]{1,0:T(8,128)S(1)}) custom-call(bf16[1936,128]{1,0:T(8,128)(2,1)S(1)} %get-tuple-element.32.refs_0_.refs_2_, bf16[1936,128]{1,0:T(8,128)(2,1)S(1)} %collective-permute-done.5.refs_1_.refs_4_, bf16[1936,128]{1,0:T(8,128)(2,1)S(1)} %collective-permute-done.1.refs_2_.refs_8_, ...), custom_call_target="tpu_custom_call" | custom-call | tf_op jit(solution)/shard_map/first_factor/pallas_call | solution.py:390
  29.7 4.4 %second_factor.1.inverse = f32[256,256]{1,0:T(8,128)S(1)} custom-call(f32[128,128]{1,0:T(8,128)S(1)} %get-tuple-element.34.first, f32[128,128]{1,0:T(8,128)S(1)} %get-tuple-element.35.below, f32[128,128]{1,0:T(8,128)S(1)} %get-tuple-element.36.rest), custom_call_target="tpu_custom_call" | custom-call | tf_op jit(solution)/shard_map/second_factor/pallas_call | solution.py:397
  34.1 3.2 %collective-permute-done.4.refs_10_ = bf16[2304,128]{1,0:T(8,128)(2,1)S(1)} collective-permute-done((bf16[2304,128]{1,0:T(8,128)(2,1)S(1)}, bf16[2304,128]{1,0:T(8,128)(2,1)S(1)}, u32[]{:S(2)}, u32[]{:S(2)}) %collective-permute-start.4) | collective-permute-done | bytes 589856 | tf_op jit(solution)/shard_map/ppermute | solution.py:330
  37.3 0.5 %collective-permute-start.9 = (bf16[1536,128]{1,0:T(8,128)(2,1)S(1)}, bf16[1536,128]{1,0:T(8,128)(2,1)S(1)}, u32[]{:S(2)}, u32[]{:S(2)}) collective-permute-start(bf16[1536,128]{1,0:T(8,128)(2,1)S(1)} %collective-permute-done.3.refs_0_), channel_id=1, source_target_pairs={{0,4},{4,0},{8,12},{12,8},{1,5},{5,1},{9,13},{13,9},{2,6},{6,2},{1... | collective-permute-start | bytes 1179656 | tf_op jit(solution)/shard_map/ppermute | solution.py:323
  37.8 0.0 collective-permute-start.10
  37.9 2.3 %collective-permute-done.10.refs_5_ = bf16[768,128]{1,0:T(8,128)(2,1)S(1)} collective-permute-done((bf16[768,128]{1,0:T(8,128)(2,1)S(1)}, bf16[768,128]{1,0:T(8,128)(2,1)S(1)}, u32[]{:S(2)}, u32[]{:S(2)}) %collective-permute-start.10) | collective-permute-done | bytes 196640 | tf_op jit(solution)/shard_map/ppermute | solution.py:323
  40.2 4.5 %front.1 = f32[1,2304,128]{2,1,0:T(8,128)} custom-call(s32[2,72]{1,0:T(2,128)S(1)} %pad_add_fusion.tables, s32[1,4,72]{2,1,0:T(4,128)S(1)} %bitcast.2, f32[1,2304]{1,0:T(1,128)S(1)} %copy-done, f32[256,256]{1,0:T(8,128)S(1)} %second_factor.1.inverse, bf16[1536,128]{1,0:T(8,128)(2,1)S(1)} %collective-permute-done.3.refs_0_, ...), custom_call_target="tpu_custom_call" | custom-call | tf_op jit(solution)/shard_map/front/pallas_call | solution.py:441
  (15 shorter events, 0.1 us)
Async XLA Ops:
  2.2 38.0 %copy-start = (f32[1,2304]{1,0:T(1,128)S(1)}, f32[1,2304]{1,0:T(1,128)}, u32[]{:S(2)}) copy-start(f32[1,2304]{1,0:T(1,128)} %diag.1) | copy-start | bytes 27652
  2.2 38.0 %copy-start.1 = (s32[1,72,4]{1,2,0:T(4,128)S(1)}, s32[1,72,4]{1,2,0:T(4,128)}, u32[]{:S(2)}) copy-start(s32[1,72,4]{1,2,0:T(4,128)} %param.6) | copy-start | bytes 3460
  2.2 17.7 %collective-permute-start.2 = (bf16[1936,128]{1,0:T(8,128)(2,1)S(1)}, bf16[1936,128]{1,0:T(8,128)(2,1)S(1)}, u32[]{:S(2)}, u32[]{:S(2)}) collective-permute-start(bf16[1936,128]{1,0:T(8,128)(2,1)S(1)} %get-tuple-element.26), channel_id=1, source_target_pairs={{0,16},{4,20},{8,24},{12,28},{16,0},{20,4},{24,8},{28,12},{1,17},{... | collective-permute-start | bytes 1486856 | tf_op jit(solution)/shard_map/ppermute | solution.py:330
  4.4 15.5 %collective-permute-start.1 = (bf16[1936,128]{1,0:T(8,128)(2,1)S(1)}, bf16[1936,128]{1,0:T(8,128)(2,1)S(1)}, u32[]{:S(2)}, u32[]{:S(2)}) collective-permute-start(bf16[1936,128]{1,0:T(8,128)(2,1)S(1)} %get-tuple-element.32.refs_0_.refs_2_), channel_id=1, source_target_pairs={{0,8},{4,12},{8,0},{12,4},{1,9},{5,13},{9,1},{13,5},{2,10},{6,14},... | collective-permute-start | bytes 1486856 | tf_op jit(solution)/shard_map/ppermute | solution.py:320
  5.9 14.0 %collective-permute-start = (bf16[400,128]{1,0:T(8,128)(2,1)S(1)}, bf16[400,128]{1,0:T(8,128)(2,1)S(1)}, u32[]{:S(2)}, u32[]{:S(2)}) collective-permute-start(bf16[400,128]{1,0:T(8,128)(2,1)S(1)} %get-tuple-element.24), channel_id=1, source_target_pairs={{0,24},{4,28},{8,16},{12,20},{16,8},{20,12},{24,0},{28,4},{1,25},{... | collective-permute-start | bytes 307208 | tf_op jit(solution)/shard_map/ppermute | solution.py:330
  19.9 4.7 %collective-permute-start.6 = (bf16[1936,128]{1,0:T(8,128)(2,1)S(1)}, bf16[1936,128]{1,0:T(8,128)(2,1)S(1)}, u32[]{:S(2)}, u32[]{:S(2)}) collective-permute-start(bf16[1936,128]{1,0:T(8,128)(2,1)S(1)} %collective-permute-done.1.refs_2_.refs_8_), channel_id=1, source_target_pairs={{0,4},{4,0},{8,12},{12,8},{1,5},{5,1},{9,13},{13,9},{2,6},{6,2},{1... | collective-permute-start | bytes 1486856 | tf_op jit(solution)/shard_map/ppermute | solution.py:323
  20.0 4.6 %collective-permute-start.7 = (bf16[1936,128]{1,0:T(8,128)(2,1)S(1)}, bf16[1936,128]{1,0:T(8,128)(2,1)S(1)}, u32[]{:S(2)}, u32[]{:S(2)}) collective-permute-start(bf16[1936,128]{1,0:T(8,128)(2,1)S(1)} %collective-permute-done.2.refs_4_.refs_6_), channel_id=1, source_target_pairs={{0,4},{4,0},{8,12},{12,8},{1,5},{5,1},{9,13},{13,9},{2,6},{6,2},{1... | collective-permute-start | bytes 1486856 | tf_op jit(solution)/shard_map/ppermute | solution.py:323
  20.6 2.4 %collective-permute-start.8 = (bf16[400,128]{1,0:T(8,128)(2,1)S(1)}, bf16[400,128]{1,0:T(8,128)(2,1)S(1)}, u32[]{:S(2)}, u32[]{:S(2)}) collective-permute-start(bf16[400,128]{1,0:T(8,128)(2,1)S(1)} %collective-permute-done.refs_6_), channel_id=1, source_target_pairs={{0,4},{4,0},{8,12},{12,8},{1,5},{5,1},{9,13},{13,9},{2,6},{6,2},{1... | collective-permute-start | bytes 307208 | tf_op jit(solution)/shard_map/ppermute | solution.py:323
  20.7 3.9 %collective-permute-start.5 = (bf16[1936,128]{1,0:T(8,128)(2,1)S(1)}, bf16[1936,128]{1,0:T(8,128)(2,1)S(1)}, u32[]{:S(2)}, u32[]{:S(2)}) collective-permute-start(bf16[1936,128]{1,0:T(8,128)(2,1)S(1)} %get-tuple-element.32.refs_0_.refs_2_), channel_id=1, source_target_pairs={{0,4},{4,0},{8,12},{12,8},{1,5},{5,1},{9,13},{13,9},{2,6},{6,2},{1... | collective-permute-start | bytes 1486856 | tf_op jit(solution)/shard_map/ppermute | solution.py:323
  21.1 16.2 %collective-permute-start.4 = (bf16[2304,128]{1,0:T(8,128)(2,1)S(1)}, bf16[2304,128]{1,0:T(8,128)(2,1)S(1)}, u32[]{:S(2)}, u32[]{:S(2)}) collective-permute-start(bf16[2304,128]{1,0:T(8,128)(2,1)S(1)} %get-tuple-element.31), channel_id=1, source_target_pairs={{0,24},{4,28},{8,16},{12,20},{16,8},{20,12},{24,0},{28,4},{1,25},{... | collective-permute-start | bytes 1769480 | tf_op jit(solution)/shard_map/ppermute | solution.py:330
  23.0 11.2 %collective-permute-start.3 = (bf16[1536,128]{1,0:T(8,128)(2,1)S(1)}, bf16[1536,128]{1,0:T(8,128)(2,1)S(1)}, u32[]{:S(2)}, u32[]{:S(2)}) collective-permute-start(bf16[1536,128]{1,0:T(8,128)(2,1)S(1)} %pad_maximum_fusion), channel_id=1, source_target_pairs={{0,1},{1,0},{2,3},{3,2},{4,5},{5,4},{6,7},{7,6},{8,9},{9,8},{10,11... | collective-permute-start | bytes 1179656 | tf_op jit(solution)/shard_map/ppermute | solution.py:333
  37.3 2.9 %collective-permute-start.11 = (bf16[2304,128]{1,0:T(8,128)(2,1)S(1)}, bf16[2304,128]{1,0:T(8,128)(2,1)S(1)}, u32[]{:S(2)}, u32[]{:S(2)}) collective-permute-start(bf16[2304,128]{1,0:T(8,128)(2,1)S(1)} %collective-permute-done.4.refs_10_), channel_id=1, source_target_pairs={{0,4},{4,0},{8,12},{12,8},{1,5},{5,1},{9,13},{13,9},{2,6},{6,2},{1... | collective-permute-start | bytes 1769480 | tf_op jit(solution)/shard_map/ppermute | solution.py:323
  37.3 2.8 %collective-permute-start.9 = (bf16[1536,128]{1,0:T(8,128)(2,1)S(1)}, bf16[1536,128]{1,0:T(8,128)(2,1)S(1)}, u32[]{:S(2)}, u32[]{:S(2)}) collective-permute-start(bf16[1536,128]{1,0:T(8,128)(2,1)S(1)} %collective-permute-done.3.refs_0_), channel_id=1, source_target_pairs={{0,4},{4,0},{8,12},{12,8},{1,5},{5,1},{9,13},{13,9},{2,6},{6,2},{1... | collective-permute-start | bytes 1179656 | tf_op jit(solution)/shard_map/ppermute | solution.py:323
  37.8 2.3 %collective-permute-start.10 = (bf16[768,128]{1,0:T(8,128)(2,1)S(1)}, bf16[768,128]{1,0:T(8,128)(2,1)S(1)}, u32[]{:S(2)}, u32[]{:S(2)}) collective-permute-start(bf16[768,128]{1,0:T(8,128)(2,1)S(1)} %get-tuple-element.39.refs_3_), channel_id=1, source_target_pairs={{0,4},{4,0},{8,12},{12,8},{1,5},{5,1},{9,13},{13,9},{2,6},{6,2},{1... | collective-permute-start | bytes 589832 | tf_op jit(solution)/shard_map/ppermute | solution.py:323

commit v4 on v3

--- a/solution.py
+++ b/solution.py
@@ -13,6 +13,8 @@
 F32 = jnp.float32
 BF16 = jnp.bfloat16
 HIGHEST = lax.Precision.HIGHEST
+NOTES = 2 * BLOCK
+WINDOW = NOTES + 16
 MIB = 1024 * 1024
 
 
@@ -47,7 +49,7 @@
             copy.wait()
 
 
-def select_kernel(maps_hbm, diag_hbm, kids, tables, own_side, far_window, far_side, maps, diag, sems):
+def select_kernel(maps_hbm, diag_hbm, kids, tables, own_side, far_window, far_side, maps, diag, corner, sems):
     first = pltpu.make_async_copy(maps_hbm, maps, sems.at[sems.shape[0] - 2])
     second = pltpu.make_async_copy(diag_hbm, diag, sems.at[sems.shape[0] - 1])
     first.start()
@@ -74,16 +76,16 @@
         )
         if child == 1:
             line = jnp.broadcast_to(line, (16, places)).astype(BF16)
-            far_side[3 * BLOCK : lines, 0:places] = line
-            far_window[3 * BLOCK :, 0:places] = line
+            table = jnp.concatenate([line, jnp.zeros((16, BLOCK - places), BF16)], axis=1)
     copies = []
-    for child, out in ((1, far_window), (0, own_side), (1, far_side)):
-        for at, (w, p) in enumerate(((0, 0), (1, 0), (1, 1))):
+    for child, out in ((0, own_side), (1, far_side)):
+        targets = (out.at[pl.ds(0, BLOCK)], out.at[pl.ds(BLOCK, BLOCK)], corner.at[child])
+        for (w, p), target in zip(((0, 0), (1, 0), (1, 1)), targets):
             row = found[child][w]
             offset = row - me * local
             here = (row < none) & (offset >= 0) & (offset < local)
-            target = out.at[pl.ds(at * BLOCK, BLOCK)]
             copy_columns(kids, sems, copies, found, child, p, offset * BLOCK, BLOCK, target, here)
+    corners = list(copies)
     half = rows // 2
     for child, out in ((0, own_side), (1, far_side)):
         for p in range(NPANEL):
@@ -101,8 +103,20 @@
             part = rest.astype(BF16).astype(F32)
             pieces = jnp.where(line == 3 * p + at, part, pieces)
             rest = rest - part
-    own_side[3 * BLOCK : lines, :] = jnp.where(me == 0, pieces, 0.0).astype(BF16)
-    finish(copies)
+    pieces = jnp.where(me == 0, pieces, 0.0)
+    finish(corners)
+    row_id = lax.broadcasted_iota(jnp.int32, (BLOCK, BLOCK), 0)
+    col_id = lax.broadcasted_iota(jnp.int32, (BLOCK, BLOCK), 1)
+    for child, out in ((0, own_side), (1, far_side)):
+        upper = corner[child].astype(F32)
+        lower = out[0:BLOCK, :].astype(F32)
+        out[0:BLOCK, :] = jnp.where(row_id >= col_id, lower, upper).astype(BF16)
+        middle = jnp.sum(jnp.where(row_id == col_id, upper, 0.0), axis=0, keepdims=True)
+        notes = jnp.where(line == 6, jnp.broadcast_to(middle, (16, BLOCK)), 0.0)
+        notes = notes + pieces if child == 0 else jnp.where(line == 7, table.astype(F32), notes)
+        out[NOTES:lines, :] = notes.astype(BF16)
+    far_window[...] = far_side[0:lines, :]
+    finish(copies[len(corners) :])
 
 
 def remain_kernel(tables, kids, far_all, own_rest, sems):
@@ -192,29 +206,32 @@
     own, far = refs[:n_own], refs[n_own:-3]
     inverse, below, rest = refs[-3:]
 
-    def total(at):
+    def total(group, start, size):
         value = None
-        for ref in own + far:
-            block = ref[at * BLOCK : (at + 1) * BLOCK, :].astype(F32)
-            value = block if value is None else value + block
+        for ref in group:
+            part = ref[start : start + size, :].astype(F32)
+            value = part if value is None else value + part
         return value
 
-    pieces = None
-    for ref in own:
-        part = ref[3 * BLOCK : 3 * BLOCK + 16, :].astype(F32)
-        pieces = part if pieces is None else pieces + part
-    eye = lax.broadcasted_iota(jnp.int32, (BLOCK, BLOCK), 0) == lax.broadcasted_iota(
-        jnp.int32, (BLOCK, BLOCK), 1
-    )
-
-    def diagonal(p):
-        line = pieces[3 * p : 3 * p + 1] + pieces[3 * p + 1 : 3 * p + 2]
-        line = line + pieces[3 * p + 2 : 3 * p + 3]
-        return jnp.where(eye, jnp.broadcast_to(line, (BLOCK, BLOCK)), 0.0)
-
-    inverse[...] = invert(total(0) + diagonal(0))
-    below[...] = dot(total(1), inverse[...], 1, 1)
-    rest[...] = total(2) + diagonal(1) - dot(below[...], below[...], 1, 1)
+    row_id = lax.broadcasted_iota(jnp.int32, (BLOCK, BLOCK), 0)
+    col_id = lax.broadcasted_iota(jnp.int32, (BLOCK, BLOCK), 1)
+    own_notes, far_notes = total(own, NOTES, 16), total(far, NOTES, 16)
+
+    def diagonal(line):
+        return jnp.where(row_id == col_id, jnp.broadcast_to(line, (BLOCK, BLOCK)), 0.0)
+
+    def initial(p):
+        line = own_notes[3 * p : 3 * p + 1] + own_notes[3 * p + 1 : 3 * p + 2]
+        return line + own_notes[3 * p + 2 : 3 * p + 3]
+
+    corners = total(own + far, 0, BLOCK)
+    lower = jnp.where(row_id > col_id, corners, 0.0)
+    middle = jnp.where(row_id == col_id, corners, 0.0)
+    upper = jnp.where(row_id < col_id, corners, 0.0)
+    inverse[...] = invert(lower + lower.T + middle + diagonal(initial(0)))
+    below[...] = dot(total(own + far, BLOCK, BLOCK), inverse[...], 1, 1)
+    line = own_notes[6:7] + far_notes[6:7] + initial(1)
+    rest[...] = upper + upper.T + diagonal(line) - dot(below[...], below[...], 1, 1)
 
 
 def second_kernel(first, below, rest, out):
@@ -332,7 +349,7 @@
     def neighbour(x):
         return lax.ppermute(x, "col", [(i, i ^ 1) for i in range(n_col)])
 
-    lines = 3 * BLOCK + 16
+    lines = WINDOW
     maps = jnp.swapaxes(maps, 2, 3)
     mask = jnp.swapaxes(mask, 1, 2)
     def shapes(*sizes):
@@ -353,7 +370,8 @@
         scratch_shapes=[
             pltpu.VMEM(maps.shape, jnp.int32),
             pltpu.VMEM(diag.shape, F32),
-            pltpu.SemaphoreType.DMA((17,)),
+            pltpu.VMEM((2, BLOCK, BLOCK), BF16),
+            pltpu.SemaphoreType.DMA((14,)),
         ],
         compiler_params=params(),
         cost_estimate=cost(0),
@@ -373,11 +391,13 @@
     far_windows = [parent(far_window, s) for s in range(1, chips)]
     own_sides = [along(own_side, s) for s in range(1, chips)]
     far_near = parent(far_side, 0)
-    arrived = (far_windows, own_sides, far_near, own_side, far_all)
+    own_side, own_rest, far_all = lax.optimization_barrier((own_side, own_rest, far_all))
+    own_pair, own_rest = both(own_side), both(own_rest)
+    arrived = (far_windows, own_sides, far_near, own_pair, own_rest, far_all)
     arrived = lax.optimization_barrier(arrived)
-    far_windows, own_sides, far_near, own_side, far_all = arrived
+    far_windows, own_sides, far_near, own_pair, own_rest, far_all = arrived
     far_windows = [both(x) for x in far_windows]
-    own_sides = [both(own_side)] + [both(x) for x in own_sides]
+    own_sides = [own_pair] + [both(x) for x in own_sides]
     far_near = both(far_near)
     far_alls = [parent(far_all, s) for s in range(1, chips)]
     own_parts = [x for pair in own_sides for x in pair]
@@ -385,7 +405,7 @@
     middle = slice(lines, lines + rows_here)
     halves = [x[middle] for x, _ in own_sides[1:]] + [far_near[0][middle]]
     others = neighbour(jnp.concatenate(halves, axis=0))
-    far_table = far_near[0][3 * BLOCK, : tables.shape[1]].astype(jnp.int32)
+    far_table = far_near[0][NOTES + 7, : tables.shape[1]].astype(jnp.int32)
     square = jax.ShapeDtypeStruct((BLOCK, BLOCK), F32)
     first = pl.pallas_call(
         functools.partial(first_kernel, len(own_parts)),
@@ -402,10 +422,9 @@
         name="second_factor",
     )(*first)
 
-    remote = (own_rest, others, far_alls)
-    remote, inverse = lax.optimization_barrier((remote, inverse))
-    own_rest, others, far_alls = remote
-    own_rest, others = both(own_rest), both(others)
+    remote, inverse = lax.optimization_barrier(((others, far_alls), inverse))
+    others, far_alls = remote
+    others = both(others)
 
     def owner(side, s):
         def position(me):

time: 45 us -> 42.8 us (0.951)
  waiting for transfers between devices: 17.1 us -> 14.1 us
  starting transfers between devices: 9.58 us -> 10.6 us
    ppermute x3, waiting for transfers between devices: 14.7 us -> 10.8 us  [parent(): return lax.ppermute(x, ('front', 'row'), pairs)]
    ppermute x3, starting transfers between devices: 4.8 us -> 5.92 us  [parent(): return lax.ppermute(x, ('front', 'row'), pairs)]
    ppermute x7, waiting for transfers between devices: 2.33 us -> 3.3 us  [partner(): return lax.ppermute(x, 'row', [(i, i ^ 1) for i in range(n_row)])]
  transfers between devices with their start and end apart: 12 -> 12, of which waited for: 3 -> 4; matrix products, arithmetic and copies ran while one was open for 0% -> 0% of each run, Pallas kernels for 25% -> 26%
where the time goes in v4:
time: 42.8 us; the launch traced here: 42.6 us
  Pallas kernels  17.7 us (41%)
  waiting for transfers between devices  14.1 us (33%)
  starting transfers between devices  10.6 us (25%)
    ppermute x3, waiting for transfers between devices, parent(): return lax.ppermute(x, ('front', 'row'), pairs)  10.8 us
    ppermute x3, starting transfers between devices, parent(): return lax.ppermute(x, ('front', 'row'), pairs)  5.92 us
    pallas_call x1, Pallas kernels, body(): pl.pallas_call(functools.partial(first_kernel, len(own_parts)), out_shape...  5.17 us
    pallas_call x1, Pallas kernels, body(): pl.pallas_call(functools.partial(front_kernel, layout, n_row, row_blocks)...  4.5 us
    pallas_call x1, Pallas kernels, body(): pl.pallas_call(second_kernel, out_shape=jax.ShapeDtypeStruct((NPANEL * PW...  4.37 us
    ppermute x7, waiting for transfers between devices, partner(): return lax.ppermute(x, 'row', [(i, i ^ 1) for i in range(n_row)])  3.3 us
    pallas_call x1, Pallas kernels, body(): pl.pallas_call(select_kernel, out_shape=[jax.ShapeDtypeStruct((2, maps.sh...  2.09 us
    ppermute x7, starting transfers between devices, partner(): return lax.ppermute(x, 'row', [(i, i ^ 1) for i in range(n_row)])  1.71 us
  transfers between devices with their start and end apart: 12, of which 4 were waited for; matrix products, arithmetic and copies ran while one was open for 0% of the time, Pallas kernels for 26%

profile of v4, /device:TPU:0, one launch (start us, length us, event | category | flops | bytes accessed | tf_op | source)
XLA Modules:
  0.0 42.6 jit_solution(18306962026195236893)
XLA Ops:
  0.0 2.1 %select.1 = (s32[2,72]{1,0:T(2,128)S(1)}, bf16[1808,128]{1,0:T(8,128)(2,1)S(1)}, bf16[272,128]{1,0:T(8,128)(2,1)S(1)}, bf16[1808,128]{1,0:T(8,128)(2,1)S(1)}) custom-call(s32[1,2,24,72]{3,2,1,0:T(8,128)} %bitcast.3, f32[1,2304]{1,0:T(1,128)} %diag.1, bf16[1,2,768,3072]{3,2,1,0:T(8,128)(2,1)} %kids.3), custom_call_target="tpu_custom_call" | custom-call | tf_op jit(solution)/shard_map/select/pallas_call | solution.py:364
  2.1 0.0 copy-start
  2.1 0.0 copy-start.1
  2.1 3.2 %collective-permute-start.2 = (bf16[1808,128]{1,0:T(8,128)(2,1)S(1)}, bf16[1808,128]{1,0:T(8,128)(2,1)S(1)}, u32[]{:S(2)}, u32[]{:S(2)}) collective-permute-start(bf16[1808,128]{1,0:T(8,128)(2,1)S(1)} %get-tuple-element.31), channel_id=1, source_target_pairs={{0,16},{4,20},{8,24},{12,28},{16,0},{20,4},{24,8},{28,12},{1,17},{... | collective-permute-start | bytes 1388552 | tf_op jit(solution)/shard_map/ppermute | solution.py:347
  5.3 1.5 %collective-permute-start.1 = (bf16[1808,128]{1,0:T(8,128)(2,1)S(1)}, bf16[1808,128]{1,0:T(8,128)(2,1)S(1)}, u32[]{:S(2)}, u32[]{:S(2)}) collective-permute-start(bf16[1808,128]{1,0:T(8,128)(2,1)S(1)} %get-tuple-element.40.refs_0_.refs_2_), channel_id=1, source_target_pairs={{0,8},{4,12},{8,0},{12,4},{1,9},{5,13},{9,1},{13,5},{2,10},{6,14},... | collective-permute-start | bytes 1388552 | tf_op jit(solution)/shard_map/ppermute | solution.py:337
  6.8 1.6 %remain.1 = (bf16[2304,128]{1,0:T(8,128)(2,1)S(1)}, bf16[768,128]{1,0:T(8,128)(2,1)S(1)}) custom-call(s32[2,72]{1,0:T(2,128)S(1)} %get-tuple-element.28.tables, bf16[1,2,768,3072]{3,2,1,0:T(8,128)(2,1)} %kids.3), custom_call_target="tpu_custom_call" | custom-call | tf_op jit(solution)/shard_map/remain/pallas_call | solution.py:380
  8.4 0.1 collective-permute-start.3
  8.5 0.5 %collective-permute-start.4 = (bf16[768,128]{1,0:T(8,128)(2,1)S(1)}, bf16[768,128]{1,0:T(8,128)(2,1)S(1)}, u32[]{:S(2)}, u32[]{:S(2)}) collective-permute-start(bf16[768,128]{1,0:T(8,128)(2,1)S(1)} %get-tuple-element.48.refs_3_), channel_id=1, source_target_pairs={{0,4},{4,0},{8,12},{12,8},{1,5},{5,1},{9,13},{13,9},{2,6},{6,2},{1... | collective-permute-start | bytes 589832 | tf_op jit(solution)/shard_map/ppermute | solution.py:340
  9.0 0.2 collective-permute-start
  9.1 9.5 %collective-permute-done.refs_6_ = bf16[272,128]{1,0:T(8,128)(2,1)S(1)} collective-permute-done((bf16[272,128]{1,0:T(8,128)(2,1)S(1)}, bf16[272,128]{1,0:T(8,128)(2,1)S(1)}, u32[]{:S(2)}, u32[]{:S(2)}) %collective-permute-start) | collective-permute-done | bytes 69664 | tf_op jit(solution)/shard_map/ppermute | solution.py:347
  18.6 0.0 collective-permute-done.2.refs_4_.refs_6_
  18.6 0.0 collective-permute-done.1.refs_2_.refs_8_
  18.7 0.0 collective-permute-done.3.refs_1_.refs_4_
  18.7 0.1 collective-permute-start.7
  18.8 0.6 %collective-permute-start.8 = (bf16[1808,128]{1,0:T(8,128)(2,1)S(1)}, bf16[1808,128]{1,0:T(8,128)(2,1)S(1)}, u32[]{:S(2)}, u32[]{:S(2)}) collective-permute-start(bf16[1808,128]{1,0:T(8,128)(2,1)S(1)} %collective-permute-done.2.refs_4_.refs_6_), channel_id=1, source_target_pairs={{0,4},{4,0},{8,12},{12,8},{1,5},{5,1},{9,13},{13,9},{2,6},{6,2},{1... | collective-permute-start | bytes 1388552 | tf_op jit(solution)/shard_map/ppermute | solution.py:340
  19.3 2.6 %collective-permute-start.6 = (bf16[2304,128]{1,0:T(8,128)(2,1)S(1)}, bf16[2304,128]{1,0:T(8,128)(2,1)S(1)}, u32[]{:S(2)}, u32[]{:S(2)}) collective-permute-start(bf16[2304,128]{1,0:T(8,128)(2,1)S(1)} %get-tuple-element.39), channel_id=1, source_target_pairs={{0,24},{4,28},{8,16},{12,20},{16,8},{20,12},{24,0},{28,4},{1,25},{... | collective-permute-start | bytes 1769480 | tf_op jit(solution)/shard_map/ppermute | solution.py:347
  22.0 1.5 %collective-permute-start.5 = (bf16[1536,128]{1,0:T(8,128)(2,1)S(1)}, bf16[1536,128]{1,0:T(8,128)(2,1)S(1)}, u32[]{:S(2)}, u32[]{:S(2)}) collective-permute-start(bf16[1536,128]{1,0:T(8,128)(2,1)S(1)} %pad_maximum_fusion), channel_id=1, source_target_pairs={{0,1},{1,0},{2,3},{3,2},{4,5},{5,4},{6,7},{7,6},{8,9},{9,8},{10,11... | collective-permute-start | bytes 1179656 | tf_op jit(solution)/shard_map/ppermute | solution.py:350
  23.4 1.3 %collective-permute-done.9.refs_7_ = bf16[272,128]{1,0:T(8,128)(2,1)S(1)} collective-permute-done((bf16[272,128]{1,0:T(8,128)(2,1)S(1)}, bf16[272,128]{1,0:T(8,128)(2,1)S(1)}, u32[]{:S(2)}, u32[]{:S(2)}) %collective-permute-start.9) | collective-permute-done | bytes 69664 | tf_op jit(solution)/shard_map/ppermute | solution.py:340
  24.7 5.2 %first_factor.1 = (f32[128,128]{1,0:T(8,128)S(1)}, f32[128,128]{1,0:T(8,128)S(1)}, f32[128,128]{1,0:T(8,128)S(1)}) custom-call(bf16[1808,128]{1,0:T(8,128)(2,1)S(1)} %get-tuple-element.40.refs_0_.refs_2_, bf16[1808,128]{1,0:T(8,128)(2,1)S(1)} %collective-permute-done.3.refs_1_.refs_4_, bf16[1808,128]{1,0:T(8,128)(2,1)S(1)} %collective-permute-done.1.refs_2_.refs_8_, ...), custom_call_target="tpu_custom_call" | custom-call | tf_op jit(solution)/shard_map/first_factor/pallas_call | solution.py:410
  29.9 4.4 %second_factor.1.inverse = f32[256,256]{1,0:T(8,128)S(1)} custom-call(f32[128,128]{1,0:T(8,128)S(1)} %get-tuple-element.43.first, f32[128,128]{1,0:T(8,128)S(1)} %get-tuple-element.44.below, f32[128,128]{1,0:T(8,128)S(1)} %get-tuple-element.45.rest), custom_call_target="tpu_custom_call" | custom-call | tf_op jit(solution)/shard_map/second_factor/pallas_call | solution.py:417
  34.3 1.3 %collective-permute-done.6.refs_10_ = bf16[2304,128]{1,0:T(8,128)(2,1)S(1)} collective-permute-done((bf16[2304,128]{1,0:T(8,128)(2,1)S(1)}, bf16[2304,128]{1,0:T(8,128)(2,1)S(1)}, u32[]{:S(2)}, u32[]{:S(2)}) %collective-permute-start.6) | collective-permute-done | bytes 589856 | tf_op jit(solution)/shard_map/ppermute | solution.py:347
  35.6 0.5 %collective-permute-start.10 = (bf16[1536,128]{1,0:T(8,128)(2,1)S(1)}, bf16[1536,128]{1,0:T(8,128)(2,1)S(1)}, u32[]{:S(2)}, u32[]{:S(2)}) collective-permute-start(bf16[1536,128]{1,0:T(8,128)(2,1)S(1)} %collective-permute-done.5.refs_0_), channel_id=1, source_target_pairs={{0,4},{4,0},{8,12},{12,8},{1,5},{5,1},{9,13},{13,9},{2,6},{6,2},{1... | collective-permute-start | bytes 1179656 | tf_op jit(solution)/shard_map/ppermute | solution.py:340
  36.1 2.0 %collective-permute-done.10.refs_1_ = bf16[1536,128]{1,0:T(8,128)(2,1)S(1)} collective-permute-done((bf16[1536,128]{1,0:T(8,128)(2,1)S(1)}, bf16[1536,128]{1,0:T(8,128)(2,1)S(1)}, u32[]{:S(2)}, u32[]{:S(2)}) %collective-permute-start.10) | collective-permute-done | bytes 393248 | tf_op jit(solution)/shard_map/ppermute | solution.py:340
  38.1 4.5 %front.1 = f32[1,2304,128]{2,1,0:T(8,128)} custom-call(s32[2,72]{1,0:T(2,128)S(1)} %pad_add_fusion.tables, s32[1,4,72]{2,1,0:T(4,128)S(1)} %bitcast.2, f32[1,2304]{1,0:T(1,128)S(1)} %copy-done, f32[256,256]{1,0:T(8,128)S(1)} %second_factor.1.inverse, bf16[1536,128]{1,0:T(8,128)(2,1)S(1)} %collective-permute-done.5.refs_0_, ...), custom_call_target="tpu_custom_call" | custom-call | tf_op jit(solution)/shard_map/front/pallas_call | solution.py:460
  (15 shorter events, 0.1 us)
Async XLA Ops:
  2.1 36.0 %copy-start = (f32[1,2304]{1,0:T(1,128)S(1)}, f32[1,2304]{1,0:T(1,128)}, u32[]{:S(2)}) copy-start(f32[1,2304]{1,0:T(1,128)} %diag.1) | copy-start | bytes 27652
  2.1 36.0 %copy-start.1 = (s32[1,72,4]{1,2,0:T(4,128)S(1)}, s32[1,72,4]{1,2,0:T(4,128)}, u32[]{:S(2)}) copy-start(s32[1,72,4]{1,2,0:T(4,128)} %param.6) | copy-start | bytes 3460
  2.1 16.5 %collective-permute-start.2 = (bf16[1808,128]{1,0:T(8,128)(2,1)S(1)}, bf16[1808,128]{1,0:T(8,128)(2,1)S(1)}, u32[]{:S(2)}, u32[]{:S(2)}) collective-permute-start(bf16[1808,128]{1,0:T(8,128)(2,1)S(1)} %get-tuple-element.31), channel_id=1, source_target_pairs={{0,16},{4,20},{8,24},{12,28},{16,0},{20,4},{24,8},{28,12},{1,17},{... | collective-permute-start | bytes 1388552 | tf_op jit(solution)/shard_map/ppermute | solution.py:347
  5.3 13.4 %collective-permute-start.1 = (bf16[1808,128]{1,0:T(8,128)(2,1)S(1)}, bf16[1808,128]{1,0:T(8,128)(2,1)S(1)}, u32[]{:S(2)}, u32[]{:S(2)}) collective-permute-start(bf16[1808,128]{1,0:T(8,128)(2,1)S(1)} %get-tuple-element.40.refs_0_.refs_2_), channel_id=1, source_target_pairs={{0,8},{4,12},{8,0},{12,4},{1,9},{5,13},{9,1},{13,5},{2,10},{6,14},... | collective-permute-start | bytes 1388552 | tf_op jit(solution)/shard_map/ppermute | solution.py:337
  8.4 10.2 %collective-permute-start.3 = (bf16[1808,128]{1,0:T(8,128)(2,1)S(1)}, bf16[1808,128]{1,0:T(8,128)(2,1)S(1)}, u32[]{:S(2)}, u32[]{:S(2)}) collective-permute-start(bf16[1808,128]{1,0:T(8,128)(2,1)S(1)} %get-tuple-element.40.refs_0_.refs_2_), channel_id=1, source_target_pairs={{0,4},{4,0},{8,12},{12,8},{1,5},{5,1},{9,13},{13,9},{2,6},{6,2},{1... | collective-permute-start | bytes 1388552 | tf_op jit(solution)/shard_map/ppermute | solution.py:340
  8.5 10.2 %collective-permute-start.4 = (bf16[768,128]{1,0:T(8,128)(2,1)S(1)}, bf16[768,128]{1,0:T(8,128)(2,1)S(1)}, u32[]{:S(2)}, u32[]{:S(2)}) collective-permute-start(bf16[768,128]{1,0:T(8,128)(2,1)S(1)} %get-tuple-element.48.refs_3_), channel_id=1, source_target_pairs={{0,4},{4,0},{8,12},{12,8},{1,5},{5,1},{9,13},{13,9},{2,6},{6,2},{1... | collective-permute-start | bytes 589832 | tf_op jit(solution)/shard_map/ppermute | solution.py:340
  9.0 9.7 %collective-permute-start = (bf16[272,128]{1,0:T(8,128)(2,1)S(1)}, bf16[272,128]{1,0:T(8,128)(2,1)S(1)}, u32[]{:S(2)}, u32[]{:S(2)}) collective-permute-start(bf16[272,128]{1,0:T(8,128)(2,1)S(1)} %get-tuple-element.29), channel_id=1, source_target_pairs={{0,24},{4,28},{8,16},{12,20},{16,8},{20,12},{24,0},{28,4},{1,25},{... | collective-permute-start | bytes 208904 | tf_op jit(solution)/shard_map/ppermute | solution.py:347
  18.7 6.0 %collective-permute-start.7 = (bf16[1808,128]{1,0:T(8,128)(2,1)S(1)}, bf16[1808,128]{1,0:T(8,128)(2,1)S(1)}, u32[]{:S(2)}, u32[]{:S(2)}) collective-permute-start(bf16[1808,128]{1,0:T(8,128)(2,1)S(1)} %collective-permute-done.1.refs_2_.refs_8_), channel_id=1, source_target_pairs={{0,4},{4,0},{8,12},{12,8},{1,5},{5,1},{9,13},{13,9},{2,6},{6,2},{1... | collective-permute-start | bytes 1388552 | tf_op jit(solution)/shard_map/ppermute | solution.py:340
  18.8 5.9 %collective-permute-start.8 = (bf16[1808,128]{1,0:T(8,128)(2,1)S(1)}, bf16[1808,128]{1,0:T(8,128)(2,1)S(1)}, u32[]{:S(2)}, u32[]{:S(2)}) collective-permute-start(bf16[1808,128]{1,0:T(8,128)(2,1)S(1)} %collective-permute-done.2.refs_4_.refs_6_), channel_id=1, source_target_pairs={{0,4},{4,0},{8,12},{12,8},{1,5},{5,1},{9,13},{13,9},{2,6},{6,2},{1... | collective-permute-start | bytes 1388552 | tf_op jit(solution)/shard_map/ppermute | solution.py:340
  19.3 16.2 %collective-permute-start.6 = (bf16[2304,128]{1,0:T(8,128)(2,1)S(1)}, bf16[2304,128]{1,0:T(8,128)(2,1)S(1)}, u32[]{:S(2)}, u32[]{:S(2)}) collective-permute-start(bf16[2304,128]{1,0:T(8,128)(2,1)S(1)} %get-tuple-element.39), channel_id=1, source_target_pairs={{0,24},{4,28},{8,16},{12,20},{16,8},{20,12},{24,0},{28,4},{1,25},{... | collective-permute-start | bytes 1769480 | tf_op jit(solution)/shard_map/ppermute | solution.py:347
  22.0 12.3 %collective-permute-start.5 = (bf16[1536,128]{1,0:T(8,128)(2,1)S(1)}, bf16[1536,128]{1,0:T(8,128)(2,1)S(1)}, u32[]{:S(2)}, u32[]{:S(2)}) collective-permute-start(bf16[1536,128]{1,0:T(8,128)(2,1)S(1)} %pad_maximum_fusion), channel_id=1, source_target_pairs={{0,1},{1,0},{2,3},{3,2},{4,5},{5,4},{6,7},{7,6},{8,9},{9,8},{10,11... | collective-permute-start | bytes 1179656 | tf_op jit(solution)/shard_map/ppermute | solution.py:350
  23.4 1.3 %collective-permute-start.9 = (bf16[272,128]{1,0:T(8,128)(2,1)S(1)}, bf16[272,128]{1,0:T(8,128)(2,1)S(1)}, u32[]{:S(2)}, u32[]{:S(2)}) collective-permute-start(bf16[272,128]{1,0:T(8,128)(2,1)S(1)} %collective-permute-done.refs_6_), channel_id=1, source_target_pairs={{0,4},{4,0},{8,12},{12,8},{1,5},{5,1},{9,13},{13,9},{2,6},{6,2},{1... | collective-permute-start | bytes 208904 | tf_op jit(solution)/shard_map/ppermute | solution.py:340
  35.6 2.6 %collective-permute-start.11 = (bf16[2304,128]{1,0:T(8,128)(2,1)S(1)}, bf16[2304,128]{1,0:T(8,128)(2,1)S(1)}, u32[]{:S(2)}, u32[]{:S(2)}) collective-permute-start(bf16[2304,128]{1,0:T(8,128)(2,1)S(1)} %collective-permute-done.6.refs_10_), channel_id=1, source_target_pairs={{0,4},{4,0},{8,12},{12,8},{1,5},{5,1},{9,13},{13,9},{2,6},{6,2},{1... | collective-permute-start | bytes 1769480 | tf_op jit(solution)/shard_map/ppermute | solution.py:340
  35.6 2.6 %collective-permute-start.10 = (bf16[1536,128]{1,0:T(8,128)(2,1)S(1)}, bf16[1536,128]{1,0:T(8,128)(2,1)S(1)}, u32[]{:S(2)}, u32[]{:S(2)}) collective-permute-start(bf16[1536,128]{1,0:T(8,128)(2,1)S(1)} %collective-permute-done.5.refs_0_), channel_id=1, source_target_pairs={{0,4},{4,0},{8,12},{12,8},{1,5},{5,1},{9,13},{13,9},{2,6},{6,2},{1... | collective-permute-start | bytes 1179656 | tf_op jit(solution)/shard_map/ppermute | solution.py:340

commit v5 on v4

--- a/solution.py
+++ b/solution.py
@@ -202,9 +202,9 @@
     return jnp.concatenate(inverse_factor(tiles), axis=0)
 
 
-def first_kernel(n_own, *refs):
-    own, far = refs[:n_own], refs[n_own:-3]
-    inverse, below, rest = refs[-3:]
+def factor_kernel(n_own, *refs):
+    own, far = refs[:n_own], refs[n_own:-2]
+    whole, panel = refs[-2:]
 
     def total(group, start, size):
         value = None
@@ -228,21 +228,25 @@
     lower = jnp.where(row_id > col_id, corners, 0.0)
     middle = jnp.where(row_id == col_id, corners, 0.0)
     upper = jnp.where(row_id < col_id, corners, 0.0)
-    inverse[...] = invert(lower + lower.T + middle + diagonal(initial(0)))
-    below[...] = dot(total(own + far, BLOCK, BLOCK), inverse[...], 1, 1)
+    first = invert(lower + lower.T + middle + diagonal(initial(0)))
+    below = dot(total(own + far, BLOCK, BLOCK), first, 1, 1)
     line = own_notes[6:7] + far_notes[6:7] + initial(1)
-    rest[...] = upper + upper.T + diagonal(line) - dot(below[...], below[...], 1, 1)
-
-
-def second_kernel(first, below, rest, out):
-    inverse = invert(rest[...])
-    out[0:BLOCK, 0:BLOCK] = first[...]
-    out[0:BLOCK, BLOCK:] = jnp.zeros((BLOCK, BLOCK), F32)
-    out[BLOCK:, 0:BLOCK] = -dot(inverse, dot(below[...], first[...]))
-    out[BLOCK:, BLOCK:] = inverse
-
-
-def front_kernel(layout, n_row, row_blocks, tables, mask, diag, inverse, *refs):
+    inverse = invert(upper + upper.T + diagonal(line) - dot(below, below, 1, 1))
+    base = dot(first, first, 0, 0)
+    corner = -dot(inverse, dot(below, first))
+    side = dot(corner, inverse, 0, 0)
+    left = jnp.concatenate([base + dot(corner, corner, 0, 0), side.T], axis=0)
+    right = jnp.concatenate([side, dot(inverse, inverse, 0, 0)], axis=0)
+    rest = jnp.concatenate([left, right], axis=1)
+    for at in range(3):
+        whole[at] = rest.astype(BF16)
+        rest = rest - whole[at].astype(F32)
+    is_first = lax.axis_index("col") == 0
+    panel[0:BLOCK, :] = -jnp.where(is_first, first, corner).T
+    panel[BLOCK:, :] = -jnp.where(is_first, 0.0, inverse.T)
+
+
+def front_kernel(layout, n_row, row_blocks, tables, mask, diag, whole, panel, *refs):
     out, weight, product, buffer = refs[-4:]
     me, col_index = lax.axis_index("row"), lax.axis_index("col")
     is_panel = col_index < NPANEL
@@ -256,7 +260,7 @@
         start = pl.multiple_of(owner(me) * rows, rows)
         buffer[child, pl.ds(start, rows), :] = refs[first][column : column + rows, :]
 
-    mirrored = jnp.zeros((BLOCK, wide), F32)
+    mirrored = [jnp.zeros((BLOCK, wide), F32)] * 2
     for child, owner, ref, at, side in parts:
         index = tables[child, col_index] * BLOCK
         for step in range(0, BLOCK, BLOCK // 2):
@@ -267,14 +271,17 @@
             lines = jnp.where(inside, jnp.concatenate(lines, axis=1).astype(F32), 0.0)
             empty = jnp.zeros_like(lines)
             lines = [lines, empty] if step == 0 else [empty, lines]
-            mirrored = mirrored + jnp.concatenate(lines, axis=0)
-
-    lower = inverse[...]
-    row_id = lax.broadcasted_iota(jnp.int32, (wide, PW), 0)
-    col_id = lax.broadcasted_iota(jnp.int32, (wide, PW), 1)
-    picked = -(row_id == col_id + col_index * PW).astype(F32)
-    solved = jnp.where(is_panel, picked, dot(lower, mirrored, 1, 1))
-    weight[...] = dot(lower, solved, 0, 0)
+            mirrored[child] = mirrored[child] + jnp.concatenate(lines, axis=0)
+
+    solved = panel[...] * jnp.where(is_panel, 1.0, 0.0)
+    keep = jnp.where(is_panel, 0.0, 1.0)
+    for lines in mirrored:
+        lines = (lines * keep).astype(BF16)
+        for at in range(3):
+            solved = solved + lax.dot_general(
+                whole[at], lines, (((1,), (1,)), ((), ())), preferred_element_type=F32
+            )
+    weight[...] = solved
     high = weight[...].astype(BF16)
     low = (weight[...] - high.astype(F32)).astype(BF16)
     both = jnp.concatenate([high, low], axis=1)
@@ -393,36 +400,31 @@
     far_near = parent(far_side, 0)
     own_side, own_rest, far_all = lax.optimization_barrier((own_side, own_rest, far_all))
     own_pair, own_rest = both(own_side), both(own_rest)
-    arrived = (far_windows, own_sides, far_near, own_pair, own_rest, far_all)
-    arrived = lax.optimization_barrier(arrived)
-    far_windows, own_sides, far_near, own_pair, own_rest, far_all = arrived
+    own_sides, far_all = lax.optimization_barrier((own_sides, far_all))
+    far_alls = [parent(far_all, s) for s in range(1, chips)]
+    arrived = (far_windows, own_sides, far_near, own_pair, own_rest)
+    far_windows, own_sides, far_near, own_pair, own_rest = lax.optimization_barrier(arrived)
     far_windows = [both(x) for x in far_windows]
     own_sides = [own_pair] + [both(x) for x in own_sides]
     far_near = both(far_near)
-    far_alls = [parent(far_all, s) for s in range(1, chips)]
     own_parts = [x for pair in own_sides for x in pair]
     far_parts = list(far_near) + [x for pair in far_windows for x in pair]
     middle = slice(lines, lines + rows_here)
     halves = [x[middle] for x, _ in own_sides[1:]] + [far_near[0][middle]]
     others = neighbour(jnp.concatenate(halves, axis=0))
     far_table = far_near[0][NOTES + 7, : tables.shape[1]].astype(jnp.int32)
-    square = jax.ShapeDtypeStruct((BLOCK, BLOCK), F32)
-    first = pl.pallas_call(
-        functools.partial(first_kernel, len(own_parts)),
-        out_shape=[square] * 3,
+    factors = pl.pallas_call(
+        functools.partial(factor_kernel, len(own_parts)),
+        out_shape=[
+            jax.ShapeDtypeStruct((3, NPANEL * PW, NPANEL * PW), BF16),
+            jax.ShapeDtypeStruct((NPANEL * PW, PW), F32),
+        ],
         compiler_params=params(),
         cost_estimate=cost(0),
-        name="first_factor",
+        name="factor",
     )(*own_parts, *far_parts)
-    inverse = pl.pallas_call(
-        second_kernel,
-        out_shape=jax.ShapeDtypeStruct((NPANEL * PW, NPANEL * PW), F32),
-        compiler_params=params(),
-        cost_estimate=cost(0),
-        name="second_factor",
-    )(*first)
-
-    remote, inverse = lax.optimization_barrier(((others, far_alls), inverse))
+
+    remote, factors = lax.optimization_barrier(((others, far_alls), factors))
     others, far_alls = remote
     others = both(others)
 
@@ -460,7 +462,7 @@
     return pl.pallas_call(
         functools.partial(front_kernel, layout, n_row, row_blocks),
         out_shape=jax.ShapeDtypeStruct((1, rows_dev, PW), F32),
-        in_specs=[smem, smem] + [vmem] * (2 + len(arrays)),
+        in_specs=[smem, smem] + [vmem] * (3 + len(arrays)),
         out_specs=vmem,
         scratch_shapes=[
             pltpu.VMEM((NPANEL * PW, PW), F32),
@@ -470,7 +472,7 @@
         compiler_params=params(),
         cost_estimate=cost(0),
         name="front",
-    )(tables, mask, diag, inverse, *arrays)
+    )(tables, mask, diag, *factors, *arrays)
 
 
 def solution(mesh):

time: 42.8 us -> 42.3 us (0.988)
    ppermute x3, waiting for transfers between devices: 10.8 us -> 1.44 us  [parent(): return lax.ppermute(x, ('front', 'row'), pairs)]
    ppermute x1, waiting for transfers between devices: 0.01 us -> 9.03 us  [along(): lax.ppermute(x, 'row', [(i, (i + 2 * by) % n_row) for i in range(n_row)])]
    pallas_call x1, Pallas kernels: 4.5 us -> 4.05 us  [body(): pl.pallas_call(functools.partial(front_kernel, layout, n_row, row_blocks)...]
    pallas_call x2 -> x1, Pallas kernels: 9.54 us -> 9.87 us  [body(): pl.pallas_call(functools.partial(factor_kernel, len(own_parts)), out_shap...]
  transfers between devices with their start and end apart: 12 -> 12, of which waited for: 4 -> 5; matrix products, arithmetic and copies ran while one was open for 0% -> 0% of each run, Pallas kernels for 26% -> 27%
where the time goes in v5:
time: 42.3 us; the launch traced here: 42.1 us
  Pallas kernels  17.7 us (42%)
  waiting for transfers between devices  13.8 us (33%)
  starting transfers between devices  10.4 us (25%)
    pallas_call x1, Pallas kernels, body(): pl.pallas_call(functools.partial(factor_kernel, len(own_parts)), out_shap...  9.87 us
    ppermute x1, waiting for transfers between devices, along(): lax.ppermute(x, 'row', [(i, (i + 2 * by) % n_row) for i in range(n_row)])  9.03 us
    ppermute x3, starting transfers between devices, parent(): return lax.ppermute(x, ('front', 'row'), pairs)  5.71 us
    pallas_call x1, Pallas kernels, body(): pl.pallas_call(functools.partial(front_kernel, layout, n_row, row_blocks)...  4.05 us
    ppermute x7, waiting for transfers between devices, partner(): return lax.ppermute(x, 'row', [(i, i ^ 1) for i in range(n_row)])  3.3 us
    pallas_call x1, Pallas kernels, body(): pl.pallas_call(select_kernel, out_shape=[jax.ShapeDtypeStruct((2, maps.sh...  2.14 us
    ppermute x7, starting transfers between devices, partner(): return lax.ppermute(x, 'row', [(i, i ^ 1) for i in range(n_row)])  1.71 us
    pallas_call x1, Pallas kernels, body(): pl.pallas_call(remain_kernel, out_shape=shapes(3 * rows_here, rows_here),...  1.67 us
  transfers between devices with their start and end apart: 12, of which 5 were waited for; matrix products, arithmetic and copies ran while one was open for 0% of the time, Pallas kernels for 27%

profile of v5, /device:TPU:0, one launch (start us, length us, event | category | flops | bytes accessed | tf_op | source)
XLA Modules:
  0.0 42.1 jit_solution(17944573248454356659)
XLA Ops:
  0.0 2.1 %select.1 = (s32[2,72]{1,0:T(2,128)S(1)}, bf16[1808,128]{1,0:T(8,128)(2,1)S(1)}, bf16[272,128]{1,0:T(8,128)(2,1)S(1)}, bf16[1808,128]{1,0:T(8,128)(2,1)S(1)}) custom-call(s32[1,2,24,72]{3,2,1,0:T(8,128)} %bitcast.3, f32[1,2304]{1,0:T(1,128)} %diag.1, bf16[1,2,768,3072]{3,2,1,0:T(8,128)(2,1)} %kids.3), custom_call_target="tpu_custom_call" | custom-call | tf_op jit(solution)/shard_map/select/pallas_call | solution.py:371
  2.1 3.1 %collective-permute-start.2 = (bf16[1808,128]{1,0:T(8,128)(2,1)S(1)}, bf16[1808,128]{1,0:T(8,128)(2,1)S(1)}, u32[]{:S(2)}, u32[]{:S(2)}) collective-permute-start(bf16[1808,128]{1,0:T(8,128)(2,1)S(1)} %get-tuple-element.36), channel_id=1, source_target_pairs={{0,16},{4,20},{8,24},{12,28},{16,0},{20,4},{24,8},{28,12},{1,17},{... | collective-permute-start | bytes 1388552 | tf_op jit(solution)/shard_map/ppermute | solution.py:354
  5.2 1.5 %collective-permute-start.1 = (bf16[1808,128]{1,0:T(8,128)(2,1)S(1)}, bf16[1808,128]{1,0:T(8,128)(2,1)S(1)}, u32[]{:S(2)}, u32[]{:S(2)}) collective-permute-start(bf16[1808,128]{1,0:T(8,128)(2,1)S(1)} %get-tuple-element.42.refs_0_.refs_2_), channel_id=1, source_target_pairs={{0,8},{4,12},{8,0},{12,4},{1,9},{5,13},{9,1},{13,5},{2,10},{6,14},... | collective-permute-start | bytes 1388552 | tf_op jit(solution)/shard_map/ppermute | solution.py:344
  6.7 1.7 %remain.1 = (bf16[2304,128]{1,0:T(8,128)(2,1)S(1)}, bf16[768,128]{1,0:T(8,128)(2,1)S(1)}) custom-call(s32[2,72]{1,0:T(2,128)S(1)} %get-tuple-element.29.tables, bf16[1,2,768,3072]{3,2,1,0:T(8,128)(2,1)} %kids.3), custom_call_target="tpu_custom_call" | custom-call | tf_op jit(solution)/shard_map/remain/pallas_call | solution.py:387
  8.4 0.1 collective-permute-start.3
  8.5 0.5 %collective-permute-start.4 = (bf16[768,128]{1,0:T(8,128)(2,1)S(1)}, bf16[768,128]{1,0:T(8,128)(2,1)S(1)}, u32[]{:S(2)}, u32[]{:S(2)}) collective-permute-start(bf16[768,128]{1,0:T(8,128)(2,1)S(1)} %get-tuple-element.50.refs_3_), channel_id=1, source_target_pairs={{0,4},{4,0},{8,12},{12,8},{1,5},{5,1},{9,13},{13,9},{2,6},{6,2},{1... | collective-permute-start | bytes 589832 | tf_op jit(solution)/shard_map/ppermute | solution.py:347
  9.0 0.0 collective-permute-start
  9.0 9.0 %collective-permute-done.1.refs_2_.refs_8_ = bf16[1808,128]{1,0:T(8,128)(2,1)S(1)} collective-permute-done((bf16[1808,128]{1,0:T(8,128)(2,1)S(1)}, bf16[1808,128]{1,0:T(8,128)(2,1)S(1)}, u32[]{:S(2)}, u32[]{:S(2)}) %collective-permute-start.1) | collective-permute-done | bytes 462880 | tf_op jit(solution)/shard_map/ppermute | solution.py:344
  18.0 0.5 %collective-permute-done.refs_6_ = bf16[272,128]{1,0:T(8,128)(2,1)S(1)} collective-permute-done((bf16[272,128]{1,0:T(8,128)(2,1)S(1)}, bf16[272,128]{1,0:T(8,128)(2,1)S(1)}, u32[]{:S(2)}, u32[]{:S(2)}) %collective-permute-start) | collective-permute-done | bytes 69664 | tf_op jit(solution)/shard_map/ppermute | solution.py:354
  18.6 0.0 collective-permute-done.4.refs_5_
  18.6 0.0 collective-permute-done.2.refs_4_.refs_6_
  18.6 0.0 collective-permute-done.3.refs_1_.refs_4_
  18.6 0.1 collective-permute-start.7
  18.7 0.6 %collective-permute-start.8 = (bf16[1808,128]{1,0:T(8,128)(2,1)S(1)}, bf16[1808,128]{1,0:T(8,128)(2,1)S(1)}, u32[]{:S(2)}, u32[]{:S(2)}) collective-permute-start(bf16[1808,128]{1,0:T(8,128)(2,1)S(1)} %collective-permute-done.2.refs_4_.refs_6_), channel_id=1, source_target_pairs={{0,4},{4,0},{8,12},{12,8},{1,5},{5,1},{9,13},{13,9},{2,6},{6,2},{1... | collective-permute-start | bytes 1388552 | tf_op jit(solution)/shard_map/ppermute | solution.py:347
  19.3 2.6 %collective-permute-start.6 = (bf16[2304,128]{1,0:T(8,128)(2,1)S(1)}, bf16[2304,128]{1,0:T(8,128)(2,1)S(1)}, u32[]{:S(2)}, u32[]{:S(2)}) collective-permute-start(bf16[2304,128]{1,0:T(8,128)(2,1)S(1)} %get-tuple-element.41), channel_id=1, source_target_pairs={{0,24},{4,28},{8,16},{12,20},{16,8},{20,12},{24,0},{28,4},{1,25},{... | collective-permute-start | bytes 1769480 | tf_op jit(solution)/shard_map/ppermute | solution.py:354
  21.9 1.5 %collective-permute-start.5 = (bf16[1536,128]{1,0:T(8,128)(2,1)S(1)}, bf16[1536,128]{1,0:T(8,128)(2,1)S(1)}, u32[]{:S(2)}, u32[]{:S(2)}) collective-permute-start(bf16[1536,128]{1,0:T(8,128)(2,1)S(1)} %pad_maximum_fusion), channel_id=1, source_target_pairs={{0,1},{1,0},{2,3},{3,2},{4,5},{5,4},{6,7},{7,6},{8,9},{9,8},{10,11... | collective-permute-start | bytes 1179656 | tf_op jit(solution)/shard_map/ppermute | solution.py:357
  23.4 0.0 collective-permute-start.9
  23.4 1.3 %collective-permute-done.9.refs_7_ = bf16[272,128]{1,0:T(8,128)(2,1)S(1)} collective-permute-done((bf16[272,128]{1,0:T(8,128)(2,1)S(1)}, bf16[272,128]{1,0:T(8,128)(2,1)S(1)}, u32[]{:S(2)}, u32[]{:S(2)}) %collective-permute-start.9) | collective-permute-done | bytes 69664 | tf_op jit(solution)/shard_map/ppermute | solution.py:347
  24.7 0.0 collective-permute-done.7.refs_3_.refs_9_
  24.7 9.9 %factor.1 = (bf16[3,256,256]{2,1,0:T(8,128)(2,1)S(1)}, f32[256,128]{1,0:T(8,128)S(1)}) custom-call(bf16[1808,128]{1,0:T(8,128)(2,1)S(1)} %get-tuple-element.42.refs_0_.refs_2_, bf16[1808,128]{1,0:T(8,128)(2,1)S(1)} %collective-permute-done.3.refs_1_.refs_4_, bf16[1808,128]{1,0:T(8,128)(2,1)S(1)} %collective-permute-done.1.refs_2_.refs_8_, ...), custom_call_target="tpu_custom_call" | custom-call | tf_op jit(solution)/shard_map/factor/pallas_call | solution.py:416
  34.6 0.9 %collective-permute-done.6.refs_10_ = bf16[2304,128]{1,0:T(8,128)(2,1)S(1)} collective-permute-done((bf16[2304,128]{1,0:T(8,128)(2,1)S(1)}, bf16[2304,128]{1,0:T(8,128)(2,1)S(1)}, u32[]{:S(2)}, u32[]{:S(2)}) %collective-permute-start.6) | collective-permute-done | bytes 589856 | tf_op jit(solution)/shard_map/ppermute | solution.py:354
  35.5 0.5 %collective-permute-start.10 = (bf16[1536,128]{1,0:T(8,128)(2,1)S(1)}, bf16[1536,128]{1,0:T(8,128)(2,1)S(1)}, u32[]{:S(2)}, u32[]{:S(2)}) collective-permute-start(bf16[1536,128]{1,0:T(8,128)(2,1)S(1)} %collective-permute-done.5.refs_0_), channel_id=1, source_target_pairs={{0,4},{4,0},{8,12},{12,8},{1,5},{5,1},{9,13},{13,9},{2,6},{6,2},{1... | collective-permute-start | bytes 1179656 | tf_op jit(solution)/shard_map/ppermute | solution.py:347
  36.0 2.0 %collective-permute-done.10.refs_1_ = bf16[1536,128]{1,0:T(8,128)(2,1)S(1)} collective-permute-done((bf16[1536,128]{1,0:T(8,128)(2,1)S(1)}, bf16[1536,128]{1,0:T(8,128)(2,1)S(1)}, u32[]{:S(2)}, u32[]{:S(2)}) %collective-permute-start.10) | collective-permute-done | bytes 393248 | tf_op jit(solution)/shard_map/ppermute | solution.py:347
  38.1 4.0 %front.1 = f32[1,2304,128]{2,1,0:T(8,128)} custom-call(s32[2,72]{1,0:T(2,128)S(1)} %pad_add_fusion.tables, s32[1,4,72]{2,1,0:T(4,128)S(1)} %bitcast.2, f32[1,2304]{1,0:T(1,128)S(1)} %copy-done, bf16[3,256,256]{2,1,0:T(8,128)(2,1)S(1)} %get-tuple-element.47.whole, f32[256,128]{1,0:T(8,128)S(1)} %get-tuple-element.48.panel, ...), custom_call_target="tpu_custom_call" | custom-call | tf_op jit(solution)/shard_map/front/pallas_call | solution.py:462
  (14 shorter events, 0.1 us)
Async XLA Ops:
  0.0 38.1 %copy-start = (f32[1,2304]{1,0:T(1,128)S(1)}, f32[1,2304]{1,0:T(1,128)}, u32[]{:S(2)}) copy-start(f32[1,2304]{1,0:T(1,128)} %diag.1) | copy-start | bytes 27652
  0.0 38.1 %copy-start.1 = (s32[1,72,4]{1,2,0:T(4,128)S(1)}, s32[1,72,4]{1,2,0:T(4,128)}, u32[]{:S(2)}) copy-start(s32[1,72,4]{1,2,0:T(4,128)} %param.6) | copy-start | bytes 3460
  2.1 16.4 %collective-permute-start.2 = (bf16[1808,128]{1,0:T(8,128)(2,1)S(1)}, bf16[1808,128]{1,0:T(8,128)(2,1)S(1)}, u32[]{:S(2)}, u32[]{:S(2)}) collective-permute-start(bf16[1808,128]{1,0:T(8,128)(2,1)S(1)} %get-tuple-element.36), channel_id=1, source_target_pairs={{0,16},{4,20},{8,24},{12,28},{16,0},{20,4},{24,8},{28,12},{1,17},{... | collective-permute-start | bytes 1388552 | tf_op jit(solution)/shard_map/ppermute | solution.py:354
  5.2 12.8 %collective-permute-start.1 = (bf16[1808,128]{1,0:T(8,128)(2,1)S(1)}, bf16[1808,128]{1,0:T(8,128)(2,1)S(1)}, u32[]{:S(2)}, u32[]{:S(2)}) collective-permute-start(bf16[1808,128]{1,0:T(8,128)(2,1)S(1)} %get-tuple-element.42.refs_0_.refs_2_), channel_id=1, source_target_pairs={{0,8},{4,12},{8,0},{12,4},{1,9},{5,13},{9,1},{13,5},{2,10},{6,14},... | collective-permute-start | bytes 1388552 | tf_op jit(solution)/shard_map/ppermute | solution.py:344
  8.4 10.2 %collective-permute-start.3 = (bf16[1808,128]{1,0:T(8,128)(2,1)S(1)}, bf16[1808,128]{1,0:T(8,128)(2,1)S(1)}, u32[]{:S(2)}, u32[]{:S(2)}) collective-permute-start(bf16[1808,128]{1,0:T(8,128)(2,1)S(1)} %get-tuple-element.42.refs_0_.refs_2_), channel_id=1, source_target_pairs={{0,4},{4,0},{8,12},{12,8},{1,5},{5,1},{9,13},{13,9},{2,6},{6,2},{1... | collective-permute-start | bytes 1388552 | tf_op jit(solution)/shard_map/ppermute | solution.py:347
  8.5 10.1 %collective-permute-start.4 = (bf16[768,128]{1,0:T(8,128)(2,1)S(1)}, bf16[768,128]{1,0:T(8,128)(2,1)S(1)}, u32[]{:S(2)}, u32[]{:S(2)}) collective-permute-start(bf16[768,128]{1,0:T(8,128)(2,1)S(1)} %get-tuple-element.50.refs_3_), channel_id=1, source_target_pairs={{0,4},{4,0},{8,12},{12,8},{1,5},{5,1},{9,13},{13,9},{2,6},{6,2},{1... | collective-permute-start | bytes 589832 | tf_op jit(solution)/shard_map/ppermute | solution.py:347
  9.0 9.6 %collective-permute-start = (bf16[272,128]{1,0:T(8,128)(2,1)S(1)}, bf16[272,128]{1,0:T(8,128)(2,1)S(1)}, u32[]{:S(2)}, u32[]{:S(2)}) collective-permute-start(bf16[272,128]{1,0:T(8,128)(2,1)S(1)} %get-tuple-element.30), channel_id=1, source_target_pairs={{0,24},{4,28},{8,16},{12,20},{16,8},{20,12},{24,0},{28,4},{1,25},{... | collective-permute-start | bytes 208904 | tf_op jit(solution)/shard_map/ppermute | solution.py:354
  18.6 6.1 %collective-permute-start.7 = (bf16[1808,128]{1,0:T(8,128)(2,1)S(1)}, bf16[1808,128]{1,0:T(8,128)(2,1)S(1)}, u32[]{:S(2)}, u32[]{:S(2)}) collective-permute-start(bf16[1808,128]{1,0:T(8,128)(2,1)S(1)} %collective-permute-done.1.refs_2_.refs_8_), channel_id=1, source_target_pairs={{0,4},{4,0},{8,12},{12,8},{1,5},{5,1},{9,13},{13,9},{2,6},{6,2},{1... | collective-permute-start | bytes 1388552 | tf_op jit(solution)/shard_map/ppermute | solution.py:347
  18.7 6.0 %collective-permute-start.8 = (bf16[1808,128]{1,0:T(8,128)(2,1)S(1)}, bf16[1808,128]{1,0:T(8,128)(2,1)S(1)}, u32[]{:S(2)}, u32[]{:S(2)}) collective-permute-start(bf16[1808,128]{1,0:T(8,128)(2,1)S(1)} %collective-permute-done.2.refs_4_.refs_6_), channel_id=1, source_target_pairs={{0,4},{4,0},{8,12},{12,8},{1,5},{5,1},{9,13},{13,9},{2,6},{6,2},{1... | collective-permute-start | bytes 1388552 | tf_op jit(solution)/shard_map/ppermute | solution.py:347
  19.3 16.2 %collective-permute-start.6 = (bf16[2304,128]{1,0:T(8,128)(2,1)S(1)}, bf16[2304,128]{1,0:T(8,128)(2,1)S(1)}, u32[]{:S(2)}, u32[]{:S(2)}) collective-permute-start(bf16[2304,128]{1,0:T(8,128)(2,1)S(1)} %get-tuple-element.41), channel_id=1, source_target_pairs={{0,24},{4,28},{8,16},{12,20},{16,8},{20,12},{24,0},{28,4},{1,25},{... | collective-permute-start | bytes 1769480 | tf_op jit(solution)/shard_map/ppermute | solution.py:354
  21.9 12.7 %collective-permute-start.5 = (bf16[1536,128]{1,0:T(8,128)(2,1)S(1)}, bf16[1536,128]{1,0:T(8,128)(2,1)S(1)}, u32[]{:S(2)}, u32[]{:S(2)}) collective-permute-start(bf16[1536,128]{1,0:T(8,128)(2,1)S(1)} %pad_maximum_fusion), channel_id=1, source_target_pairs={{0,1},{1,0},{2,3},{3,2},{4,5},{5,4},{6,7},{7,6},{8,9},{9,8},{10,11... | collective-permute-start | bytes 1179656 | tf_op jit(solution)/shard_map/ppermute | solution.py:357
  23.4 1.3 %collective-permute-start.9 = (bf16[272,128]{1,0:T(8,128)(2,1)S(1)}, bf16[272,128]{1,0:T(8,128)(2,1)S(1)}, u32[]{:S(2)}, u32[]{:S(2)}) collective-permute-start(bf16[272,128]{1,0:T(8,128)(2,1)S(1)} %collective-permute-done.refs_6_), channel_id=1, source_target_pairs={{0,4},{4,0},{8,12},{12,8},{1,5},{5,1},{9,13},{13,9},{2,6},{6,2},{1... | collective-permute-start | bytes 208904 | tf_op jit(solution)/shard_map/ppermute | solution.py:347
  35.5 2.6 %collective-permute-start.11 = (bf16[2304,128]{1,0:T(8,128)(2,1)S(1)}, bf16[2304,128]{1,0:T(8,128)(2,1)S(1)}, u32[]{:S(2)}, u32[]{:S(2)}) collective-permute-start(bf16[2304,128]{1,0:T(8,128)(2,1)S(1)} %collective-permute-done.6.refs_10_), channel_id=1, source_target_pairs={{0,4},{4,0},{8,12},{12,8},{1,5},{5,1},{9,13},{13,9},{2,6},{6,2},{1... | collective-permute-start | bytes 1769480 | tf_op jit(solution)/shard_map/ppermute | solution.py:347
  35.5 2.6 %collective-permute-start.10 = (bf16[1536,128]{1,0:T(8,128)(2,1)S(1)}, bf16[1536,128]{1,0:T(8,128)(2,1)S(1)}, u32[]{:S(2)}, u32[]{:S(2)}) collective-permute-start(bf16[1536,128]{1,0:T(8,128)(2,1)S(1)} %collective-permute-done.5.refs_0_), channel_id=1, source_target_pairs={{0,4},{4,0},{8,12},{12,8},{1,5},{5,1},{9,13},{13,9},{2,6},{6,2},{1... | collective-permute-start | bytes 1179656 | tf_op jit(solution)/shard_map/ppermute | solution.py:347

commit v6 on v5

--- a/solution.py
+++ b/solution.py
@@ -246,8 +246,12 @@
     panel[BLOCK:, :] = -jnp.where(is_first, 0.0, inverse.T)
 
 
-def front_kernel(layout, n_row, row_blocks, tables, mask, diag, whole, panel, *refs):
-    out, weight, product, buffer = refs[-4:]
+def front_kernel(layout, n_row, row_blocks, tables_any, mask_any, diag, whole, panel, *refs):
+    result, out, weight, product, buffer, tables, mask, sems = refs[-8:]
+    first_copy = pltpu.make_async_copy(tables_any, tables, sems.at[0])
+    second_copy = pltpu.make_async_copy(mask_any, mask, sems.at[1])
+    first_copy.start()
+    second_copy.start()
     me, col_index = lax.axis_index("row"), lax.axis_index("col")
     is_panel = col_index < NPANEL
     rows = (product.shape[1] - BLOCK) // n_row
@@ -259,6 +263,12 @@
         parts.append((child, owner(me), refs[second], at, 1 - col_index % 2))
         start = pl.multiple_of(owner(me) * rows, rows)
         buffer[child, pl.ds(start, rows), :] = refs[first][column : column + rows, :]
+
+    for child in range(2):
+        product[child, n_row * rows :, :] = jnp.zeros((BLOCK, PW), F32)
+        buffer[child, n_row * rows :, :] = jnp.zeros((BLOCK, PW), BF16)
+    first_copy.wait()
+    second_copy.wait()
 
     mirrored = [jnp.zeros((BLOCK, wide), F32)] * 2
     for child, owner, ref, at, side in parts:
@@ -292,11 +302,14 @@
         value = jnp.dot(left, both, preferred_element_type=F32)
         start = pl.multiple_of(owner * rows + side * half, half)
         product[child, pl.ds(start, half), :] = value[:, :PW] + value[:, PW:]
-    for child in range(2):
-        product[child, n_row * rows :, :] = jnp.zeros((BLOCK, PW), F32)
-        buffer[child, n_row * rows :, :] = jnp.zeros((BLOCK, PW), BF16)
-
-    for p in range(row_blocks):
+    row_id = lax.broadcasted_iota(jnp.int32, (BLOCK, BLOCK), 0)
+    col_id = lax.broadcasted_iota(jnp.int32, (BLOCK, BLOCK), 1)
+
+    def diagonal(p):
+        line = jnp.broadcast_to(diag[0:1, p * BLOCK : (p + 1) * BLOCK], (BLOCK, BLOCK))
+        return jnp.where(row_id == col_id, line, 0.0)
+
+    def place(p):
         at = me * row_blocks + p
         first, second = (
             pl.ds(pl.multiple_of(tables[child, at] * BLOCK, BLOCK), BLOCK) for child in range(2)
@@ -304,31 +317,38 @@
         base = buffer[0, first, :].astype(F32) + buffer[1, second, :].astype(F32)
         keep = jnp.where(is_panel | (mask[0, col_index, at] > 0), 1.0, 0.0)
         value = jnp.where(is_panel, 0.0, base) - keep * (product[0, first, :] + product[1, second, :])
-        out[0, p * BLOCK : (p + 1) * BLOCK, :] = value
-
-    row_id = lax.broadcasted_iota(jnp.int32, (BLOCK, BLOCK), 0)
-    col_id = lax.broadcasted_iota(jnp.int32, (BLOCK, BLOCK), 1)
-
-    def diagonal(p):
-        line = jnp.broadcast_to(diag[0:1, p * BLOCK : (p + 1) * BLOCK], (BLOCK, BLOCK))
-        return jnp.where(row_id == col_id, line, 0.0)
-
-    for p in range(NPANEL):
-
+        out[p * BLOCK : (p + 1) * BLOCK, :] = value
+
+    def correct(p):
         @pl.when(me == 0)
         def _():
             keep = jnp.where(is_panel | (mask[0, col_index, p] > 0), 1.0, 0.0)
             column = jnp.sum(diagonal(p), axis=1, keepdims=True)
-            value = out[0, p * BLOCK : (p + 1) * BLOCK, :]
+            value = out[p * BLOCK : (p + 1) * BLOCK, :]
             value = value - keep * column * weight[p * BLOCK : (p + 1) * BLOCK, :]
             above = row_id + p * BLOCK < col_id + col_index * PW
-            out[0, p * BLOCK : (p + 1) * BLOCK, :] = jnp.where(is_panel & above, 0.0, value)
-
-    for p in range(row_blocks):
-
+            out[p * BLOCK : (p + 1) * BLOCK, :] = jnp.where(is_panel & above, 0.0, value)
+
+    def add_diagonal(p):
         @pl.when(jnp.logical_not(is_panel) & (me * row_blocks + p == col_index))
         def _():
-            out[0, p * BLOCK : (p + 1) * BLOCK, :] += diagonal(p)
+            out[p * BLOCK : (p + 1) * BLOCK, :] += diagonal(p)
+
+    copies = []
+    step = 3
+    for start in range(0, row_blocks, step):
+        for p in range(start, start + step):
+            place(p)
+        for p in range(start, start + step):
+            if p < NPANEL:
+                correct(p)
+            add_diagonal(p)
+        lines = pl.ds(start * BLOCK, step * BLOCK)
+        copy = pltpu.make_async_copy(out.at[lines], result.at[0, lines], sems.at[2 + start // step])
+        copy.start()
+        copies.append(copy)
+    for copy in copies:
+        copy.wait()
 
 
 def body(kids, maps, mask, diag):
@@ -462,12 +482,16 @@
     return pl.pallas_call(
         functools.partial(front_kernel, layout, n_row, row_blocks),
         out_shape=jax.ShapeDtypeStruct((1, rows_dev, PW), F32),
-        in_specs=[smem, smem] + [vmem] * (3 + len(arrays)),
-        out_specs=vmem,
+        in_specs=[anywhere, anywhere] + [vmem] * (3 + len(arrays)),
+        out_specs=hbm,
         scratch_shapes=[
+            pltpu.VMEM((rows_dev, PW), F32),
             pltpu.VMEM((NPANEL * PW, PW), F32),
             pltpu.VMEM((2, height, PW), F32),
             pltpu.VMEM((2, height, PW), BF16),
+            pltpu.SMEM(tables.shape, jnp.int32),
+            pltpu.SMEM(mask.shape, jnp.int32),
+            pltpu.SemaphoreType.DMA((2 + row_blocks // 3,)),
         ],
         compiler_params=params(),
         cost_estimate=cost(0),

time: 42.3 us -> 41.8 us (0.988)
  starting transfers between devices: 10.4 us -> 9.17 us
  waiting for transfers between devices: 13.8 us -> 14.9 us
    ppermute x3, starting transfers between devices: 5.71 us -> 4.33 us  [parent(): return lax.ppermute(x, ('front', 'row'), pairs)]
    ppermute x3, waiting for transfers between devices: 1.44 us -> 2.53 us  [parent(): return lax.ppermute(x, ('front', 'row'), pairs)]
  transfers between devices with their start and end apart: 12 -> 12, of which waited for: 5 -> 5; matrix products, arithmetic and copies ran while one was open for 0% -> 0% of each run, Pallas kernels for 27% -> 28%
where the time goes in v6:
time: 41.8 us; the launch traced here: 41.6 us
  Pallas kernels  17.3 us (41%)
  waiting for transfers between devices  14.9 us (36%)
  starting transfers between devices  9.17 us (22%)
    pallas_call x1, Pallas kernels, body(): pl.pallas_call(functools.partial(factor_kernel, len(own_parts)), out_shap...  9.87 us
    ppermute x1, waiting for transfers between devices, along(): lax.ppermute(x, 'row', [(i, (i + 2 * by) % n_row) for i in range(n_row)])  9.09 us
    ppermute x3, starting transfers between devices, parent(): return lax.ppermute(x, ('front', 'row'), pairs)  4.33 us
    pallas_call x1, Pallas kernels, body(): pl.pallas_call(functools.partial(front_kernel, layout, n_row, row_blocks)...  3.8 us
    ppermute x7, waiting for transfers between devices, partner(): return lax.ppermute(x, 'row', [(i, i ^ 1) for i in range(n_row)])  3.3 us
    ppermute x3, waiting for transfers between devices, parent(): return lax.ppermute(x, ('front', 'row'), pairs)  2.53 us
    pallas_call x1, Pallas kernels, body(): pl.pallas_call(select_kernel, out_shape=[jax.ShapeDtypeStruct((2, maps.sh...  2.02 us
    ppermute x7, starting transfers between devices, partner(): return lax.ppermute(x, 'row', [(i, i ^ 1) for i in range(n_row)])  1.71 us
  transfers between devices with their start and end apart: 12, of which 5 were waited for; matrix products, arithmetic and copies ran while one was open for 0% of the time, Pallas kernels for 28%

profile of v6, /device:TPU:0, one launch (start us, length us, event | category | flops | bytes accessed | tf_op | source)
XLA Modules:
  0.0 41.6 jit_solution(11038018065125093363)
XLA Ops:
  0.0 2.0 %select.1 = (s32[2,72]{1,0:T(2,128)S(1)}, bf16[1808,128]{1,0:T(8,128)(2,1)S(1)}, bf16[272,128]{1,0:T(8,128)(2,1)S(1)}, bf16[1808,128]{1,0:T(8,128)(2,1)S(1)}) custom-call(s32[1,2,24,72]{3,2,1,0:T(8,128)} %bitcast.3, f32[1,2304]{1,0:T(1,128)} %diag.1, bf16[1,2,768,3072]{3,2,1,0:T(8,128)(2,1)} %kids.3), custom_call_target="tpu_custom_call" | custom-call | tf_op jit(solution)/shard_map/select/pallas_call | solution.py:391
  2.0 2.3 %collective-permute-start.2 = (bf16[1808,128]{1,0:T(8,128)(2,1)S(1)}, bf16[1808,128]{1,0:T(8,128)(2,1)S(1)}, u32[]{:S(2)}, u32[]{:S(2)}) collective-permute-start(bf16[1808,128]{1,0:T(8,128)(2,1)S(1)} %get-tuple-element.36), channel_id=1, source_target_pairs={{0,16},{4,20},{8,24},{12,28},{16,0},{20,4},{24,8},{28,12},{1,17},{... | collective-permute-start | bytes 1388552 | tf_op jit(solution)/shard_map/ppermute | solution.py:374
  4.4 1.5 %collective-permute-start.1 = (bf16[1808,128]{1,0:T(8,128)(2,1)S(1)}, bf16[1808,128]{1,0:T(8,128)(2,1)S(1)}, u32[]{:S(2)}, u32[]{:S(2)}) collective-permute-start(bf16[1808,128]{1,0:T(8,128)(2,1)S(1)} %get-tuple-element.42.refs_0_.refs_2_), channel_id=1, source_target_pairs={{0,8},{4,12},{8,0},{12,4},{1,9},{5,13},{9,1},{13,5},{2,10},{6,14},... | collective-permute-start | bytes 1388552 | tf_op jit(solution)/shard_map/ppermute | solution.py:364
  5.9 1.6 %remain.1 = (bf16[2304,128]{1,0:T(8,128)(2,1)S(1)}, bf16[768,128]{1,0:T(8,128)(2,1)S(1)}) custom-call(s32[2,72]{1,0:T(2,128)S(1)} %get-tuple-element.29.tables, bf16[1,2,768,3072]{3,2,1,0:T(8,128)(2,1)} %kids.3), custom_call_target="tpu_custom_call" | custom-call | tf_op jit(solution)/shard_map/remain/pallas_call | solution.py:407
  7.5 0.1 collective-permute-start.3
  7.6 0.5 %collective-permute-start.4 = (bf16[768,128]{1,0:T(8,128)(2,1)S(1)}, bf16[768,128]{1,0:T(8,128)(2,1)S(1)}, u32[]{:S(2)}, u32[]{:S(2)}) collective-permute-start(bf16[768,128]{1,0:T(8,128)(2,1)S(1)} %get-tuple-element.50.refs_3_), channel_id=1, source_target_pairs={{0,4},{4,0},{8,12},{12,8},{1,5},{5,1},{9,13},{13,9},{2,6},{6,2},{1... | collective-permute-start | bytes 589832 | tf_op jit(solution)/shard_map/ppermute | solution.py:367
  8.1 0.0 collective-permute-start
  8.1 9.1 %collective-permute-done.1.refs_2_.refs_8_ = bf16[1808,128]{1,0:T(8,128)(2,1)S(1)} collective-permute-done((bf16[1808,128]{1,0:T(8,128)(2,1)S(1)}, bf16[1808,128]{1,0:T(8,128)(2,1)S(1)}, u32[]{:S(2)}, u32[]{:S(2)}) %collective-permute-start.1) | collective-permute-done | bytes 462880 | tf_op jit(solution)/shard_map/ppermute | solution.py:364
  17.2 1.1 %collective-permute-done.refs_6_ = bf16[272,128]{1,0:T(8,128)(2,1)S(1)} collective-permute-done((bf16[272,128]{1,0:T(8,128)(2,1)S(1)}, bf16[272,128]{1,0:T(8,128)(2,1)S(1)}, u32[]{:S(2)}, u32[]{:S(2)}) %collective-permute-start) | collective-permute-done | bytes 69664 | tf_op jit(solution)/shard_map/ppermute | solution.py:374
  18.3 0.0 collective-permute-done.4.refs_5_
  18.3 0.0 collective-permute-done.3.refs_1_.refs_4_
  18.4 0.1 collective-permute-start.7
  18.5 0.6 %collective-permute-start.8 = (bf16[1808,128]{1,0:T(8,128)(2,1)S(1)}, bf16[1808,128]{1,0:T(8,128)(2,1)S(1)}, u32[]{:S(2)}, u32[]{:S(2)}) collective-permute-start(bf16[1808,128]{1,0:T(8,128)(2,1)S(1)} %collective-permute-done.2.refs_4_.refs_6_), channel_id=1, source_target_pairs={{0,4},{4,0},{8,12},{12,8},{1,5},{5,1},{9,13},{13,9},{2,6},{6,2},{1... | collective-permute-start | bytes 1388552 | tf_op jit(solution)/shard_map/ppermute | solution.py:367
  19.0 2.0 %collective-permute-start.6 = (bf16[2304,128]{1,0:T(8,128)(2,1)S(1)}, bf16[2304,128]{1,0:T(8,128)(2,1)S(1)}, u32[]{:S(2)}, u32[]{:S(2)}) collective-permute-start(bf16[2304,128]{1,0:T(8,128)(2,1)S(1)} %get-tuple-element.41), channel_id=1, source_target_pairs={{0,24},{4,28},{8,16},{12,20},{16,8},{20,12},{24,0},{28,4},{1,25},{... | collective-permute-start | bytes 1769480 | tf_op jit(solution)/shard_map/ppermute | solution.py:374
  21.0 1.6 %collective-permute-start.5 = (bf16[1536,128]{1,0:T(8,128)(2,1)S(1)}, bf16[1536,128]{1,0:T(8,128)(2,1)S(1)}, u32[]{:S(2)}, u32[]{:S(2)}) collective-permute-start(bf16[1536,128]{1,0:T(8,128)(2,1)S(1)} %pad_maximum_fusion), channel_id=1, source_target_pairs={{0,1},{1,0},{2,3},{3,2},{4,5},{5,4},{6,7},{7,6},{8,9},{9,8},{10,11... | collective-permute-start | bytes 1179656 | tf_op jit(solution)/shard_map/ppermute | solution.py:377
  22.7 0.0 collective-permute-start.9
  22.7 1.3 %collective-permute-done.9.refs_7_ = bf16[272,128]{1,0:T(8,128)(2,1)S(1)} collective-permute-done((bf16[272,128]{1,0:T(8,128)(2,1)S(1)}, bf16[272,128]{1,0:T(8,128)(2,1)S(1)}, u32[]{:S(2)}, u32[]{:S(2)}) %collective-permute-start.9) | collective-permute-done | bytes 69664 | tf_op jit(solution)/shard_map/ppermute | solution.py:367
  23.9 0.0 collective-permute-done.7.refs_3_.refs_9_
  23.9 9.9 %factor.1 = (bf16[3,256,256]{2,1,0:T(8,128)(2,1)S(1)}, f32[256,128]{1,0:T(8,128)S(1)}) custom-call(bf16[1808,128]{1,0:T(8,128)(2,1)S(1)} %get-tuple-element.42.refs_0_.refs_2_, bf16[1808,128]{1,0:T(8,128)(2,1)S(1)} %collective-permute-done.3.refs_1_.refs_4_, bf16[1808,128]{1,0:T(8,128)(2,1)S(1)} %collective-permute-done.1.refs_2_.refs_8_, ...), custom_call_target="tpu_custom_call" | custom-call | tf_op jit(solution)/shard_map/factor/pallas_call | solution.py:436
  33.8 1.4 %collective-permute-done.6.refs_10_ = bf16[2304,128]{1,0:T(8,128)(2,1)S(1)} collective-permute-done((bf16[2304,128]{1,0:T(8,128)(2,1)S(1)}, bf16[2304,128]{1,0:T(8,128)(2,1)S(1)}, u32[]{:S(2)}, u32[]{:S(2)}) %collective-permute-start.6) | collective-permute-done | bytes 589856 | tf_op jit(solution)/shard_map/ppermute | solution.py:374
  35.2 0.5 %collective-permute-start.10 = (bf16[1536,128]{1,0:T(8,128)(2,1)S(1)}, bf16[1536,128]{1,0:T(8,128)(2,1)S(1)}, u32[]{:S(2)}, u32[]{:S(2)}) collective-permute-start(bf16[1536,128]{1,0:T(8,128)(2,1)S(1)} %collective-permute-done.5.refs_0_), channel_id=1, source_target_pairs={{0,4},{4,0},{8,12},{12,8},{1,5},{5,1},{9,13},{13,9},{2,6},{6,2},{1... | collective-permute-start | bytes 1179656 | tf_op jit(solution)/shard_map/ppermute | solution.py:367
  35.8 2.0 %collective-permute-done.10.refs_1_ = bf16[1536,128]{1,0:T(8,128)(2,1)S(1)} collective-permute-done((bf16[1536,128]{1,0:T(8,128)(2,1)S(1)}, bf16[1536,128]{1,0:T(8,128)(2,1)S(1)}, u32[]{:S(2)}, u32[]{:S(2)}) %collective-permute-start.10) | collective-permute-done | bytes 393248 | tf_op jit(solution)/shard_map/ppermute | solution.py:367
  37.8 0.0 collective-permute-done.11.refs_11_
  37.8 3.8 %front.1 = f32[1,2304,128]{2,1,0:T(8,128)} custom-call(s32[2,72]{1,0:T(2,128)S(1)} %pad_add_fusion.tables_any, s32[1,4,72]{2,1,0:T(4,128)S(1)} %bitcast.2, f32[1,2304]{1,0:T(1,128)S(1)} %copy-done, bf16[3,256,256]{2,1,0:T(8,128)(2,1)S(1)} %get-tuple-element.47.whole, f32[256,128]{1,0:T(8,128)S(1)} %get-tuple-element.48.panel, ...), custom_call_target="tpu_custom_call" | custom-call | tf_op jit(solution)/shard_map/front/pallas_call | solution.py:482
  (14 shorter events, 0.1 us)
Async XLA Ops:
  0.0 37.8 %copy-start = (f32[1,2304]{1,0:T(1,128)S(1)}, f32[1,2304]{1,0:T(1,128)}, u32[]{:S(2)}) copy-start(f32[1,2304]{1,0:T(1,128)} %diag.1) | copy-start | bytes 27652
  0.0 37.8 %copy-start.1 = (s32[1,72,4]{1,2,0:T(4,128)S(1)}, s32[1,72,4]{1,2,0:T(4,128)}, u32[]{:S(2)}) copy-start(s32[1,72,4]{1,2,0:T(4,128)} %param.6) | copy-start | bytes 3460
  2.0 16.3 %collective-permute-start.2 = (bf16[1808,128]{1,0:T(8,128)(2,1)S(1)}, bf16[1808,128]{1,0:T(8,128)(2,1)S(1)}, u32[]{:S(2)}, u32[]{:S(2)}) collective-permute-start(bf16[1808,128]{1,0:T(8,128)(2,1)S(1)} %get-tuple-element.36), channel_id=1, source_target_pairs={{0,16},{4,20},{8,24},{12,28},{16,0},{20,4},{24,8},{28,12},{1,17},{... | collective-permute-start | bytes 1388552 | tf_op jit(solution)/shard_map/ppermute | solution.py:374
  4.4 12.8 %collective-permute-start.1 = (bf16[1808,128]{1,0:T(8,128)(2,1)S(1)}, bf16[1808,128]{1,0:T(8,128)(2,1)S(1)}, u32[]{:S(2)}, u32[]{:S(2)}) collective-permute-start(bf16[1808,128]{1,0:T(8,128)(2,1)S(1)} %get-tuple-element.42.refs_0_.refs_2_), channel_id=1, source_target_pairs={{0,8},{4,12},{8,0},{12,4},{1,9},{5,13},{9,1},{13,5},{2,10},{6,14},... | collective-permute-start | bytes 1388552 | tf_op jit(solution)/shard_map/ppermute | solution.py:364
  7.5 10.8 %collective-permute-start.3 = (bf16[1808,128]{1,0:T(8,128)(2,1)S(1)}, bf16[1808,128]{1,0:T(8,128)(2,1)S(1)}, u32[]{:S(2)}, u32[]{:S(2)}) collective-permute-start(bf16[1808,128]{1,0:T(8,128)(2,1)S(1)} %get-tuple-element.42.refs_0_.refs_2_), channel_id=1, source_target_pairs={{0,4},{4,0},{8,12},{12,8},{1,5},{5,1},{9,13},{13,9},{2,6},{6,2},{1... | collective-permute-start | bytes 1388552 | tf_op jit(solution)/shard_map/ppermute | solution.py:367
  7.6 10.7 %collective-permute-start.4 = (bf16[768,128]{1,0:T(8,128)(2,1)S(1)}, bf16[768,128]{1,0:T(8,128)(2,1)S(1)}, u32[]{:S(2)}, u32[]{:S(2)}) collective-permute-start(bf16[768,128]{1,0:T(8,128)(2,1)S(1)} %get-tuple-element.50.refs_3_), channel_id=1, source_target_pairs={{0,4},{4,0},{8,12},{12,8},{1,5},{5,1},{9,13},{13,9},{2,6},{6,2},{1... | collective-permute-start | bytes 589832 | tf_op jit(solution)/shard_map/ppermute | solution.py:367
  8.1 10.2 %collective-permute-start = (bf16[272,128]{1,0:T(8,128)(2,1)S(1)}, bf16[272,128]{1,0:T(8,128)(2,1)S(1)}, u32[]{:S(2)}, u32[]{:S(2)}) collective-permute-start(bf16[272,128]{1,0:T(8,128)(2,1)S(1)} %get-tuple-element.30), channel_id=1, source_target_pairs={{0,24},{4,28},{8,16},{12,20},{16,8},{20,12},{24,0},{28,4},{1,25},{... | collective-permute-start | bytes 208904 | tf_op jit(solution)/shard_map/ppermute | solution.py:374
  18.4 5.6 %collective-permute-start.7 = (bf16[1808,128]{1,0:T(8,128)(2,1)S(1)}, bf16[1808,128]{1,0:T(8,128)(2,1)S(1)}, u32[]{:S(2)}, u32[]{:S(2)}) collective-permute-start(bf16[1808,128]{1,0:T(8,128)(2,1)S(1)} %collective-permute-done.1.refs_2_.refs_8_), channel_id=1, source_target_pairs={{0,4},{4,0},{8,12},{12,8},{1,5},{5,1},{9,13},{13,9},{2,6},{6,2},{1... | collective-permute-start | bytes 1388552 | tf_op jit(solution)/shard_map/ppermute | solution.py:367
  18.5 5.5 %collective-permute-start.8 = (bf16[1808,128]{1,0:T(8,128)(2,1)S(1)}, bf16[1808,128]{1,0:T(8,128)(2,1)S(1)}, u32[]{:S(2)}, u32[]{:S(2)}) collective-permute-start(bf16[1808,128]{1,0:T(8,128)(2,1)S(1)} %collective-permute-done.2.refs_4_.refs_6_), channel_id=1, source_target_pairs={{0,4},{4,0},{8,12},{12,8},{1,5},{5,1},{9,13},{13,9},{2,6},{6,2},{1... | collective-permute-start | bytes 1388552 | tf_op jit(solution)/shard_map/ppermute | solution.py:367
  19.0 16.2 %collective-permute-start.6 = (bf16[2304,128]{1,0:T(8,128)(2,1)S(1)}, bf16[2304,128]{1,0:T(8,128)(2,1)S(1)}, u32[]{:S(2)}, u32[]{:S(2)}) collective-permute-start(bf16[2304,128]{1,0:T(8,128)(2,1)S(1)} %get-tuple-element.41), channel_id=1, source_target_pairs={{0,24},{4,28},{8,16},{12,20},{16,8},{20,12},{24,0},{28,4},{1,25},{... | collective-permute-start | bytes 1769480 | tf_op jit(solution)/shard_map/ppermute | solution.py:374
  21.0 12.8 %collective-permute-start.5 = (bf16[1536,128]{1,0:T(8,128)(2,1)S(1)}, bf16[1536,128]{1,0:T(8,128)(2,1)S(1)}, u32[]{:S(2)}, u32[]{:S(2)}) collective-permute-start(bf16[1536,128]{1,0:T(8,128)(2,1)S(1)} %pad_maximum_fusion), channel_id=1, source_target_pairs={{0,1},{1,0},{2,3},{3,2},{4,5},{5,4},{6,7},{7,6},{8,9},{9,8},{10,11... | collective-permute-start | bytes 1179656 | tf_op jit(solution)/shard_map/ppermute | solution.py:377
  22.7 1.3 %collective-permute-start.9 = (bf16[272,128]{1,0:T(8,128)(2,1)S(1)}, bf16[272,128]{1,0:T(8,128)(2,1)S(1)}, u32[]{:S(2)}, u32[]{:S(2)}) collective-permute-start(bf16[272,128]{1,0:T(8,128)(2,1)S(1)} %collective-permute-done.refs_6_), channel_id=1, source_target_pairs={{0,4},{4,0},{8,12},{12,8},{1,5},{5,1},{9,13},{13,9},{2,6},{6,2},{1... | collective-permute-start | bytes 208904 | tf_op jit(solution)/shard_map/ppermute | solution.py:367
  35.2 2.6 %collective-permute-start.11 = (bf16[2304,128]{1,0:T(8,128)(2,1)S(1)}, bf16[2304,128]{1,0:T(8,128)(2,1)S(1)}, u32[]{:S(2)}, u32[]{:S(2)}) collective-permute-start(bf16[2304,128]{1,0:T(8,128)(2,1)S(1)} %collective-permute-done.6.refs_10_), channel_id=1, source_target_pairs={{0,4},{4,0},{8,12},{12,8},{1,5},{5,1},{9,13},{13,9},{2,6},{6,2},{1... | collective-permute-start | bytes 1769480 | tf_op jit(solution)/shard_map/ppermute | solution.py:367
  35.2 2.6 %collective-permute-start.10 = (bf16[1536,128]{1,0:T(8,128)(2,1)S(1)}, bf16[1536,128]{1,0:T(8,128)(2,1)S(1)}, u32[]{:S(2)}, u32[]{:S(2)}) collective-permute-start(bf16[1536,128]{1,0:T(8,128)(2,1)S(1)} %collective-permute-done.5.refs_0_), channel_id=1, source_target_pairs={{0,4},{4,0},{8,12},{12,8},{1,5},{5,1},{9,13},{13,9},{2,6},{6,2},{1... | collective-permute-start | bytes 1179656 | tf_op jit(solution)/shard_map/ppermute | solution.py:367
